TPU v7x, 32 devices: a whole 2x2x4 slice. The times are simulated.
32 devices in a mesh: frame: 8 (over z, y), space: 4 (over x, core).
Axes of the slice: x: 2, y: 2, z: 4, core: 2. Of those that a mesh axis runs over, the one named last changes fastest.
Arguments:
- hidden_in: bfloat16 [2, 8, 8, 64, 1152], P(None, 'frame', 'space'), may hold values from -6 to 6
- attn_cotangent: bfloat16 [2, 8, 8, 64, 1152], P(None, 'frame', 'space'), may hold values from -6 to 6
- w_qkv: bfloat16 [1152, 3456], P('space'), may hold values from -0.1875 to 0.1875
- modulation_table: bfloat16 [1000, 2, 1152], replicated, may hold values from -3 to 3
- snr_table: float32 [1000], replicated, may hold values from 0.1 to 1
- timestep: int32 [2], replicated, may hold values from 0 to 999
- weight_index: int32 [2], replicated, may hold values from 0 to 999
Outputs:
- grad_input: bfloat16 [2, 8, 8, 64, 1152], P(None, 'frame', 'space')
- grad_w_qkv: float32 [1152, 3456], P('space')
- grad_modulation: float32 [2, 2, 1152], replicated
All inputs are finite; a program needn't handle non-finite values.
Results may differ from a plain program's by a relative error of at most 0.029.
Values may be sent and summed in bfloat16 or wider, within the bound.
No kernel may reach another device: no remote copies, remote signals or barrier semaphores. Data moves between devices by JAX's collectives and lax.ppermute only.
A program may use at most 128 MiB of HBM per device.

v0:
```python
import jax
import jax.numpy as jnp
from jax import lax
from jax.sharding import PartitionSpec as P

HEADS = 16
HEAD_DIM = 72


def attend_back(queries, keys, values, upstream):
    factor = queries.shape[-1] ** (-0.5)
    queries = queries.astype(jnp.float32)
    keys = keys.astype(jnp.float32)
    values = values.astype(jnp.float32)
    upstream = upstream.astype(jnp.float32)
    highest = lax.Precision.HIGHEST
    scores = jnp.einsum("bfxhe,bgxhe->bxhfg", queries, keys, precision=highest) * factor
    expd = jnp.exp(scores)
    probs = expd / jnp.sum(expd, axis=-1, keepdims=True)
    grad_probs = jnp.einsum("bfxhe,bgxhe->bxhfg", upstream, values, precision=highest)
    grad_values = jnp.einsum("bxhfg,bfxhe->bgxhe", probs, upstream, precision=highest)
    grad_scores = probs * (grad_probs - jnp.sum(probs * grad_probs, axis=-1, keepdims=True))
    grad_queries = jnp.einsum("bxhfg,bgxhe->bfxhe", grad_scores, keys, precision=highest) * factor
    grad_keys = jnp.einsum("bxhfg,bfxhe->bgxhe", grad_scores, queries, precision=highest) * factor
    return (
        grad_queries.astype(jnp.bfloat16),
        grad_keys.astype(jnp.bfloat16),
        grad_values.astype(jnp.bfloat16),
    )


def per_device(
    hidden_in, attn_cotangent, w_qkv, modulation_table, snr_table, timestep, weight_index
):
    clip_count, frame_dev, row_dev, col_count, model_width = hidden_in.shape
    positions = row_dev * col_count
    values_in = hidden_in.astype(jnp.float32)
    average = jnp.mean(values_in, axis=-1, keepdims=True)
    centered = values_in - average
    variance = jnp.mean(centered * centered, axis=-1, keepdims=True)
    inverse_std = lax.rsqrt(variance + 1e-06)
    normed = centered * inverse_std
    modulation = modulation_table[timestep].astype(jnp.float32)
    shift = modulation[:, 0][:, None, None, None, :]
    scale = modulation[:, 1][:, None, None, None, :]
    modulated = (normed * (1.0 + scale) + shift).astype(jnp.bfloat16)
    mod_rows = modulated.reshape(-1, model_width)
    w_full = lax.all_gather(w_qkv, "space", axis=0, tiled=True)
    projected = jnp.dot(mod_rows, w_full, preferred_element_type=jnp.float32).astype(jnp.bfloat16)
    projected = projected.reshape(clip_count, frame_dev, positions, 3, model_width)
    loss_weight = snr_table[weight_index]
    upstream = (loss_weight[:, None, None, None, None] * attn_cotangent.astype(jnp.float32)).astype(
        jnp.bfloat16
    )
    upstream = upstream.reshape(clip_count, frame_dev, positions, 1, model_width)
    packed = jnp.concatenate([projected, upstream], axis=3)
    received = lax.all_to_all(packed, "frame", split_axis=2, concat_axis=1, tiled=True)
    item_count = received.shape[0]
    frames = received.shape[1]
    across = received.shape[2]
    pieces = received.reshape(item_count, frames, across, 4, HEADS, HEAD_DIM)
    head_grads = attend_back(
        pieces[:, :, :, 0], pieces[:, :, :, 1], pieces[:, :, :, 2], pieces[:, :, :, 3]
    )
    stacked = jnp.stack(head_grads, axis=3).reshape(item_count, frames, across, 3, model_width)
    grad_projected = lax.all_to_all(stacked, "frame", split_axis=1, concat_axis=2, tiled=True)
    grad_rows = grad_projected.reshape(-1, 3 * model_width)
    device_count = lax.axis_size("frame") * lax.axis_size("space")
    grad_scale_factor = float(mod_rows.shape[0] * device_count) ** (-0.5)
    row_share = lax.psum_scatter(
        lax.dot_general(
            mod_rows, grad_rows, (((0,), (0,)), ((), ())), preferred_element_type=jnp.float32
        ).astype(jnp.bfloat16),
        "space",
        scatter_dimension=0,
        tiled=True,
    )
    grad_weight = lax.psum(row_share, "frame").astype(jnp.float32) * grad_scale_factor
    grad_hidden = lax.dot_general(
        grad_rows, w_full, (((1,), (1,)), ((), ())), preferred_element_type=jnp.float32
    )
    grad_hidden = grad_hidden.reshape(values_in.shape)
    local_sums = jnp.stack(
        [jnp.sum(grad_hidden, axis=(1, 2, 3)), jnp.sum(grad_hidden * normed, axis=(1, 2, 3))],
        axis=1,
    )
    grad_modulation = lax.psum(local_sums, ("frame", "space")) * grad_scale_factor
    grad_normed = grad_hidden * (1.0 + scale)
    grad_input = (
        grad_normed
        - jnp.mean(grad_normed, axis=-1, keepdims=True)
        - normed * jnp.mean(grad_normed * normed, axis=-1, keepdims=True)
    ) * inverse_std
    return (grad_input.astype(jnp.bfloat16), grad_weight, grad_modulation)


def solution(mesh):
    in_specs = (
        P(None, "frame", "space", None, None),
        P(None, "frame", "space", None, None),
        P("space", None),
        P(),
        P(),
        P(),
        P(),
    )
    out_specs = (P(None, "frame", "space", None, None), P("space", None), P())
    return jax.shard_map(
        per_device, mesh=mesh, in_specs=in_specs, out_specs=out_specs, check_vma=False
    )
```

profile of v0, /device:TPU:0, one launch (start us, length us, event | category | flops | bytes accessed | tf_op | source)
XLA Modules:
  0.0 418.5 jit_solution(3720432954036185294)
XLA Ops:
  8.7 2.9 gather_fusion
  12.5 1.8 copy.65
  15.1 53.1 %all-gather.2.cloned.1.call-done = bf16[1152,3456]{1,0:T(8,128)(2,1)} async-done(((bf16[288,3456]{1,0:T(8,128)(2,1)}), bf16[1152,3456]{1,0:T(8,128)(2,1)}) %all-gather.2.cloned.1.call-update) | async-done | bytes 7962640 | tf_op jit(solution)/shard_map/all_gather | solution.py:48
  68.2 7.0 %convolution_convert_fusion.1 = bf16[256,3456]{1,0:T(8,128)(2,1)} fusion(bf16[256,1152]{1,0:T(8,128)(2,1)S(1)} %bitcast.75, bf16[1152,3456]{1,0:T(8,128)(2,1)} %all-gather.2.cloned.1.call-done), kind=kOutput, calls=%fused_computation.3 | convolution fusion | flops 2039316480 | bytes 10321920 | tf_op jit(solution)/shard_map/dot_general | solution.py:49
  75.2 2.6 copy.63
  77.9 1.9 reshape.124
  79.8 5.2 %pad_maximum_fusion = bf16[2,1,128,4,1152]{2,0,4,3,1:T(2,128)(2,1)S(1)} fusion(bf16[2,1,128,1,1152]{2,0,4,3,1:T(2,128)(2,1)} %copy.65, bf16[2,1,128,3,1152]{2,0,4,3,1:T(2,128)(2,1)} %reshape.124), kind=kLoop, calls=%fused_computation.5 | loop fusion | flops 1179648 | bytes 4718592 | tf_op jit(solution)/shard_map/concatenate | solution.py:56
  85.0 4.6 %copy.66 = bf16[2,1,128,4,1152]{4,3,1,0,2:T(4,128)(2,1)} copy(bf16[2,1,128,4,1152]{2,0,4,3,1:T(2,128)(2,1)S(1)} %pad_maximum_fusion) | data formatting | bytes 4718592 | tf_op jit(solution)/shard_map/concatenate | solution.py:56
  89.6 59.7 %all_to_all.8 = bf16[2,1,128,4,1152]{4,3,1,0,2:T(4,128)(2,1)S(1)} all-to-all(bf16[2,1,128,4,1152]{4,3,1,0,2:T(4,128)(2,1)} %copy.66), channel_id=1, replica_groups=mesh['frame'=8,'space'=4] {'frame'}, dimensions={2} | all-to-all | bytes 4718592 | tf_op jit(solution)/shard_map/all_to_all | solution.py:57
  149.3 8.8 %reshape.147 = bf16[2,8,16,4,16,72]{5,4,3,0,2,1:T(8,128)(2,1)} reshape(bf16[2,1,128,4,1152]{4,3,1,0,2:T(4,128)(2,1)S(1)} %all_to_all.8) | data formatting | bytes 4718592 | tf_op jit(solution)/shard_map/reshape | solution.py:61
  158.1 3.5 fusion.25
  161.6 1.8 fusion.1
  163.4 1.9 multiply_reduce_fusion
  165.3 2.8 fusion.9
  168.2 3.8 fusion.10
  171.9 3.7 fusion.8
  175.9 1.3 stack.21
  177.2 1.4 copy.74
  178.6 1.3 stack.22
  179.9 1.4 copy.75
  181.4 2.2 stack.23
  183.5 1.3 pad_maximum_fusion.1
  185.0 44.7 %all_to_all.9 = bf16[2,8,16,3,1152]{4,2,0,3,1:T(8,128)(2,1)S(1)} all-to-all(bf16[2,8,16,3,1152]{4,2,0,3,1:T(8,128)(2,1)S(1)} %copy.76), channel_id=1, replica_groups=mesh['frame'=8,'space'=4] {'frame'}, dimensions={1} | all-to-all | bytes 3538944 | tf_op jit(solution)/shard_map/all_to_all | solution.py:66
  229.7 1.2 copy.77
  231.2 5.5 %convolution_convert_fusion = bf16[1152,3456]{1,0:T(8,128)(2,1)} fusion(bf16[256,1152]{1,0:T(8,128)(2,1)S(1)} %bitcast.76, bf16[256,3456]{1,0:T(8,128)(2,1)S(1)} %bitcast.72), kind=kOutput, calls=%fused_computation.2 | convolution fusion | flops 2042413056 | bytes 10321920 | tf_op jit(solution)/shard_map/dot_general | solution.py:71
  236.8 67.3 %reduce-scatter.2.cloned.1.call-done = bf16[288,3456]{1,0:T(8,128)(2,1)} async-done(((bf16[1152,3456]{1,0:T(8,128)(2,1)}), bf16[288,3456]{1,0:T(8,128)(2,1)}) %reduce-scatter.2.cloned.1.call-update) | async-done | bytes 1990672 | tf_op jit(solution)/shard_map/reduce_scatter | solution.py:70
  304.0 6.5 %fusion.19 = (f32[256]{0:T(256)}, f32[256,1152]{1,0:T(8,128)S(1)}) fusion(f32[2,1152]{1,0:T(2,128)S(1)} %bitcast.79, bf16[256,3456]{1,0:T(8,128)(2,1)S(1)} %bitcast.73, bf16[1152,3456]{1,0:T(8,128)(2,1)} %all-gather.2.cloned.1.call-done), kind=kOutput, calls=%fused_computation.35 | convolution fusion | flops 2039021312 | bytes 10921984 | tf_op jit(solution)/shard_map/dot_general | solution.py:79
  310.6 1.1 fusion.17
  311.8 41.3 %psum.15 = f32[2,2,1152]{2,0,1:T(2,128)S(1)} all-reduce(f32[2,2,1152]{2,0,1:T(2,128)S(1)} %pad_maximum_fusion.2), channel_id=1, replica_groups=mesh['frame'=8,'space'=4] {'frame','space'}, use_global_device_ids=true, to_apply=%region_10.0 | all-reduce | flops 4608 | bytes 36864 | tf_op jit(solution)/shard_map/psum | solution.py:87
  353.8 1.9 fusion.16
  355.7 52.4 %all-reduce.2.cloned.1.call-done = bf16[288,3456]{1,0:T(8,128)(2,1)} async-done(((bf16[288,3456]{1,0:T(8,128)(2,1)}), bf16[288,3456]{1,0:T(8,128)(2,1)}) %all-reduce.2.cloned.1.call-update) | async-done | bytes 1990672 | tf_op jit(solution)/shard_map/psum | solution.py:78
  408.2 3.8 convert_multiply_fusion
  (50 shorter events, 4.6 us)
Async XLA Ops:
  7.2 4.5 %copy-start = (f32[1000]{0:T(1024)S(1)}, f32[1000]{0:T(1024)}, u32[]{:S(2)}) copy-start(f32[1000]{0:T(1024)} %param.11) | copy-start | bytes 12004
  7.2 4.5 %copy-start.8 = (s32[2]{0:T(128)S(1)}, s32[2]{0:T(128)}, u32[]{:S(2)}) copy-start(s32[2]{0:T(128)} %param.13) | copy-start | bytes 28
  7.2 5.1 %copy-start.3 = (bf16[2,1,2,64,1152]{4,3,2,1,0:T(8,128)(2,1)S(1)}, bf16[2,1,2,64,1152]{4,3,2,1,0:T(8,128)(2,1)}, u32[]{:S(2)}) copy-start(bf16[2,1,2,64,1152]{4,3,2,1,0:T(8,128)(2,1)} %param.8) | copy-start | bytes 1769476
  7.2 7.0 %copy-start.2 = (bf16[2,1,2,64,1152]{4,3,2,1,0:T(8,128)(2,1)S(1)}, bf16[2,1,2,64,1152]{4,3,2,1,0:T(8,128)(2,1)}, u32[]{:S(2)}) copy-start(bf16[2,1,2,64,1152]{4,3,2,1,0:T(8,128)(2,1)} %param.7) | copy-start | bytes 1769476
  7.2 61.0 %all-gather.2.cloned.1.call-start = ((), (), s32[]{:S(2)}) async-start(), calls=%async_computation.3 | async-start | bytes 9953280 | tf_op jit(solution)/shard_map/all_gather | solution.py:48
  7.9 296.1 %reduce-scatter.2.cloned.1.call-start = ((), (), s32[]{:S(2)}) async-start(), calls=%async_computation.4 | async-start | bytes 9953280 | tf_op jit(solution)/shard_map/reduce_scatter | solution.py:70
  14.4 296.2 %copy-start.4 = (f32[2,2,64]{2,1,0:T(2,128)}, f32[2,2,64]{2,1,0:T(2,128)S(1)}, u32[]{:S(2)}) copy-start(f32[2,2,64]{2,1,0:T(2,128)S(1)} %broadcast_multiply_fusion.2) | copy-start | bytes 3076
  14.7 53.5 %copy-start.5 = (f32[2,2,64]{2,1,0:T(2,128)}, f32[2,2,64]{2,1,0:T(2,128)S(1)}, u32[]{:S(2)}) copy-start(f32[2,2,64]{2,1,0:T(2,128)S(1)} %add_rsqrt_fusion) | copy-start | bytes 3076
  236.7 171.4 %all-reduce.2.cloned.1.call-start = ((), (), s32[]{:S(2)}) async-start(), calls=%async_computation.5 | async-start | bytes 3981312 | tf_op jit(solution)/shard_map/psum | solution.py:78
  310.6 43.2 %copy-start.7 = (f32[256]{0:T(256)S(1)}, f32[256]{0:T(256)}, u32[]{:S(2)}) copy-start(f32[256]{0:T(256)} %get-tuple-element.25) | copy-start | bytes 3076
  310.6 43.3 %copy-start.6 = (f32[2,2,64]{2,1,0:T(2,128)S(1)}, f32[2,2,64]{2,1,0:T(2,128)}, u32[]{:S(2)}) copy-start(f32[2,2,64]{2,1,0:T(2,128)} %copy-done.5) | copy-start | bytes 3076
  353.8 58.1 %copy-start.1 = (f32[1000]{0:T(1024)S(1)}, f32[1000]{0:T(1024)}, u32[]{:S(2)}) copy-start(f32[1000]{0:T(1024)} %param.11) | copy-start | bytes 12004
Sparse Core Ops, SparseCore 0:
  9.6 58.5 all-gather.1
  236.8 67.1 reduce-scatter.1
  307.6 100.4 all-reduce.1
where the time goes:
time: 419 us; the launch traced here: 418 us
  waiting for transfers between devices  174 us (42%)
  blocking collectives  146 us (35%)
  local copies, waits for them, and re-layouts  36.8 us (9%)
  matrix products  33.1 us (8%)
  other arithmetic  15.1 us (4%)
  between operations  14 us (3%)
    reduce_scatter x1, waiting for transfers between devices, per_device(): lax.psum_scatter(lax.dot_general(mod_rows, grad_rows, (((0,), (0,)), ((),...  67.3 us
    all_to_all x1, blocking collectives, per_device(): lax.all_to_all(packed, 'frame', split_axis=2, concat_axis=1, tiled=True)  59.7 us
    all_gather x1, waiting for transfers between devices, per_device(): w_full = lax.all_gather(w_qkv, 'space', axis=0, tiled=True)  53.1 us
    psum x1, waiting for transfers between devices, per_device(): lax.psum(row_share, 'frame').astype(jnp.float32) * grad_scale_factor  52.4 us
    all_to_all x1, blocking collectives, per_device(): lax.all_to_all(stacked, 'frame', split_axis=1, concat_axis=2, tiled=True)  44.7 us
    psum x1, blocking collectives, per_device(): lax.psum(local_sums, ('frame', 'space')) * grad_scale_factor  41.3 us
    reshape x1, local copies, waits for them, and re-layouts, per_device(): pieces = received.reshape(item_count, frames, across, 4, HEADS, HEAD_DIM)  8.77 us
  transfers between devices with their start and end apart: 3, of which 3 were waited for; matrix products, arithmetic and copies ran while one was open for 4% of the time, Pallas kernels for 0%

commit v1 on v0

v1 whole, which is shorter than its diff:
```python
import functools

import jax
import jax.numpy as jnp
from jax import lax
from jax.experimental import pallas as pl
from jax.experimental.pallas import tpu as pltpu
from jax.sharding import PartitionSpec as P

HEADS = 16
HEAD_DIM = 72
EPS = 1e-06
SLAB = 16
LANES = 128
F32 = jnp.float32
BF16 = jnp.bfloat16
VMEM = pl.BlockSpec(memory_space=pltpu.VMEM)
SMEM = pl.BlockSpec(memory_space=pltpu.SMEM)
ANY = pl.BlockSpec(memory_space=pl.ANY)


def cost(flops, moved):
    return pl.CostEstimate(flops=flops, bytes_accessed=moved, transcendentals=0)


def call(kernel, name, out_shape, in_specs, scratch=(), flops=0, moved=1 << 20):
    return pl.pallas_call(
        kernel,
        name=name,
        out_shape=out_shape,
        in_specs=in_specs,
        out_specs=jax.tree.map(lambda _: VMEM, out_shape),
        scratch_shapes=list(scratch),
        cost_estimate=cost(flops, moved),
        compiler_params=pltpu.CompilerParams(vmem_limit_bytes=40 << 20),
    )


def shape(dims, kind=BF16):
    return jax.ShapeDtypeStruct(dims, kind)


def place():
    frame, space = lax.axis_index("frame"), lax.axis_index("space")
    return frame // 2, frame % 2, space


def dot(a, b, dims=(((1,), (0,)), ((), ()))):
    return lax.dot_general(a, b, dims, preferred_element_type=F32)


ROWS_ROWS = (((1,), (1,)), ((), ()))


def pick(cond, a, b):
    return jnp.where(cond, a, b)


def halves_kernel(w_ref, out_ref):
    _, y, _ = place()
    width = w_ref.shape[1] // 3
    half = width // 2

    def take(lane):
        parts = [w_ref[:, j * width + lane : j * width + lane + half] for j in range(3)]
        out_ref[...] = jnp.concatenate(parts, axis=1)

    @pl.when(y == 0)
    def _():
        take(0)

    @pl.when(y == 1)
    def _():
        take(half)


def layer_norm(values):
    average = jnp.mean(values, axis=-1, keepdims=True)
    centered = values - average
    variance = jnp.mean(centered * centered, axis=-1, keepdims=True)
    inverse_std = lax.rsqrt(variance + EPS)
    return centered * inverse_std, inverse_std


def prep_kernel(groups, h_ref, c_ref, tab_ref, ts_ref, snr_ref, wi_ref, *rest):
    send, keep = rest[:groups], rest[groups : 2 * groups]
    mod_ref, scratch, sems = rest[2 * groups :]
    z, y, _ = place()
    clips, positions, width = h_ref.shape
    chunk, half = positions // groups, width // 2
    copies = [
        pltpu.make_async_copy(tab_ref.at[ts_ref[b]], scratch.at[b], sems.at[b])
        for b in range(clips)
    ]
    for copy in copies:
        copy.start()
    for copy in copies:
        copy.wait()
    for b in range(clips):
        table = scratch[b].astype(F32)
        mod_ref[b] = table
        shift, scale = table[0:1], 1.0 + table[1:2]
        weight = snr_ref[wi_ref[b]]
        for k in range(groups):
            rows = pl.ds(pl.multiple_of((z ^ k) * chunk, chunk), chunk)
            normed, _ = layer_norm(h_ref[b, rows, :].astype(F32))
            send[k][b, :, :width] = (normed * scale + shift).astype(BF16)
            up = c_ref[b, rows, :].astype(F32) * weight
            low, high = up[:, :half], up[:, half:]
            send[k][b, :, width:] = pick(y == 0, high, low).astype(BF16)
            keep[k][b] = pick(y == 0, low, high).astype(BF16)


def main_kernel(groups, shares, others, *refs):
    near, kept, far = refs[:groups], refs[groups : 2 * groups], refs[2 * groups : 3 * groups]
    weights = refs[3 * groups : 3 * groups + shares]
    rest = refs[3 * groups + shares :]
    outs, scratches = rest[: 2 + (others > 0)], rest[2 + (others > 0) :]
    grads, mod_t = outs[0], outs[1]
    w, mod, up, qw, kw, vw, dq, dk, dv, sems = scratches
    _, _, s = place()
    clips, chunk, _ = near[0].shape
    depth, wide = w.shape
    half = wide // 3
    frames = 2 * groups
    block = frames * SLAB
    slabs = chunk // SLAB
    share = depth // shares
    pad = qw.shape[1]
    copies = []
    for k in range(shares):
        rows = pl.ds(pl.multiple_of((s ^ k) * share, share), share) if shares > 1 else pl.ds(0, depth)
        copies.append(pltpu.make_async_copy(weights[k], w.at[rows], sems.at[k]))
        copies[-1].start()
    for b in range(clips):
        for i in range(slabs):
            base = (b * slabs + i) * block
            take = slice(i * SLAB, (i + 1) * SLAB)
            for k in range(groups):
                own = slice(base + k * SLAB, base + (k + 1) * SLAB)
                mod[own, :] = near[k][b, take, :depth]
                up[own, :half] = kept[k][b, take, :]
                its = slice(base + (groups + k) * SLAB, base + (groups + k + 1) * SLAB)
                mod[its, :] = far[k][b, take, :depth]
                up[its, :half] = far[k][b, take, depth:]
    up[:, half:] = jnp.zeros((up.shape[0], pad - half), BF16)
    vw[:, half:] = jnp.zeros((block, pad - half), BF16)
    for copy in copies:
        copy.wait()

    lane = lax.broadcasted_iota(jnp.int32, (block, 2 * LANES), 1)
    row = lax.broadcasted_iota(jnp.int32, (block, 2 * block), 0)
    col = lax.broadcasted_iota(jnp.int32, (block, 2 * block), 1)
    same = (row % SLAB) == (col % SLAB)
    pair = 2 * HEAD_DIM
    factor = HEAD_DIM ** (-0.5)
    seam = half // LANES * LANES

    @pl.loop(0, clips * slabs)
    def _(n):
        rows = pl.ds(pl.multiple_of(n * block, block), block)
        tokens = mod[rows, :]
        mod_t[:, rows] = tokens.T
        projected = dot(tokens, w[...])
        qw[...] = projected[:, :pad].astype(BF16)
        kw[...] = pltpu.roll(projected[:, seam : seam + pad], pad - (half - seam), 1).astype(BF16)
        vw[:, :half] = projected[:, 2 * half :].astype(BF16)
        dq[...] = jnp.zeros_like(dq)
        dk[...] = jnp.zeros_like(dk)
        dv[...] = jnp.zeros_like(dv)
        for i in range(half // pair):
            tile = pair * i // LANES * LANES
            off = pair * i - tile
            win = slice(tile, tile + 2 * LANES)
            first = ((lane >= off) & (lane < off + HEAD_DIM)).astype(F32).astype(BF16)
            second = ((lane >= off + HEAD_DIM) & (lane < off + pair)).astype(F32).astype(BF16)

            def split(x):
                return jnp.concatenate([x * first, x * second], axis=0)

            q, k, v, u = qw[:, win], kw[:, win], vw[:, win], up[rows, win]
            qs, ks, us = split(q), split(k), split(u)
            scores = jnp.where(same, dot(k, qs, ROWS_ROWS) * factor, -1e30)
            expd = jnp.exp(scores - jnp.max(scores, axis=0, keepdims=True))
            probs = expd * (1.0 / jnp.sum(expd, axis=0, keepdims=True))
            grad_probs = dot(v, us, ROWS_ROWS)
            delta = jnp.sum(probs * grad_probs, axis=0, keepdims=True)
            grad_scores = (probs * (grad_probs - delta)).astype(BF16)
            turned = jnp.concatenate([grad_scores[:, :block].T, grad_scores[:, block:].T], axis=1)
            dv[:, win] += dot(probs.astype(BF16), us)
            dk[:, win] += dot(grad_scores, qs)
            dq[:, win] += dot(turned, ks)
        near_q = dq[...] * factor
        near_k = pltpu.roll(dk[...] * factor, half - seam, 1)
        grads[rows, :seam] = near_q[:, :seam].astype(BF16)
        edge = lax.broadcasted_iota(jnp.int32, (block, LANES), 1) < half - seam
        grads[rows, seam : seam + LANES] = jnp.where(edge, near_q[:, seam:], near_k[:, :LANES]).astype(BF16)
        grads[rows, seam + LANES : 2 * half] = near_k[:, LANES:].astype(BF16)
        grads[rows, 2 * half :] = dv[:, :half].astype(BF16)

    if others:
        slices(outs[2], mod_t, grads, s ^ 1, share, others)


def slices(out, mod_t, grads, first, share, count):
    groups, rows = out.shape[1], out.shape[2]
    for j in range(count):
        start = pl.multiple_of((first ^ (2 * j)) * share, share)
        total = dot(mod_t[pl.ds(start, share), :], grads[...])
        for g in range(groups):
            out[j, g] = total[g * rows : (g + 1) * rows].astype(out.dtype)


def own_kernel(step, share, mod_t, grads, got, out):
    _, _, s = place()
    groups, rows = out.shape[0], out.shape[1]
    start = pl.multiple_of((s ^ (2 * step)) * share, share)
    total = dot(mod_t[pl.ds(start, share), :], grads[...])
    for g in range(groups):
        out[g] = (total[g * rows : (g + 1) * rows] + got[step, g].astype(F32)).astype(out.dtype)


def hidden_kernel(groups, shares, grads, *refs):
    weights, (near, far, w, part, sems) = refs[:shares], refs[shares:]
    _, _, s = place()
    depth = w.shape[0]
    share = depth // shares
    copies = []
    for k in range(shares):
        rows = pl.ds(pl.multiple_of((s ^ k) * share, share), share) if shares > 1 else pl.ds(0, depth)
        copies.append(pltpu.make_async_copy(weights[k], w.at[rows], sems.at[k]))
        copies[-1].start()
    _, clips, chunk, _ = near.shape
    slabs = chunk // SLAB
    block = 2 * groups * SLAB
    side = block // 2
    for copy in copies:
        copy.wait()
    for which, out in ((1, far), (0, near)):
        for n in range(clips * slabs):
            start = n * block + which * side
            part[n * side : (n + 1) * side, :] = grads[start : start + side, :]
        total = dot(part[...], w[...], ROWS_ROWS)
        for b in range(clips):
            for i in range(slabs):
                for k in range(groups):
                    start = (b * slabs + i) * side + k * SLAB
                    out[k, b, i * SLAB : (i + 1) * SLAB, :] = total[start : start + SLAB].astype(out.dtype)


def meet_kernel(near, got, *outs):
    for k, out in enumerate(outs):
        out[...] = (near[k].astype(F32) + got[k].astype(F32)).astype(out.dtype)


def input_kernel(groups, h_ref, mod_ref, *refs):
    parts, (out_ref, sums_ref) = refs[:groups], refs[groups:]
    z, _, _ = place()
    clips, positions, _ = h_ref.shape
    chunk = positions // groups
    for b in range(clips):
        scale = 1.0 + mod_ref[b][1:2]
        shift_sum, scale_sum = 0.0, 0.0
        for k in range(groups):
            rows = pl.ds(pl.multiple_of((z ^ k) * chunk, chunk), chunk)
            normed, inverse_std = layer_norm(h_ref[b, rows, :].astype(F32))
            grad_hidden = parts[k][b].astype(F32)
            by_normed = grad_hidden * normed
            shift_sum += jnp.sum(grad_hidden, axis=0, keepdims=True)
            scale_sum += jnp.sum(by_normed, axis=0, keepdims=True)
            grad_normed = grad_hidden * scale
            first = jnp.mean(grad_normed, axis=-1, keepdims=True)
            second = jnp.mean(by_normed * scale, axis=-1, keepdims=True)
            out_ref[b, rows, :] = ((grad_normed - first - normed * second) * inverse_std).astype(BF16)
        sums_ref[b, 0:1, :] = shift_sum
        sums_ref[b, 1:2, :] = scale_sum


def spread_kernel(own, *refs):
    groups = own.shape[0]
    got, outs = refs[:-groups], refs[-groups:]
    z, _, _ = place()
    for k in range(groups):
        total = own[z ^ k]
        for other in got:
            total += other[z ^ k].astype(F32)
        outs[k][...] = total.astype(outs[k].dtype)


def add_kernel(own, *refs):
    total = own[...]
    for other in refs[:-1]:
        total += other[...].astype(F32)
    refs[-1][...] = total.astype(BF16)


def weight_kernel(groups, scale, *refs):
    mine, other, out = refs[:groups], refs[groups : 2 * groups], refs[-1]
    z, y, _ = place()
    rows, wide = mine[0].shape
    half = wide // 3
    for k in range(groups):
        a, b = mine[k][...].astype(F32) * scale, other[k][...].astype(F32) * scale
        low, high = pick(y == 0, a, b), pick(y == 0, b, a)
        parts = []
        for j in range(3):
            cut = slice(j * half, (j + 1) * half)
            parts += [low[:, cut], high[:, cut]]
        out[pl.ds(pl.multiple_of((z ^ k) * rows, rows), rows), :] = jnp.concatenate(parts, axis=1)


def per_device(
    hidden_in, attn_cotangent, w_qkv, modulation_table, snr_table, timestep, weight_index
):
    clips, frame_dev, row_dev, col_count, width = hidden_in.shape
    frames, spaces = lax.axis_size("frame"), lax.axis_size("space")
    groups, lines = frames // 2, spaces // 2
    positions = frame_dev * row_dev * col_count
    chunk = positions // groups
    share, wide = w_qkv.shape[0], w_qkv.shape[1] // 2
    half = width // 2
    tokens = clips * frames * chunk
    block = frames * SLAB
    rows = share // groups
    pieces = share % 16 == 0 and share % (8 * groups) == 0
    shares = spaces if pieces else 1
    grad_scale_factor = float(clips * positions * frames * spaces) ** (-0.5)

    def over_space(x, step):
        return lax.ppermute(x, "space", [(i, i ^ step) for i in range(spaces)])

    def over_y(x):
        return lax.ppermute(x, "frame", [(i, i ^ 1) for i in range(frames)])

    def over_z(x, step):
        return lax.ppermute(x, "frame", [(i, i ^ (2 * step)) for i in range(frames)])

    hidden = hidden_in.reshape(clips, positions, width)
    cotangent = attn_cotangent.reshape(clips, positions, width)

    w_half = call(halves_kernel, "w_half", shape((share, wide)), [VMEM], moved=3 << 20)(w_qkv)
    if pieces:
        weights = [w_half, over_space(w_half, 1)]
        for j in range(1, lines):
            crossed = over_space(w_half, 2 * j)
            weights += [crossed, over_space(crossed, 1)]
    else:
        weights = [lax.all_gather(w_half, "space", axis=0, tiled=True)]

    prep = call(
        functools.partial(prep_kernel, groups),
        "prep",
        [shape((clips, chunk, width + half))] * groups
        + [shape((clips, chunk, half))] * groups
        + [shape((clips, 2, width), F32)],
        [VMEM, VMEM, ANY, SMEM, SMEM, SMEM],
        [pltpu.VMEM((clips, 2, width), BF16), pltpu.SemaphoreType.DMA((clips,))],
        moved=3 << 20,
    )(hidden, cotangent, modulation_table, timestep, snr_table, weight_index)
    send, keep, modulation = prep[:groups], prep[groups : 2 * groups], prep[-1]
    near = [send[0]] + [over_z(send[k], k) for k in range(1, groups)]
    far = [over_y(x) for x in near]
    kept = [keep[0]] + [over_z(keep[k], k) for k in range(1, groups)]

    pad = -(-half // LANES) * LANES
    outs = [shape((tokens, wide)), shape((width, tokens))]
    if pieces:
        outs.append(shape((lines, groups, rows, wide)))
    w_scratch = pltpu.VMEM((width, wide), BF16)
    main = call(
        functools.partial(main_kernel, groups, shares, lines if pieces else 0),
        "attend",
        outs,
        [VMEM] * (3 * groups) + [ANY] * shares,
        [
            w_scratch,
            pltpu.VMEM((tokens, width), BF16),
            pltpu.VMEM((tokens, pad), BF16),
            pltpu.VMEM((block, pad), BF16),
            pltpu.VMEM((block, pad), BF16),
            pltpu.VMEM((block, pad), BF16),
            pltpu.VMEM((block, pad), F32),
            pltpu.VMEM((block, pad), F32),
            pltpu.VMEM((block, pad), F32),
            pltpu.SemaphoreType.DMA((shares,)),
        ],
        flops=2 * tokens * width * wide * 3,
        moved=20 << 20,
    )(*near, *kept, *far, *weights)
    grads, mod_t = main[0], main[1]

    near_hidden, far_hidden = call(
        functools.partial(hidden_kernel, groups, shares),
        "grad_hidden",
        [shape((groups, clips, chunk, width))] * 2,
        [VMEM] + [ANY] * shares,
        [w_scratch, pltpu.VMEM((tokens // 2, wide), BF16), pltpu.SemaphoreType.DMA((shares,))],
        flops=2 * tokens * width * wide,
        moved=8 << 20,
    )(grads, *weights)

    if pieces:
        got = over_space(main[2], 1)

        def own(step, kind):
            return call(
                functools.partial(own_kernel, step, share),
                "grad_w_rows",
                shape((groups, rows, wide), kind),
                [VMEM] * 3,
                flops=2 * tokens * share * wide,
                moved=8 << 20,
            )(mod_t, grads, got)

        crossed = [over_space(own(j, BF16), 2 * j) for j in range(1, lines)]
        mine = own(0, F32)
        spread = call(
            spread_kernel,
            "spread",
            [shape((rows, wide), F32)] + [shape((rows, wide))] * (groups - 1),
            [VMEM] * lines,
            moved=4 << 20,
        )(mine, *crossed)
        summed = call(add_kernel, "sum_z", shape((rows, wide)), [VMEM] * groups)(
            spread[0], *[over_z(spread[k], k) for k in range(1, groups)]
        )
        halves = [summed] + [over_z(summed, k) for k in range(1, groups)]
        others = [over_y(x) for x in halves]
        grad_weight = call(
            functools.partial(weight_kernel, groups, grad_scale_factor),
            "grad_w",
            shape((share, 2 * wide), F32),
            [VMEM] * (2 * groups),
            moved=8 << 20,
        )(*halves, *others)
    else:
        partial = jnp.dot(mod_t, grads, preferred_element_type=F32).astype(BF16)
        summed = lax.psum_scatter(partial, "space", scatter_dimension=0, tiled=True)
        sides = [list(range(side, frames, 2)) for side in range(2)]
        summed = lax.psum(summed, "frame", axis_index_groups=sides)
        other = over_y(summed)
        first = lax.axis_index("frame") % 2 == 0
        low = jnp.where(first, summed, other).reshape(share, 3, half)
        high = jnp.where(first, other, summed).reshape(share, 3, half)
        grad_weight = jnp.concatenate([low, high], axis=2).reshape(share, 2 * wide)
        grad_weight = grad_weight.astype(F32) * grad_scale_factor

    back = call(
        meet_kernel, "meet", [shape((clips, chunk, width))] * groups, [VMEM] * 2, moved=2 << 20
    )(near_hidden, over_y(far_hidden))
    back = [back[0]] + [over_z(back[k], k) for k in range(1, groups)]
    grad_input, sums = call(
        functools.partial(input_kernel, groups),
        "grad_input",
        [shape((clips, positions, width)), shape((clips, 2, width), F32)],
        [VMEM] * (2 + groups),
        moved=2 << 20,
    )(hidden, modulation, *back)
    step = 1
    while step < spaces:
        sums += over_space(sums, step)
        step *= 2
    sums += over_y(sums)
    step = 1
    while step < groups:
        sums += over_z(sums, step)
        step *= 2
    return (grad_input.reshape(hidden_in.shape), grad_weight, sums * grad_scale_factor)


def solution(mesh):
    in_specs = (
        P(None, "frame", "space", None, None),
        P(None, "frame", "space", None, None),
        P("space", None),
        P(),
        P(),
        P(),
        P(),
    )
    out_specs = (P(None, "frame", "space", None, None), P("space", None), P())
    return jax.shard_map(
        per_device, mesh=mesh, in_specs=in_specs, out_specs=out_specs, check_vma=False
    )
```

time: 419 us -> 224 us (0.53)
  blocking collectives: 146 us -> 0 us
  starting transfers between devices: 0.12 us -> 60 us
  waiting for transfers between devices: 174 us -> 134 us
  matrix products: 33.1 us -> 0 us
  local copies, waits for them, and re-layouts: 36.8 us -> 3.87 us
  Pallas kernels: 0 us -> 24.3 us
  other arithmetic: 15.1 us -> 0.67 us
  between operations: 14 us -> 0.81 us
    ppermute x0 -> x34, waiting for transfers between devices: none -> 134 us  [the longest x17 55.1 us: over_z(): return lax.ppermute(x, 'frame', [(i, i ^ 2 * step) for i in range(frames)])]
    all_to_all x2 -> x0, blocking collectives: 104 us -> none  [the longest x1 59.7 us: per_device(): lax.all_to_all(packed, 'frame', split_axis=2, concat_axis=1, tiled=True)]
    reduce_scatter x1 -> x0, waiting for transfers between devices: 67.3 us -> none  [per_device(): lax.psum_scatter(lax.dot_general(mod_rows, grad_rows, (((0,), (0,)), ((),...]
    ppermute x0 -> x34, starting transfers between devices: none -> 60 us  [the longest x17 41 us: over_z(): return lax.ppermute(x, 'frame', [(i, i ^ 2 * step) for i in range(frames)])]
    all_gather x1 -> x0, waiting for transfers between devices: 53.1 us -> none  [per_device(): w_full = lax.all_gather(w_qkv, 'space', axis=0, tiled=True)]
    psum x1 -> x0, waiting for transfers between devices: 52.4 us -> none  [per_device(): lax.psum(row_share, 'frame').astype(jnp.float32) * grad_scale_factor]
    psum x1 -> x0, blocking collectives: 41.3 us -> none  [per_device(): lax.psum(local_sums, ('frame', 'space')) * grad_scale_factor]
    dot_general x8 -> x0, matrix products: 33.1 us -> none  [the longest x1 7.03 us: per_device(): jnp.dot(mod_rows, w_full, preferred_element_type=jnp.float32)]
  transfers between devices with their start and end apart: 3 -> 34, of which waited for: 3 -> 20; matrix products, arithmetic and copies ran while one was open for 4% -> 0% of each run, Pallas kernels for 0% -> 4%
where the time goes in v1:
time: 224 us
  waiting for transfers between devices  134 us (60%)
  starting transfers between devices  60 us (27%)
  Pallas kernels  24.3 us (11%)
  local copies, waits for them, and re-layouts  3.87 us (2%)
    ppermute x17, waiting for transfers between devices, over_z(): return lax.ppermute(x, 'frame', [(i, i ^ 2 * step) for i in range(frames)])  55.1 us
    ppermute x7, waiting for transfers between devices, over_space(): return lax.ppermute(x, 'space', [(i, i ^ step) for i in range(spaces)])  47 us
    ppermute x17, starting transfers between devices, over_z(): return lax.ppermute(x, 'frame', [(i, i ^ 2 * step) for i in range(frames)])  41 us
    ppermute x10, waiting for transfers between devices, over_y(): return lax.ppermute(x, 'frame', [(i, i ^ 1) for i in range(frames)])  32 us
    ppermute x10, starting transfers between devices, over_y(): return lax.ppermute(x, 'frame', [(i, i ^ 1) for i in range(frames)])  12.7 us
    pallas_call x1, Pallas kernels, per_device(): call(functools.partial(main_kernel, groups, shares, lines if pieces else...  11.1 us
    ppermute x7, starting transfers between devices, over_space(): return lax.ppermute(x, 'space', [(i, i ^ step) for i in range(spaces)])  6.26 us
  transfers between devices with their start and end apart: 34, of which 20 were waited for; matrix products, arithmetic and copies ran while one was open for 0% of the time, Pallas kernels for 4%

profile of v1, /device:TPU:0, one launch (start us, length us, event | category | flops | bytes accessed | tf_op | source)
XLA Modules:
  0.0 223.7 jit_solution(13421761072639951947)
XLA Ops:
  2.4 3.0 %collective-permute-start.11 = (bf16[288,1728]{1,0:T(8,128)(2,1)S(1)}, bf16[288,1728]{1,0:T(8,128)(2,1)S(1)}, u32[]{:S(2)}, u32[]{:S(2)}) collective-permute-start(bf16[288,1728]{1,0:T(8,128)(2,1)S(1)} %w_half.1.refs_12_.refs_0_), channel_id=1, source_target_pairs={{0,2},{1,3},{2,0},{3,1},{4,6},{5,7},{6,4},{7,5},{8,10},{9,11},{10,... | collective-permute-start | bytes 2985992 | tf_op jit(solution)/shard_map/ppermute | solution.py:330
  5.4 22.8 %collective-permute-done.11.refs_14_.refs_2_ = bf16[288,1728]{1,0:T(8,128)(2,1)S(1)} collective-permute-done((bf16[288,1728]{1,0:T(8,128)(2,1)S(1)}, bf16[288,1728]{1,0:T(8,128)(2,1)S(1)}, u32[]{:S(2)}, u32[]{:S(2)}) %collective-permute-start.11) | collective-permute-done | bytes 995360 | tf_op jit(solution)/shard_map/ppermute | solution.py:330
  28.3 2.3 %copy-done = bf16[1000,2,1152]{2,1,0:T(2,128)(2,1)S(1)} copy-done((bf16[1000,2,1152]{2,1,0:T(2,128)(2,1)S(1)}, bf16[1000,2,1152]{2,1,0:T(2,128)(2,1)}, u32[]{:S(2)}) %copy-start) | copy-done | bytes 4608024
  30.6 2.2 prep.1
  34.9 2.8 %collective-permute-start.4 = (bf16[2,32,576]{2,1,0:T(8,128)(2,1)S(1)}, bf16[2,32,576]{2,1,0:T(8,128)(2,1)S(1)}, u32[]{:S(2)}, u32[]{:S(2)}) collective-permute-start(bf16[2,32,576]{2,1,0:T(8,128)(2,1)S(1)} %get-tuple-element.34), channel_id=1, source_target_pairs={{0,16},{4,20},{8,24},{12,28},{16,0},{20,4},{24,8},{28,12},{1,17},{... | collective-permute-start | bytes 221192 | tf_op jit(solution)/shard_map/ppermute | solution.py:336
  37.7 6.7 %collective-permute-done.3.refs_5_ = bf16[2,32,576]{2,1,0:T(8,128)(2,1)S(1)} collective-permute-done((bf16[2,32,576]{2,1,0:T(8,128)(2,1)S(1)}, bf16[2,32,576]{2,1,0:T(8,128)(2,1)S(1)}, u32[]{:S(2)}, u32[]{:S(2)}) %collective-permute-start.3) | collective-permute-done | bytes 73760 | tf_op jit(solution)/shard_map/ppermute | solution.py:336
  44.5 3.8 %collective-permute-start.5 = (bf16[2,32,576]{2,1,0:T(8,128)(2,1)S(1)}, bf16[2,32,576]{2,1,0:T(8,128)(2,1)S(1)}, u32[]{:S(2)}, u32[]{:S(2)}) collective-permute-start(bf16[2,32,576]{2,1,0:T(8,128)(2,1)S(1)} %get-tuple-element.35), channel_id=1, source_target_pairs={{0,24},{4,28},{8,16},{12,20},{16,8},{20,12},{24,0},{28,4},{1,25},{... | collective-permute-start | bytes 221192 | tf_op jit(solution)/shard_map/ppermute | solution.py:336
  48.2 3.4 %collective-permute-done.5.refs_7_ = bf16[2,32,576]{2,1,0:T(8,128)(2,1)S(1)} collective-permute-done((bf16[2,32,576]{2,1,0:T(8,128)(2,1)S(1)}, bf16[2,32,576]{2,1,0:T(8,128)(2,1)S(1)}, u32[]{:S(2)}, u32[]{:S(2)}) %collective-permute-start.5) | collective-permute-done | bytes 73760 | tf_op jit(solution)/shard_map/ppermute | solution.py:336
  51.6 3.8 %collective-permute-start.2 = (bf16[2,32,1728]{2,1,0:T(8,128)(2,1)S(1)}, bf16[2,32,1728]{2,1,0:T(8,128)(2,1)S(1)}, u32[]{:S(2)}, u32[]{:S(2)}) collective-permute-start(bf16[2,32,1728]{2,1,0:T(8,128)(2,1)S(1)} %get-tuple-element.31), channel_id=1, source_target_pairs={{0,24},{4,28},{8,16},{12,20},{16,8},{20,12},{24,0},{28,4},{1,25},{... | collective-permute-start | bytes 663560 | tf_op jit(solution)/shard_map/ppermute | solution.py:336
  57.0 8.5 %collective-permute-done.1.refs_2_ = bf16[2,32,1728]{2,1,0:T(8,128)(2,1)S(1)} collective-permute-done((bf16[2,32,1728]{2,1,0:T(8,128)(2,1)S(1)}, bf16[2,32,1728]{2,1,0:T(8,128)(2,1)S(1)}, u32[]{:S(2)}, u32[]{:S(2)}) %collective-permute-start.1) | collective-permute-done | bytes 221216 | tf_op jit(solution)/shard_map/ppermute | solution.py:336
  69.2 4.8 %collective-permute-done.7.refs_9_ = bf16[2,32,1728]{2,1,0:T(8,128)(2,1)S(1)} collective-permute-done((bf16[2,32,1728]{2,1,0:T(8,128)(2,1)S(1)}, bf16[2,32,1728]{2,1,0:T(8,128)(2,1)S(1)}, u32[]{:S(2)}, u32[]{:S(2)}) %collective-permute-start.7) | collective-permute-done | bytes 221216 | tf_op jit(solution)/shard_map/ppermute | solution.py:333
  74.0 4.9 %collective-permute-done.8.refs_10_ = bf16[2,32,1728]{2,1,0:T(8,128)(2,1)S(1)} collective-permute-done((bf16[2,32,1728]{2,1,0:T(8,128)(2,1)S(1)}, bf16[2,32,1728]{2,1,0:T(8,128)(2,1)S(1)}, u32[]{:S(2)}, u32[]{:S(2)}) %collective-permute-start.8) | collective-permute-done | bytes 221216 | tf_op jit(solution)/shard_map/ppermute | solution.py:333
  78.9 3.9 %collective-permute-done.9.refs_11_ = bf16[2,32,1728]{2,1,0:T(8,128)(2,1)S(1)} collective-permute-done((bf16[2,32,1728]{2,1,0:T(8,128)(2,1)S(1)}, bf16[2,32,1728]{2,1,0:T(8,128)(2,1)S(1)}, u32[]{:S(2)}, u32[]{:S(2)}) %collective-permute-start.9) | collective-permute-done | bytes 221216 | tf_op jit(solution)/shard_map/ppermute | solution.py:333
  82.8 11.1 %attend.1 = (bf16[512,1728]{1,0:T(8,128)(2,1)S(1)}, bf16[1152,512]{1,0:T(8,128)(2,1)S(1)}, bf16[2,4,72,1728]{3,2,1,0:T(8,128)(2,1)S(1)}) custom-call(bf16[2,32,1728]{2,1,0:T(8,128)(2,1)S(1)} %get-tuple-element.28.refs_0_, bf16[2,32,1728]{2,1,0:T(8,128)(2,1)S(1)} %collective-permute-done.refs_1_, bf16[2,32,1728]{2,1,0:T(8,128)(2,1)S(1)} %collective-permute-done.1.refs_2_, ...), custom_call_target="tpu_custom_call" | custom-call | flops 6115295232 | bytes 20971520 | tf_op jit(solution)/shard_map/attend/pallas_call | solution.py:370
  94.0 4.1 %collective-permute-done.17.got = bf16[2,4,72,1728]{3,2,1,0:T(8,128)(2,1)S(1)} collective-permute-done((bf16[2,4,72,1728]{3,2,1,0:T(8,128)(2,1)S(1)}, bf16[2,4,72,1728]{3,2,1,0:T(8,128)(2,1)S(1)}, u32[]{:S(2)}, u32[]{:S(2)}) %collective-permute-start.17) | collective-permute-done | bytes 1990688 | tf_op jit(solution)/shard_map/ppermute | solution.py:330
  100.4 4.3 %grad_hidden.1 = (bf16[4,2,32,1152]{3,2,1,0:T(8,128)(2,1)S(1)}, bf16[4,2,32,1152]{3,2,1,0:T(8,128)(2,1)S(1)}) custom-call(bf16[512,1728]{1,0:T(8,128)(2,1)S(1)} %get-tuple-element.36.grads, bf16[288,1728]{1,0:T(8,128)(2,1)S(1)} %w_half.1.refs_12_.refs_0_, bf16[288,1728]{1,0:T(8,128)(2,1)S(1)} %collective-permute-done.10.refs_13_.refs_1_, ...), custom_call_target="tpu_custom_call" | custom-call | flops 2038431744 | bytes 8388608 | tf_op jit(solution)/shard_map/grad_hidden/pallas_call | solution.py:392
  107.1 16.7 %collective-permute-done.18.refs_0_ = bf16[4,72,1728]{2,1,0:T(8,128)(2,1)S(1)} collective-permute-done((bf16[4,72,1728]{2,1,0:T(8,128)(2,1)S(1)}, bf16[4,72,1728]{2,1,0:T(8,128)(2,1)S(1)}, u32[]{:S(2)}, u32[]{:S(2)}) %collective-permute-start.18) | collective-permute-done | bytes 995360 | tf_op jit(solution)/shard_map/ppermute | solution.py:330
  128.7 9.5 %collective-permute-done.19.refs_0_ = bf16[72,1728]{1,0:T(8,128)(2,1)S(1)} collective-permute-done((bf16[72,1728]{1,0:T(8,128)(2,1)S(1)}, bf16[72,1728]{1,0:T(8,128)(2,1)S(1)}, u32[]{:S(2)}, u32[]{:S(2)}) %collective-permute-start.19) | collective-permute-done | bytes 248864 | tf_op jit(solution)/shard_map/ppermute | solution.py:336
  138.2 7.5 %collective-permute-done.20.refs_1_ = bf16[72,1728]{1,0:T(8,128)(2,1)S(1)} collective-permute-done((bf16[72,1728]{1,0:T(8,128)(2,1)S(1)}, bf16[72,1728]{1,0:T(8,128)(2,1)S(1)}, u32[]{:S(2)}, u32[]{:S(2)}) %collective-permute-start.20) | collective-permute-done | bytes 248864 | tf_op jit(solution)/shard_map/ppermute | solution.py:336
  145.9 2.0 collective-permute-start.24
  147.9 12.5 %collective-permute-start.23 = (bf16[72,1728]{1,0:T(8,128)(2,1)S(1)}, bf16[72,1728]{1,0:T(8,128)(2,1)S(1)}, u32[]{:S(2)}, u32[]{:S(2)}) collective-permute-start(bf16[72,1728]{1,0:T(8,128)(2,1)S(1)} %sum_z.1.refs_0_), channel_id=1, source_target_pairs={{0,16},{4,20},{8,24},{12,28},{16,0},{20,4},{24,8},{28,12},{1,17},{... | collective-permute-start | bytes 746504 | tf_op jit(solution)/shard_map/ppermute | solution.py:336
  160.5 2.5 %collective-permute-start.15 = (bf16[2,32,1152]{2,1,0:T(8,128)(2,1)S(1)}, bf16[2,32,1152]{2,1,0:T(8,128)(2,1)S(1)}, u32[]{:S(2)}, u32[]{:S(2)}) collective-permute-start(bf16[2,32,1152]{2,1,0:T(8,128)(2,1)S(1)} %get-tuple-element.41), channel_id=1, source_target_pairs={{0,16},{4,20},{8,24},{12,28},{16,0},{20,4},{24,8},{28,12},{1,17},{... | collective-permute-start | bytes 442376 | tf_op jit(solution)/shard_map/ppermute | solution.py:336
  164.8 17.7 %collective-permute-done.15.refs_2_ = bf16[2,32,1152]{2,1,0:T(8,128)(2,1)S(1)} collective-permute-done((bf16[2,32,1152]{2,1,0:T(8,128)(2,1)S(1)}, bf16[2,32,1152]{2,1,0:T(8,128)(2,1)S(1)}, u32[]{:S(2)}, u32[]{:S(2)}) %collective-permute-start.15) | collective-permute-done | bytes 147488 | tf_op jit(solution)/shard_map/ppermute | solution.py:336
  187.1 2.2 collective-permute-done.30
  191.1 2.1 collective-permute-done.31
  193.2 2.2 collective-permute-start.32
  197.2 2.8 %collective-permute-start.33 = (f32[2,2,1152]{2,1,0:T(2,128)S(1)}, f32[2,2,1152]{2,1,0:T(2,128)S(1)}, u32[]{:S(2)}, u32[]{:S(2)}) collective-permute-start(f32[2,2,1152]{2,1,0:T(2,128)S(1)} %add.18), channel_id=1, source_target_pairs={{0,16},{4,20},{8,24},{12,28},{16,0},{20,4},{24,8},{28,12},{1,17},{... | collective-permute-start | bytes 55304 | tf_op jit(solution)/shard_map/ppermute | solution.py:336
  204.6 4.5 %collective-permute-done.25.refs_4_ = bf16[72,1728]{1,0:T(8,128)(2,1)S(1)} collective-permute-done((bf16[72,1728]{1,0:T(8,128)(2,1)S(1)}, bf16[72,1728]{1,0:T(8,128)(2,1)S(1)}, u32[]{:S(2)}, u32[]{:S(2)}) %collective-permute-start.25) | collective-permute-done | bytes 248864 | tf_op jit(solution)/shard_map/ppermute | solution.py:333
  209.1 5.5 %collective-permute-done.28.refs_7_ = bf16[72,1728]{1,0:T(8,128)(2,1)S(1)} collective-permute-done((bf16[72,1728]{1,0:T(8,128)(2,1)S(1)}, bf16[72,1728]{1,0:T(8,128)(2,1)S(1)}, u32[]{:S(2)}, u32[]{:S(2)}) %collective-permute-start.28) | collective-permute-done | bytes 248864 | tf_op jit(solution)/shard_map/ppermute | solution.py:333
  214.6 3.5 %collective-permute-done.27.refs_6_ = bf16[72,1728]{1,0:T(8,128)(2,1)S(1)} collective-permute-done((bf16[72,1728]{1,0:T(8,128)(2,1)S(1)}, bf16[72,1728]{1,0:T(8,128)(2,1)S(1)}, u32[]{:S(2)}, u32[]{:S(2)}) %collective-permute-start.27) | collective-permute-done | bytes 248864 | tf_op jit(solution)/shard_map/ppermute | solution.py:333
  218.1 2.8 %collective-permute-done.26.refs_5_ = bf16[72,1728]{1,0:T(8,128)(2,1)S(1)} collective-permute-done((bf16[72,1728]{1,0:T(8,128)(2,1)S(1)}, bf16[72,1728]{1,0:T(8,128)(2,1)S(1)}, u32[]{:S(2)}, u32[]{:S(2)}) %collective-permute-start.26) | collective-permute-done | bytes 248864 | tf_op jit(solution)/shard_map/ppermute | solution.py:333
  220.9 2.8 %grad_w.1 = f32[288,3456]{1,0:T(8,128)} custom-call(bf16[72,1728]{1,0:T(8,128)(2,1)S(1)} %sum_z.1.refs_0_, bf16[72,1728]{1,0:T(8,128)(2,1)S(1)} %collective-permute-done.22.refs_1_, bf16[72,1728]{1,0:T(8,128)(2,1)S(1)} %collective-permute-done.23.refs_2_, bf16[72,1728]{1,0:T(8,128)(2,1)S(1)} %collective-permute-done.24.refs_3_, ...), custom_call_target="tpu_custom_call" | custom-call | bytes 8388608 | tf_op jit(solution)/shard_map/grad_w/pallas_call | solution.py:429
  (66 shorter events, 33.6 us)
Async XLA Ops:
  2.4 25.8 %collective-permute-start.11 = (bf16[288,1728]{1,0:T(8,128)(2,1)S(1)}, bf16[288,1728]{1,0:T(8,128)(2,1)S(1)}, u32[]{:S(2)}, u32[]{:S(2)}) collective-permute-start(bf16[288,1728]{1,0:T(8,128)(2,1)S(1)} %w_half.1.refs_12_.refs_0_), channel_id=1, source_target_pairs={{0,2},{1,3},{2,0},{3,1},{4,6},{5,7},{6,4},{7,5},{8,10},{9,11},{10,... | collective-permute-start | bytes 2985992 | tf_op jit(solution)/shard_map/ppermute | solution.py:330
  5.4 77.4 %collective-permute-start.10 = (bf16[288,1728]{1,0:T(8,128)(2,1)S(1)}, bf16[288,1728]{1,0:T(8,128)(2,1)S(1)}, u32[]{:S(2)}, u32[]{:S(2)}) collective-permute-start(bf16[288,1728]{1,0:T(8,128)(2,1)S(1)} %w_half.1.refs_12_.refs_0_), channel_id=1, source_target_pairs={{0,1},{1,0},{2,3},{3,2},{4,5},{5,4},{6,7},{7,6},{8,9},{9,8},{10,11... | collective-permute-start | bytes 2985992 | tf_op jit(solution)/shard_map/ppermute | solution.py:330
  28.2 54.6 %collective-permute-start.12 = (bf16[288,1728]{1,0:T(8,128)(2,1)S(1)}, bf16[288,1728]{1,0:T(8,128)(2,1)S(1)}, u32[]{:S(2)}, u32[]{:S(2)}) collective-permute-start(bf16[288,1728]{1,0:T(8,128)(2,1)S(1)} %collective-permute-done.11.refs_14_.refs_2_), channel_id=1, source_target_pairs={{0,1},{1,0},{2,3},{3,2},{4,5},{5,4},{6,7},{7,6},{8,9},{9,8},{10,11... | collective-permute-start | bytes 2985992 | tf_op jit(solution)/shard_map/ppermute | solution.py:330
  32.8 22.6 %collective-permute-start = (bf16[2,32,1728]{2,1,0:T(8,128)(2,1)S(1)}, bf16[2,32,1728]{2,1,0:T(8,128)(2,1)S(1)}, u32[]{:S(2)}, u32[]{:S(2)}) collective-permute-start(bf16[2,32,1728]{2,1,0:T(8,128)(2,1)S(1)} %get-tuple-element.29), channel_id=1, source_target_pairs={{0,8},{4,12},{8,0},{12,4},{16,24},{20,28},{24,16},{28,20},{1,9},{5... | collective-permute-start | bytes 663560 | tf_op jit(solution)/shard_map/ppermute | solution.py:336
  34.7 9.8 %collective-permute-start.3 = (bf16[2,32,576]{2,1,0:T(8,128)(2,1)S(1)}, bf16[2,32,576]{2,1,0:T(8,128)(2,1)S(1)}, u32[]{:S(2)}, u32[]{:S(2)}) collective-permute-start(bf16[2,32,576]{2,1,0:T(8,128)(2,1)S(1)} %get-tuple-element.33), channel_id=1, source_target_pairs={{0,8},{4,12},{8,0},{12,4},{16,24},{20,28},{24,16},{28,20},{1,9},{5... | collective-permute-start | bytes 221192 | tf_op jit(solution)/shard_map/ppermute | solution.py:336
  34.9 13.3 %collective-permute-start.4 = (bf16[2,32,576]{2,1,0:T(8,128)(2,1)S(1)}, bf16[2,32,576]{2,1,0:T(8,128)(2,1)S(1)}, u32[]{:S(2)}, u32[]{:S(2)}) collective-permute-start(bf16[2,32,576]{2,1,0:T(8,128)(2,1)S(1)} %get-tuple-element.34), channel_id=1, source_target_pairs={{0,16},{4,20},{8,24},{12,28},{16,0},{20,4},{24,8},{28,12},{1,17},{... | collective-permute-start | bytes 221192 | tf_op jit(solution)/shard_map/ppermute | solution.py:336
  44.5 7.1 %collective-permute-start.5 = (bf16[2,32,576]{2,1,0:T(8,128)(2,1)S(1)}, bf16[2,32,576]{2,1,0:T(8,128)(2,1)S(1)}, u32[]{:S(2)}, u32[]{:S(2)}) collective-permute-start(bf16[2,32,576]{2,1,0:T(8,128)(2,1)S(1)} %get-tuple-element.35), channel_id=1, source_target_pairs={{0,24},{4,28},{8,16},{12,20},{16,8},{20,12},{24,0},{28,4},{1,25},{... | collective-permute-start | bytes 221192 | tf_op jit(solution)/shard_map/ppermute | solution.py:336
  48.2 17.3 %collective-permute-start.1 = (bf16[2,32,1728]{2,1,0:T(8,128)(2,1)S(1)}, bf16[2,32,1728]{2,1,0:T(8,128)(2,1)S(1)}, u32[]{:S(2)}, u32[]{:S(2)}) collective-permute-start(bf16[2,32,1728]{2,1,0:T(8,128)(2,1)S(1)} %get-tuple-element.30), channel_id=1, source_target_pairs={{0,16},{4,20},{8,24},{12,28},{16,0},{20,4},{24,8},{28,12},{1,17},{... | collective-permute-start | bytes 663560 | tf_op jit(solution)/shard_map/ppermute | solution.py:336
  51.6 15.6 %collective-permute-start.2 = (bf16[2,32,1728]{2,1,0:T(8,128)(2,1)S(1)}, bf16[2,32,1728]{2,1,0:T(8,128)(2,1)S(1)}, u32[]{:S(2)}, u32[]{:S(2)}) collective-permute-start(bf16[2,32,1728]{2,1,0:T(8,128)(2,1)S(1)} %get-tuple-element.31), channel_id=1, source_target_pairs={{0,24},{4,28},{8,16},{12,20},{16,8},{20,12},{24,0},{28,4},{1,25},{... | collective-permute-start | bytes 663560 | tf_op jit(solution)/shard_map/ppermute | solution.py:336
  55.4 12.1 %collective-permute-start.6 = (bf16[2,32,1728]{2,1,0:T(8,128)(2,1)S(1)}, bf16[2,32,1728]{2,1,0:T(8,128)(2,1)S(1)}, u32[]{:S(2)}, u32[]{:S(2)}) collective-permute-start(bf16[2,32,1728]{2,1,0:T(8,128)(2,1)S(1)} %get-tuple-element.28.refs_0_), channel_id=1, source_target_pairs={{0,4},{4,0},{8,12},{12,8},{16,20},{20,16},{24,28},{28,24},{1,5},{5... | collective-permute-start | bytes 663560 | tf_op jit(solution)/shard_map/ppermute | solution.py:333
  65.5 8.5 %collective-permute-start.7 = (bf16[2,32,1728]{2,1,0:T(8,128)(2,1)S(1)}, bf16[2,32,1728]{2,1,0:T(8,128)(2,1)S(1)}, u32[]{:S(2)}, u32[]{:S(2)}) collective-permute-start(bf16[2,32,1728]{2,1,0:T(8,128)(2,1)S(1)} %collective-permute-done.refs_1_), channel_id=1, source_target_pairs={{0,4},{4,0},{8,12},{12,8},{16,20},{20,16},{24,28},{28,24},{1,5},{5... | collective-permute-start | bytes 663560 | tf_op jit(solution)/shard_map/ppermute | solution.py:333
  67.2 11.8 %collective-permute-start.8 = (bf16[2,32,1728]{2,1,0:T(8,128)(2,1)S(1)}, bf16[2,32,1728]{2,1,0:T(8,128)(2,1)S(1)}, u32[]{:S(2)}, u32[]{:S(2)}) collective-permute-start(bf16[2,32,1728]{2,1,0:T(8,128)(2,1)S(1)} %collective-permute-done.1.refs_2_), channel_id=1, source_target_pairs={{0,4},{4,0},{8,12},{12,8},{16,20},{20,16},{24,28},{28,24},{1,5},{5... | collective-permute-start | bytes 663560 | tf_op jit(solution)/shard_map/ppermute | solution.py:333
  67.6 15.2 %collective-permute-start.9 = (bf16[2,32,1728]{2,1,0:T(8,128)(2,1)S(1)}, bf16[2,32,1728]{2,1,0:T(8,128)(2,1)S(1)}, u32[]{:S(2)}, u32[]{:S(2)}) collective-permute-start(bf16[2,32,1728]{2,1,0:T(8,128)(2,1)S(1)} %collective-permute-done.2.refs_3_), channel_id=1, source_target_pairs={{0,4},{4,0},{8,12},{12,8},{16,20},{20,16},{24,28},{28,24},{1,5},{5... | collective-permute-start | bytes 663560 | tf_op jit(solution)/shard_map/ppermute | solution.py:333
  94.0 4.2 %collective-permute-start.17 = (bf16[2,4,72,1728]{3,2,1,0:T(8,128)(2,1)S(1)}, bf16[2,4,72,1728]{3,2,1,0:T(8,128)(2,1)S(1)}, u32[]{:S(2)}, u32[]{:S(2)}) collective-permute-start(bf16[2,4,72,1728]{3,2,1,0:T(8,128)(2,1)S(1)} %get-tuple-element.45), channel_id=1, source_target_pairs={{0,1},{1,0},{2,3},{3,2},{4,5},{5,4},{6,7},{7,6},{8,9},{9,8},{10,11... | collective-permute-start | bytes 5971976 | tf_op jit(solution)/shard_map/ppermute | solution.py:330
  98.8 24.9 %collective-permute-start.18 = (bf16[4,72,1728]{2,1,0:T(8,128)(2,1)S(1)}, bf16[4,72,1728]{2,1,0:T(8,128)(2,1)S(1)}, u32[]{:S(2)}, u32[]{:S(2)}) collective-permute-start(bf16[4,72,1728]{2,1,0:T(8,128)(2,1)S(1)} %grad_w_rows.3), channel_id=1, source_target_pairs={{0,2},{1,3},{2,0},{3,1},{4,6},{5,7},{6,4},{7,5},{8,10},{9,11},{10,... | collective-permute-start | bytes 2985992 | tf_op jit(solution)/shard_map/ppermute | solution.py:330
  104.7 23.7 %collective-permute-start.13 = (bf16[4,2,32,1152]{3,2,1,0:T(8,128)(2,1)S(1)}, bf16[4,2,32,1152]{3,2,1,0:T(8,128)(2,1)S(1)}, u32[]{:S(2)}, u32[]{:S(2)}) collective-permute-start(bf16[4,2,32,1152]{3,2,1,0:T(8,128)(2,1)S(1)} %get-tuple-element.38), channel_id=1, source_target_pairs={{0,4},{4,0},{8,12},{12,8},{16,20},{20,16},{24,28},{28,24},{1,5},{5... | collective-permute-start | bytes 1769480 | tf_op jit(solution)/shard_map/ppermute | solution.py:333
  124.0 14.2 %collective-permute-start.19 = (bf16[72,1728]{1,0:T(8,128)(2,1)S(1)}, bf16[72,1728]{1,0:T(8,128)(2,1)S(1)}, u32[]{:S(2)}, u32[]{:S(2)}) collective-permute-start(bf16[72,1728]{1,0:T(8,128)(2,1)S(1)} %get-tuple-element.47), channel_id=1, source_target_pairs={{0,8},{4,12},{8,0},{12,4},{16,24},{20,28},{24,16},{28,20},{1,9},{5... | collective-permute-start | bytes 746504 | tf_op jit(solution)/shard_map/ppermute | solution.py:336
  124.6 21.2 %collective-permute-start.20 = (bf16[72,1728]{1,0:T(8,128)(2,1)S(1)}, bf16[72,1728]{1,0:T(8,128)(2,1)S(1)}, u32[]{:S(2)}, u32[]{:S(2)}) collective-permute-start(bf16[72,1728]{1,0:T(8,128)(2,1)S(1)} %get-tuple-element.48), channel_id=1, source_target_pairs={{0,16},{4,20},{8,24},{12,28},{16,0},{20,4},{24,8},{28,12},{1,17},{... | collective-permute-start | bytes 746504 | tf_op jit(solution)/shard_map/ppermute | solution.py:336
  126.6 19.2 %collective-permute-start.21 = (bf16[72,1728]{1,0:T(8,128)(2,1)S(1)}, bf16[72,1728]{1,0:T(8,128)(2,1)S(1)}, u32[]{:S(2)}, u32[]{:S(2)}) collective-permute-start(bf16[72,1728]{1,0:T(8,128)(2,1)S(1)} %get-tuple-element.49), channel_id=1, source_target_pairs={{0,24},{4,28},{8,16},{12,20},{16,8},{20,12},{24,0},{28,4},{1,25},{... | collective-permute-start | bytes 746504 | tf_op jit(solution)/shard_map/ppermute | solution.py:336
  128.6 34.4 %collective-permute-start.14 = (bf16[2,32,1152]{2,1,0:T(8,128)(2,1)S(1)}, bf16[2,32,1152]{2,1,0:T(8,128)(2,1)S(1)}, u32[]{:S(2)}, u32[]{:S(2)}) collective-permute-start(bf16[2,32,1152]{2,1,0:T(8,128)(2,1)S(1)} %get-tuple-element.40), channel_id=1, source_target_pairs={{0,8},{4,12},{8,0},{12,4},{16,24},{20,28},{24,16},{28,20},{1,9},{5... | collective-permute-start | bytes 442376 | tf_op jit(solution)/shard_map/ppermute | solution.py:336
  145.9 55.6 %collective-permute-start.24 = (bf16[72,1728]{1,0:T(8,128)(2,1)S(1)}, bf16[72,1728]{1,0:T(8,128)(2,1)S(1)}, u32[]{:S(2)}, u32[]{:S(2)}) collective-permute-start(bf16[72,1728]{1,0:T(8,128)(2,1)S(1)} %sum_z.1.refs_0_), channel_id=1, source_target_pairs={{0,24},{4,28},{8,16},{12,20},{16,8},{20,12},{24,0},{28,4},{1,25},{... | collective-permute-start | bytes 746504 | tf_op jit(solution)/shard_map/ppermute | solution.py:336
  147.9 54.1 %collective-permute-start.23 = (bf16[72,1728]{1,0:T(8,128)(2,1)S(1)}, bf16[72,1728]{1,0:T(8,128)(2,1)S(1)}, u32[]{:S(2)}, u32[]{:S(2)}) collective-permute-start(bf16[72,1728]{1,0:T(8,128)(2,1)S(1)} %sum_z.1.refs_0_), channel_id=1, source_target_pairs={{0,16},{4,20},{8,24},{12,28},{16,0},{20,4},{24,8},{28,12},{1,17},{... | collective-permute-start | bytes 746504 | tf_op jit(solution)/shard_map/ppermute | solution.py:336
  160.5 43.1 %collective-permute-start.22 = (bf16[72,1728]{1,0:T(8,128)(2,1)S(1)}, bf16[72,1728]{1,0:T(8,128)(2,1)S(1)}, u32[]{:S(2)}, u32[]{:S(2)}) collective-permute-start(bf16[72,1728]{1,0:T(8,128)(2,1)S(1)} %sum_z.1.refs_0_), channel_id=1, source_target_pairs={{0,8},{4,12},{8,0},{12,4},{16,24},{20,28},{24,16},{28,20},{1,9},{5... | collective-permute-start | bytes 746504 | tf_op jit(solution)/shard_map/ppermute | solution.py:336
  160.5 22.1 %collective-permute-start.15 = (bf16[2,32,1152]{2,1,0:T(8,128)(2,1)S(1)}, bf16[2,32,1152]{2,1,0:T(8,128)(2,1)S(1)}, u32[]{:S(2)}, u32[]{:S(2)}) collective-permute-start(bf16[2,32,1152]{2,1,0:T(8,128)(2,1)S(1)} %get-tuple-element.41), channel_id=1, source_target_pairs={{0,16},{4,20},{8,24},{12,28},{16,0},{20,4},{24,8},{28,12},{1,17},{... | collective-permute-start | bytes 442376 | tf_op jit(solution)/shard_map/ppermute | solution.py:336
  163.0 19.5 %collective-permute-start.16 = (bf16[2,32,1152]{2,1,0:T(8,128)(2,1)S(1)}, bf16[2,32,1152]{2,1,0:T(8,128)(2,1)S(1)}, u32[]{:S(2)}, u32[]{:S(2)}) collective-permute-start(bf16[2,32,1152]{2,1,0:T(8,128)(2,1)S(1)} %get-tuple-element.42), channel_id=1, source_target_pairs={{0,24},{4,28},{8,16},{12,20},{16,8},{20,12},{24,0},{28,4},{1,25},{... | collective-permute-start | bytes 442376 | tf_op jit(solution)/shard_map/ppermute | solution.py:336
  185.5 3.8 %collective-permute-start.30 = (f32[2,2,1152]{2,1,0:T(2,128)S(1)}, f32[2,2,1152]{2,1,0:T(2,128)S(1)}, u32[]{:S(2)}, u32[]{:S(2)}) collective-permute-start(f32[2,2,1152]{2,1,0:T(2,128)S(1)} %add.15), channel_id=1, source_target_pairs={{0,2},{1,3},{2,0},{3,1},{4,6},{5,7},{6,4},{7,5},{8,10},{9,11},{10,... | collective-permute-start | bytes 55304 | tf_op jit(solution)/shard_map/ppermute | solution.py:330
  193.2 3.9 %collective-permute-start.32 = (f32[2,2,1152]{2,1,0:T(2,128)S(1)}, f32[2,2,1152]{2,1,0:T(2,128)S(1)}, u32[]{:S(2)}, u32[]{:S(2)}) collective-permute-start(f32[2,2,1152]{2,1,0:T(2,128)S(1)} %add.17), channel_id=1, source_target_pairs={{0,8},{4,12},{8,0},{12,4},{16,24},{20,28},{24,16},{28,20},{1,9},{5... | collective-permute-start | bytes 55304 | tf_op jit(solution)/shard_map/ppermute | solution.py:336
  197.2 6.8 %collective-permute-start.33 = (f32[2,2,1152]{2,1,0:T(2,128)S(1)}, f32[2,2,1152]{2,1,0:T(2,128)S(1)}, u32[]{:S(2)}, u32[]{:S(2)}) collective-permute-start(f32[2,2,1152]{2,1,0:T(2,128)S(1)} %add.18), channel_id=1, source_target_pairs={{0,16},{4,20},{8,24},{12,28},{16,0},{20,4},{24,8},{28,12},{1,17},{... | collective-permute-start | bytes 55304 | tf_op jit(solution)/shard_map/ppermute | solution.py:336
  199.9 9.2 %collective-permute-start.25 = (bf16[72,1728]{1,0:T(8,128)(2,1)S(1)}, bf16[72,1728]{1,0:T(8,128)(2,1)S(1)}, u32[]{:S(2)}, u32[]{:S(2)}) collective-permute-start(bf16[72,1728]{1,0:T(8,128)(2,1)S(1)} %sum_z.1.refs_0_), channel_id=1, source_target_pairs={{0,4},{4,0},{8,12},{12,8},{16,20},{20,16},{24,28},{28,24},{1,5},{5... | collective-permute-start | bytes 746504 | tf_op jit(solution)/shard_map/ppermute | solution.py:333
  201.5 13.1 %collective-permute-start.28 = (bf16[72,1728]{1,0:T(8,128)(2,1)S(1)}, bf16[72,1728]{1,0:T(8,128)(2,1)S(1)}, u32[]{:S(2)}, u32[]{:S(2)}) collective-permute-start(bf16[72,1728]{1,0:T(8,128)(2,1)S(1)} %collective-permute-done.24.refs_3_), channel_id=1, source_target_pairs={{0,4},{4,0},{8,12},{12,8},{16,20},{20,16},{24,28},{28,24},{1,5},{5... | collective-permute-start | bytes 746504 | tf_op jit(solution)/shard_map/ppermute | solution.py:333
  202.0 16.2 %collective-permute-start.27 = (bf16[72,1728]{1,0:T(8,128)(2,1)S(1)}, bf16[72,1728]{1,0:T(8,128)(2,1)S(1)}, u32[]{:S(2)}, u32[]{:S(2)}) collective-permute-start(bf16[72,1728]{1,0:T(8,128)(2,1)S(1)} %collective-permute-done.23.refs_2_), channel_id=1, source_target_pairs={{0,4},{4,0},{8,12},{12,8},{16,20},{20,16},{24,28},{28,24},{1,5},{5... | collective-permute-start | bytes 746504 | tf_op jit(solution)/shard_map/ppermute | solution.py:333
  203.5 17.4 %collective-permute-start.26 = (bf16[72,1728]{1,0:T(8,128)(2,1)S(1)}, bf16[72,1728]{1,0:T(8,128)(2,1)S(1)}, u32[]{:S(2)}, u32[]{:S(2)}) collective-permute-start(bf16[72,1728]{1,0:T(8,128)(2,1)S(1)} %collective-permute-done.22.refs_1_), channel_id=1, source_target_pairs={{0,4},{4,0},{8,12},{12,8},{16,20},{20,16},{24,28},{28,24},{1,5},{5... | collective-permute-start | bytes 746504 | tf_op jit(solution)/shard_map/ppermute | solution.py:333
  (9 other events, 139.0 us)

commit v2 on v1

--- a/solution.py
+++ b/solution.py
@@ -52,6 +52,10 @@
 ROWS_ROWS = (((1,), (1,)), ((), ()))
 
 
+def after(x, *others):
+    return lax.optimization_barrier((x, *others))[0]
+
+
 def pick(cond, a, b):
     return jnp.where(cond, a, b)
 
@@ -83,8 +87,8 @@
 
 
 def prep_kernel(groups, h_ref, c_ref, tab_ref, ts_ref, snr_ref, wi_ref, *rest):
-    send, keep = rest[:groups], rest[groups : 2 * groups]
-    mod_ref, scratch, sems = rest[2 * groups :]
+    send = rest[:groups]
+    mod_ref, scratch, sems = rest[groups:]
     z, y, _ = place()
     clips, positions, width = h_ref.shape
     chunk, half = positions // groups, width // 2
@@ -107,14 +111,14 @@
             send[k][b, :, :width] = (normed * scale + shift).astype(BF16)
             up = c_ref[b, rows, :].astype(F32) * weight
             low, high = up[:, :half], up[:, half:]
-            send[k][b, :, width:] = pick(y == 0, high, low).astype(BF16)
-            keep[k][b] = pick(y == 0, low, high).astype(BF16)
+            send[k][b, :, width : width + half] = pick(y == 0, high, low).astype(BF16)
+            send[k][b, :, width + half :] = pick(y == 0, low, high).astype(BF16)
 
 
 def main_kernel(groups, shares, others, *refs):
-    near, kept, far = refs[:groups], refs[groups : 2 * groups], refs[2 * groups : 3 * groups]
-    weights = refs[3 * groups : 3 * groups + shares]
-    rest = refs[3 * groups + shares :]
+    near, far = refs[:groups], refs[groups : 2 * groups]
+    weights = refs[2 * groups : 2 * groups + shares]
+    rest = refs[2 * groups + shares :]
     outs, scratches = rest[: 2 + (others > 0)], rest[2 + (others > 0) :]
     grads, mod_t = outs[0], outs[1]
     w, mod, up, qw, kw, vw, dq, dk, dv, sems = scratches
@@ -139,10 +143,10 @@
             for k in range(groups):
                 own = slice(base + k * SLAB, base + (k + 1) * SLAB)
                 mod[own, :] = near[k][b, take, :depth]
-                up[own, :half] = kept[k][b, take, :]
+                up[own, :half] = near[k][b, take, depth + half :]
                 its = slice(base + (groups + k) * SLAB, base + (groups + k + 1) * SLAB)
                 mod[its, :] = far[k][b, take, :depth]
-                up[its, :half] = far[k][b, take, depth:]
+                up[its, :half] = far[k][b, take, depth : depth + half]
     up[:, half:] = jnp.zeros((up.shape[0], pad - half), BF16)
     vw[:, half:] = jnp.zeros((block, pad - half), BF16)
     for copy in copies:
@@ -287,11 +291,43 @@
         outs[k][...] = total.astype(outs[k].dtype)
 
 
-def add_kernel(own, *refs):
-    total = own[...]
-    for other in refs[:-1]:
+def add_kernel(*refs):
+    total = refs[0][...].astype(F32)
+    for other in refs[1:-1]:
         total += other[...].astype(F32)
-    refs[-1][...] = total.astype(BF16)
+    refs[-1][...] = total.astype(refs[-1].dtype)
+
+
+def reduce_z(terms, over_z, beside):
+    dims = terms[0].shape
+
+    def total(parts):
+        return call(add_kernel, "sum_z", shape(dims), [VMEM] * len(parts))(*parts)
+
+    step = 1
+    parts = [[x] for x in terms]
+    while len(parts) > 1:
+        for d in reversed(range(1, len(parts), 2)):
+            send = parts[d][0] if step == 1 else total(parts[d])
+            got = over_z(send, step)
+            if beside and (step > 1 or d == len(parts) - 1):
+                got = after(got, beside.pop(0))
+            parts[d - 1].append(got)
+        parts = parts[::2]
+        step *= 2
+    return total(parts[0])
+
+
+def gather_z(summed, groups, over_z, over_y):
+    held = [summed] + [None] * (groups - 1)
+    other = [over_y(summed)] + [None] * (groups - 1)
+    step = groups // 2
+    while step:
+        for k in range(0, groups, 2 * step):
+            held[k ^ step] = after(over_z(held[k], step), other[0])
+            other[k ^ step] = over_y(held[k ^ step])
+        step //= 2
+    return held, other
 
 
 def weight_kernel(groups, scale, *refs):
@@ -340,27 +376,27 @@
 
     w_half = call(halves_kernel, "w_half", shape((share, wide)), [VMEM], moved=3 << 20)(w_qkv)
     if pieces:
-        weights = [w_half, over_space(w_half, 1)]
-        for j in range(1, lines):
-            crossed = over_space(w_half, 2 * j)
-            weights += [crossed, over_space(crossed, 1)]
-    else:
-        weights = [lax.all_gather(w_half, "space", axis=0, tiled=True)]
+        crossed = [over_space(w_half, 2 * j) for j in range(1, lines)]
 
     prep = call(
         functools.partial(prep_kernel, groups),
         "prep",
-        [shape((clips, chunk, width + half))] * groups
-        + [shape((clips, chunk, half))] * groups
-        + [shape((clips, 2, width), F32)],
+        [shape((clips, chunk, 2 * width))] * groups + [shape((clips, 2, width), F32)],
         [VMEM, VMEM, ANY, SMEM, SMEM, SMEM],
         [pltpu.VMEM((clips, 2, width), BF16), pltpu.SemaphoreType.DMA((clips,))],
         moved=3 << 20,
     )(hidden, cotangent, modulation_table, timestep, snr_table, weight_index)
-    send, keep, modulation = prep[:groups], prep[groups : 2 * groups], prep[-1]
+    send, modulation = prep[:groups], prep[-1]
     near = [send[0]] + [over_z(send[k], k) for k in range(1, groups)]
-    far = [over_y(x) for x in near]
-    kept = [keep[0]] + [over_z(keep[k], k) for k in range(1, groups)]
+    far = [over_y(near[0])]
+    near[1:-1] = lax.optimization_barrier((far[0], *near[1:-1]))[1:]
+    far += [over_y(x) for x in near[1:]]
+    if pieces:
+        weights = [w_half, over_space(w_half, 1)]
+        for x in crossed:
+            weights += [x, over_space(after(x, near[-1], *far[1:-1]), 1)]
+    else:
+        weights = [lax.all_gather(w_half, "space", axis=0, tiled=True)]
 
     pad = -(-half // LANES) * LANES
     outs = [shape((tokens, wide)), shape((width, tokens))]
@@ -371,7 +407,7 @@
         functools.partial(main_kernel, groups, shares, lines if pieces else 0),
         "attend",
         outs,
-        [VMEM] * (3 * groups) + [ANY] * shares,
+        [VMEM] * (2 * groups) + [ANY] * shares,
         [
             w_scratch,
             pltpu.VMEM((tokens, width), BF16),
@@ -386,7 +422,7 @@
         ],
         flops=2 * tokens * width * wide * 3,
         moved=20 << 20,
-    )(*near, *kept, *far, *weights)
+    )(*near, *far, *weights)
     grads, mod_t = main[0], main[1]
 
     near_hidden, far_hidden = call(
@@ -399,8 +435,31 @@
         moved=8 << 20,
     )(grads, *weights)
 
+    back = call(
+        meet_kernel, "meet", [shape((clips, chunk, width))] * groups, [VMEM] * 2, moved=2 << 20
+    )(near_hidden, over_y(far_hidden))
+    back = [back[0]] + [over_z(back[k], k) for k in range(1, groups)]
+
+    grad_input, sums = call(
+        functools.partial(input_kernel, groups),
+        "grad_input",
+        [shape((clips, positions, width)), shape((clips, 2, width), F32)],
+        [VMEM] * (2 + groups),
+        moved=2 << 20,
+    )(hidden, modulation, *back)
+    sums = [sums]
+    step = 1
+    while step < spaces:
+        sums.append(sums[-1] + over_space(sums[-1], step))
+        step *= 2
+    sums.append(sums[-1] + over_y(sums[-1]))
+    step = 1
+    while step < groups:
+        sums.append(sums[-1] + over_z(sums[-1], step))
+        step *= 2
+
     if pieces:
-        got = over_space(main[2], 1)
+        got = after(over_space(main[2], 1), far_hidden)
 
         def own(step, kind):
             return call(
@@ -414,18 +473,16 @@
 
         crossed = [over_space(own(j, BF16), 2 * j) for j in range(1, lines)]
         mine = own(0, F32)
+        crossed = [after(x, sums[0]) for x in crossed]
         spread = call(
             spread_kernel,
             "spread",
-            [shape((rows, wide), F32)] + [shape((rows, wide))] * (groups - 1),
+            [shape((rows, wide), BF16 if k % 2 else F32) for k in range(groups)],
             [VMEM] * lines,
             moved=4 << 20,
         )(mine, *crossed)
-        summed = call(add_kernel, "sum_z", shape((rows, wide)), [VMEM] * groups)(
-            spread[0], *[over_z(spread[k], k) for k in range(1, groups)]
-        )
-        halves = [summed] + [over_z(summed, k) for k in range(1, groups)]
-        others = [over_y(x) for x in halves]
+        summed = reduce_z(spread, over_z, [sums[2], sums[4]])
+        halves, others = gather_z(summed, groups, over_z, over_y)
         grad_weight = call(
             functools.partial(weight_kernel, groups, grad_scale_factor),
             "grad_w",
@@ -445,27 +502,7 @@
         grad_weight = jnp.concatenate([low, high], axis=2).reshape(share, 2 * wide)
         grad_weight = grad_weight.astype(F32) * grad_scale_factor
 
-    back = call(
-        meet_kernel, "meet", [shape((clips, chunk, width))] * groups, [VMEM] * 2, moved=2 << 20
-    )(near_hidden, over_y(far_hidden))
-    back = [back[0]] + [over_z(back[k], k) for k in range(1, groups)]
-    grad_input, sums = call(
-        functools.partial(input_kernel, groups),
-        "grad_input",
-        [shape((clips, positions, width)), shape((clips, 2, width), F32)],
-        [VMEM] * (2 + groups),
-        moved=2 << 20,
-    )(hidden, modulation, *back)
-    step = 1
-    while step < spaces:
-        sums += over_space(sums, step)
-        step *= 2
-    sums += over_y(sums)
-    step = 1
-    while step < groups:
-        sums += over_z(sums, step)
-        step *= 2
-    return (grad_input.reshape(hidden_in.shape), grad_weight, sums * grad_scale_factor)
+    return (grad_input.reshape(hidden_in.shape), grad_weight, sums[-1] * grad_scale_factor)
 
 
 def solution(mesh):

time: 224 us -> 164 us (0.73)
  waiting for transfers between devices: 134 us -> 94.8 us
  starting transfers between devices: 60 us -> 38.8 us
    ppermute x7, waiting for transfers between devices: 47 us -> 3.88 us  [over_space(): return lax.ppermute(x, 'space', [(i, i ^ step) for i in range(spaces)])]
    ppermute x17 -> x14, starting transfers between devices: 41 us -> 20.2 us  [over_z(): return lax.ppermute(x, 'frame', [(i, i ^ 2 * step) for i in range(frames)])]
    ppermute x10, waiting for transfers between devices: 32 us -> 41.8 us  [over_y(): return lax.ppermute(x, 'frame', [(i, i ^ 1) for i in range(frames)])]
    ppermute x17 -> x14, waiting for transfers between devices: 55.1 us -> 49.1 us  [over_z(): return lax.ppermute(x, 'frame', [(i, i ^ 2 * step) for i in range(frames)])]
  transfers between devices with their start and end apart: 34 -> 31, of which waited for: 20 -> 17; matrix products, arithmetic and copies ran while one was open for 0% -> 0% of each run, Pallas kernels for 4% -> 6%
where the time goes in v2:
time: 164 us
  waiting for transfers between devices  94.8 us (58%)
  starting transfers between devices  38.8 us (24%)
  Pallas kernels  24.9 us (15%)
  local copies, waits for them, and re-layouts  3.87 us (2%)
    ppermute x14, waiting for transfers between devices, over_z(): return lax.ppermute(x, 'frame', [(i, i ^ 2 * step) for i in range(frames)])  49.1 us
    ppermute x10, waiting for transfers between devices, over_y(): return lax.ppermute(x, 'frame', [(i, i ^ 1) for i in range(frames)])  41.8 us
    ppermute x14, starting transfers between devices, over_z(): return lax.ppermute(x, 'frame', [(i, i ^ 2 * step) for i in range(frames)])  20.2 us
    ppermute x10, starting transfers between devices, over_y(): return lax.ppermute(x, 'frame', [(i, i ^ 1) for i in range(frames)])  13.4 us
    pallas_call x1, Pallas kernels, per_device(): call(functools.partial(main_kernel, groups, shares, lines if pieces else...  11.2 us
    ppermute x7, starting transfers between devices, over_space(): return lax.ppermute(x, 'space', [(i, i ^ step) for i in range(spaces)])  5.23 us
    pallas_call x1, Pallas kernels, per_device(): call(functools.partial(hidden_kernel, groups, shares), 'grad_hidden', [sh...  4.3 us
    ppermute x7, waiting for transfers between devices, over_space(): return lax.ppermute(x, 'space', [(i, i ^ step) for i in range(spaces)])  3.88 us
  transfers between devices with their start and end apart: 31, of which 17 were waited for; matrix products, arithmetic and copies ran while one was open for 0% of the time, Pallas kernels for 6%

profile of v2, /device:TPU:0, one launch (start us, length us, event | category | flops | bytes accessed | tf_op | source)
XLA Modules:
  0.0 163.8 jit_solution(17144894797063278810)
XLA Ops:
  2.4 3.0 %collective-permute-start.8 = (bf16[288,1728]{1,0:T(8,128)(2,1)S(1)}, bf16[288,1728]{1,0:T(8,128)(2,1)S(1)}, u32[]{:S(2)}, u32[]{:S(2)}) collective-permute-start(bf16[288,1728]{1,0:T(8,128)(2,1)S(1)} %w_half.1.refs_8_.refs_0_), channel_id=1, source_target_pairs={{0,2},{1,3},{2,0},{3,1},{4,6},{5,7},{6,4},{7,5},{8,10},{9,11},{10,... | collective-permute-start | bytes 2985992 | tf_op jit(solution)/shard_map/ppermute | solution.py:366
  5.4 2.3 %copy-done = bf16[1000,2,1152]{2,1,0:T(2,128)(2,1)S(1)} copy-done((bf16[1000,2,1152]{2,1,0:T(2,128)(2,1)S(1)}, bf16[1000,2,1152]{2,1,0:T(2,128)(2,1)}, u32[]{:S(2)}) %copy-start) | copy-done | bytes 4608024
  7.7 2.7 %prep.1 = (bf16[2,32,2304]{2,1,0:T(8,128)(2,1)S(1)}, bf16[2,32,2304]{2,1,0:T(8,128)(2,1)S(1)}, bf16[2,32,2304]{2,1,0:T(8,128)(2,1)S(1)}, bf16[2,32,2304]{2,1,0:T(8,128)(2,1)S(1)}, f32[2,2,1152]{2,1,0:T(2,128)S(1)}) custom-call(bf16[2,128,1152]{2,1,0:T(8,128)(2,1)S(1)} %bitcast.5, bf16[2,128,1152]{2,1,0:T(8,128)(2,1)S(1)} %bitcast.7, ...), custom_call_target="tpu_custom_call" | custom-call | bytes 3145728 | tf_op jit(solution)/shard_map/prep/pallas_call | solution.py:381
  10.4 1.6 %collective-permute-start.1 = (bf16[2,32,2304]{2,1,0:T(8,128)(2,1)S(1)}, bf16[2,32,2304]{2,1,0:T(8,128)(2,1)S(1)}, u32[]{:S(2)}, u32[]{:S(2)}) collective-permute-start(bf16[2,32,2304]{2,1,0:T(8,128)(2,1)S(1)} %get-tuple-element.35), channel_id=1, source_target_pairs={{0,8},{4,12},{8,0},{12,4},{16,24},{20,28},{24,16},{28,20},{1,9},{5... | collective-permute-start | bytes 884744 | tf_op jit(solution)/shard_map/ppermute | solution.py:372
  12.1 2.6 %collective-permute-start.2 = (bf16[2,32,2304]{2,1,0:T(8,128)(2,1)S(1)}, bf16[2,32,2304]{2,1,0:T(8,128)(2,1)S(1)}, u32[]{:S(2)}, u32[]{:S(2)}) collective-permute-start(bf16[2,32,2304]{2,1,0:T(8,128)(2,1)S(1)} %get-tuple-element.36), channel_id=1, source_target_pairs={{0,16},{4,20},{8,24},{12,28},{16,0},{20,4},{24,8},{28,12},{1,17},{... | collective-permute-start | bytes 884744 | tf_op jit(solution)/shard_map/ppermute | solution.py:372
  16.5 7.9 %collective-permute-done.1.refs_1_ = bf16[2,32,2304]{2,1,0:T(8,128)(2,1)S(1)} collective-permute-done((bf16[2,32,2304]{2,1,0:T(8,128)(2,1)S(1)}, bf16[2,32,2304]{2,1,0:T(8,128)(2,1)S(1)}, u32[]{:S(2)}, u32[]{:S(2)}) %collective-permute-start.1) | collective-permute-done | bytes 294944 | tf_op jit(solution)/shard_map/ppermute | solution.py:372
  24.4 11.2 %collective-permute-done.2.refs_2_ = bf16[2,32,2304]{2,1,0:T(8,128)(2,1)S(1)} collective-permute-done((bf16[2,32,2304]{2,1,0:T(8,128)(2,1)S(1)}, bf16[2,32,2304]{2,1,0:T(8,128)(2,1)S(1)}, u32[]{:S(2)}, u32[]{:S(2)}) %collective-permute-start.2) | collective-permute-done | bytes 294944 | tf_op jit(solution)/shard_map/ppermute | solution.py:372
  35.6 1.6 collective-permute-start.4
  37.6 4.7 %collective-permute-done.4.refs_5_ = bf16[2,32,2304]{2,1,0:T(8,128)(2,1)S(1)} collective-permute-done((bf16[2,32,2304]{2,1,0:T(8,128)(2,1)S(1)}, bf16[2,32,2304]{2,1,0:T(8,128)(2,1)S(1)}, u32[]{:S(2)}, u32[]{:S(2)}) %collective-permute-start.4) | collective-permute-done | bytes 294944 | tf_op jit(solution)/shard_map/ppermute | solution.py:369
  42.3 3.2 %collective-permute-done.5.refs_6_ = bf16[2,32,2304]{2,1,0:T(8,128)(2,1)S(1)} collective-permute-done((bf16[2,32,2304]{2,1,0:T(8,128)(2,1)S(1)}, bf16[2,32,2304]{2,1,0:T(8,128)(2,1)S(1)}, u32[]{:S(2)}, u32[]{:S(2)}) %collective-permute-start.5) | collective-permute-done | bytes 294944 | tf_op jit(solution)/shard_map/ppermute | solution.py:369
  45.5 1.6 collective-permute-start.6
  47.1 7.8 %collective-permute-done.6.refs_7_ = bf16[2,32,2304]{2,1,0:T(8,128)(2,1)S(1)} collective-permute-done((bf16[2,32,2304]{2,1,0:T(8,128)(2,1)S(1)}, bf16[2,32,2304]{2,1,0:T(8,128)(2,1)S(1)}, u32[]{:S(2)}, u32[]{:S(2)}) %collective-permute-start.6) | collective-permute-done | bytes 294944 | tf_op jit(solution)/shard_map/ppermute | solution.py:369
  54.9 11.2 %attend.1 = (bf16[512,1728]{1,0:T(8,128)(2,1)S(1)}, bf16[1152,512]{1,0:T(8,128)(2,1)S(1)}, bf16[2,4,72,1728]{3,2,1,0:T(8,128)(2,1)S(1)}) custom-call(bf16[2,32,2304]{2,1,0:T(8,128)(2,1)S(1)} %get-tuple-element.34.refs_0_, bf16[2,32,2304]{2,1,0:T(8,128)(2,1)S(1)} %collective-permute-done.1.refs_1_, bf16[2,32,2304]{2,1,0:T(8,128)(2,1)S(1)} %collective-permute-done.2.refs_2_, ...), custom_call_target="tpu_custom_call" | custom-call | flops 6115295232 | bytes 20971520 | tf_op jit(solution)/shard_map/attend/pallas_call | solution.py:406
  66.2 4.3 %grad_hidden.1 = (bf16[4,2,32,1152]{3,2,1,0:T(8,128)(2,1)S(1)}, bf16[4,2,32,1152]{3,2,1,0:T(8,128)(2,1)S(1)}) custom-call(bf16[512,1728]{1,0:T(8,128)(2,1)S(1)} %get-tuple-element.41.grads, bf16[288,1728]{1,0:T(8,128)(2,1)S(1)} %w_half.1.refs_8_.refs_0_, bf16[288,1728]{1,0:T(8,128)(2,1)S(1)} %collective-permute-done.7.refs_9_.refs_1_, ...), custom_call_target="tpu_custom_call" | custom-call | flops 2038431744 | bytes 8388608 | tf_op jit(solution)/shard_map/grad_hidden/pallas_call | solution.py:428
  73.8 13.9 %collective-permute-done.10.got = bf16[4,2,32,1152]{3,2,1,0:T(8,128)(2,1)S(1)} collective-permute-done((bf16[4,2,32,1152]{3,2,1,0:T(8,128)(2,1)S(1)}, bf16[4,2,32,1152]{3,2,1,0:T(8,128)(2,1)S(1)}, u32[]{:S(2)}, u32[]{:S(2)}) %collective-permute-start.10) | collective-permute-done | bytes 589856 | tf_op jit(solution)/shard_map/ppermute | solution.py:369
  87.9 3.0 %collective-permute-start.12 = (bf16[2,32,1152]{2,1,0:T(8,128)(2,1)S(1)}, bf16[2,32,1152]{2,1,0:T(8,128)(2,1)S(1)}, u32[]{:S(2)}, u32[]{:S(2)}) collective-permute-start(bf16[2,32,1152]{2,1,0:T(8,128)(2,1)S(1)} %get-tuple-element.46), channel_id=1, source_target_pairs={{0,16},{4,20},{8,24},{12,28},{16,0},{20,4},{24,8},{28,12},{1,17},{... | collective-permute-start | bytes 442376 | tf_op jit(solution)/shard_map/ppermute | solution.py:372
  92.3 3.0 %collective-permute-done.11.refs_1_ = bf16[2,32,1152]{2,1,0:T(8,128)(2,1)S(1)} collective-permute-done((bf16[2,32,1152]{2,1,0:T(8,128)(2,1)S(1)}, bf16[2,32,1152]{2,1,0:T(8,128)(2,1)S(1)}, u32[]{:S(2)}, u32[]{:S(2)}) %collective-permute-start.11) | collective-permute-done | bytes 147488 | tf_op jit(solution)/shard_map/ppermute | solution.py:372
  95.3 6.7 %collective-permute-done.12.refs_2_ = bf16[2,32,1152]{2,1,0:T(8,128)(2,1)S(1)} collective-permute-done((bf16[2,32,1152]{2,1,0:T(8,128)(2,1)S(1)}, bf16[2,32,1152]{2,1,0:T(8,128)(2,1)S(1)}, u32[]{:S(2)}, u32[]{:S(2)}) %collective-permute-start.12) | collective-permute-done | bytes 147488 | tf_op jit(solution)/shard_map/ppermute | solution.py:372
  102.0 1.8 %grad_input.1 = (bf16[2,128,1152]{2,1,0:T(8,128)(2,1)}, f32[2,2,1152]{2,1,0:T(2,128)S(1)}) custom-call(bf16[2,128,1152]{2,1,0:T(8,128)(2,1)S(1)} %bitcast.6, f32[2,2,1152]{2,1,0:T(2,128)S(1)} %get-tuple-element.33.mod_ref, bf16[2,32,1152]{2,1,0:T(8,128)(2,1)S(1)} %get-tuple-element.44.refs_0_, bf16[2,32,1152]{2,1,0:T(8,128)(2,1)S(1)} %collective-permute-done.11.refs_1_, ...), custom_call_target="tpu_custom_call" | custom-call | bytes 2097152 | tf_op jit(solution)/shard_map/grad_input/pallas_call | solution.py:443
  104.7 2.2 %collective-permute-start.17 = (bf16[72,1728]{1,0:T(8,128)(2,1)S(1)}, bf16[72,1728]{1,0:T(8,128)(2,1)S(1)}, u32[]{:S(2)}, u32[]{:S(2)}) collective-permute-start(bf16[72,1728]{1,0:T(8,128)(2,1)S(1)} %get-tuple-element.57), channel_id=1, source_target_pairs={{0,8},{4,12},{8,0},{12,4},{16,24},{20,28},{24,16},{28,20},{1,9},{5... | collective-permute-start | bytes 746504 | tf_op jit(solution)/shard_map/ppermute | solution.py:372
  109.3 2.7 %collective-permute-done.19 = f32[2,2,1152]{2,1,0:T(2,128)S(1)} collective-permute-done((f32[2,2,1152]{2,1,0:T(2,128)S(1)}, f32[2,2,1152]{2,1,0:T(2,128)S(1)}, u32[]{:S(2)}, u32[]{:S(2)}) %collective-permute-start.19) | collective-permute-done | bytes 18464 | tf_op jit(solution)/shard_map/ppermute | solution.py:366
  112.1 2.8 %collective-permute-start.20 = (bf16[72,1728]{1,0:T(8,128)(2,1)S(1)}, bf16[72,1728]{1,0:T(8,128)(2,1)S(1)}, u32[]{:S(2)}, u32[]{:S(2)}) collective-permute-start(bf16[72,1728]{1,0:T(8,128)(2,1)S(1)} %sum_z.2), channel_id=1, source_target_pairs={{0,16},{4,20},{8,24},{12,28},{16,0},{20,4},{24,8},{28,12},{1,17},{... | collective-permute-start | bytes 746504 | tf_op jit(solution)/shard_map/ppermute | solution.py:372
  116.7 2.2 %collective-permute-done.21 = f32[2,2,1152]{2,1,0:T(2,128)S(1)} collective-permute-done((f32[2,2,1152]{2,1,0:T(2,128)S(1)}, f32[2,2,1152]{2,1,0:T(2,128)S(1)}, u32[]{:S(2)}, u32[]{:S(2)}) %collective-permute-start.21) | collective-permute-done | bytes 18464 | tf_op jit(solution)/shard_map/ppermute | solution.py:369
  119.0 1.8 %collective-permute-start.22 = (f32[2,2,1152]{2,1,0:T(2,128)S(1)}, f32[2,2,1152]{2,1,0:T(2,128)S(1)}, u32[]{:S(2)}, u32[]{:S(2)}) collective-permute-start(f32[2,2,1152]{2,1,0:T(2,128)S(1)} %add.17), channel_id=1, source_target_pairs={{0,8},{4,12},{8,0},{12,4},{16,24},{20,28},{24,16},{28,20},{1,9},{5... | collective-permute-start | bytes 55304 | tf_op jit(solution)/shard_map/ppermute | solution.py:372
  120.8 5.9 %collective-permute-done.22 = f32[2,2,1152]{2,1,0:T(2,128)S(1)} collective-permute-done((f32[2,2,1152]{2,1,0:T(2,128)S(1)}, f32[2,2,1152]{2,1,0:T(2,128)S(1)}, u32[]{:S(2)}, u32[]{:S(2)}) %collective-permute-start.22) | collective-permute-done | bytes 18464 | tf_op jit(solution)/shard_map/ppermute | solution.py:372
  128.5 1.9 %collective-permute-start.23 = (bf16[72,1728]{1,0:T(8,128)(2,1)S(1)}, bf16[72,1728]{1,0:T(8,128)(2,1)S(1)}, u32[]{:S(2)}, u32[]{:S(2)}) collective-permute-start(bf16[72,1728]{1,0:T(8,128)(2,1)S(1)} %sum_z.3.refs_0_), channel_id=1, source_target_pairs={{0,8},{4,12},{8,0},{12,4},{16,24},{20,28},{24,16},{28,20},{1,9},{5... | collective-permute-start | bytes 746504 | tf_op jit(solution)/shard_map/ppermute | solution.py:372
  130.4 10.0 %collective-permute-done.25.refs_2_ = bf16[72,1728]{1,0:T(8,128)(2,1)S(1)} collective-permute-done((bf16[72,1728]{1,0:T(8,128)(2,1)S(1)}, bf16[72,1728]{1,0:T(8,128)(2,1)S(1)}, u32[]{:S(2)}, u32[]{:S(2)}) %collective-permute-start.25) | collective-permute-done | bytes 248864 | tf_op jit(solution)/shard_map/ppermute | solution.py:372
  140.4 2.1 %collective-permute-start.30 = (f32[2,2,1152]{2,1,0:T(2,128)S(1)}, f32[2,2,1152]{2,1,0:T(2,128)S(1)}, u32[]{:S(2)}, u32[]{:S(2)}) collective-permute-start(f32[2,2,1152]{2,1,0:T(2,128)S(1)} %add.18), channel_id=1, source_target_pairs={{0,16},{4,20},{8,24},{12,28},{16,0},{20,4},{24,8},{28,12},{1,17},{... | collective-permute-start | bytes 55304 | tf_op jit(solution)/shard_map/ppermute | solution.py:372
  144.5 4.4 %collective-permute-done.26.refs_3_ = bf16[72,1728]{1,0:T(8,128)(2,1)S(1)} collective-permute-done((bf16[72,1728]{1,0:T(8,128)(2,1)S(1)}, bf16[72,1728]{1,0:T(8,128)(2,1)S(1)}, u32[]{:S(2)}, u32[]{:S(2)}) %collective-permute-start.26) | collective-permute-done | bytes 248864 | tf_op jit(solution)/shard_map/ppermute | solution.py:372
  151.6 5.5 %collective-permute-done.27.refs_5_ = bf16[72,1728]{1,0:T(8,128)(2,1)S(1)} collective-permute-done((bf16[72,1728]{1,0:T(8,128)(2,1)S(1)}, bf16[72,1728]{1,0:T(8,128)(2,1)S(1)}, u32[]{:S(2)}, u32[]{:S(2)}) %collective-permute-start.27) | collective-permute-done | bytes 248864 | tf_op jit(solution)/shard_map/ppermute | solution.py:369
  157.1 3.9 %collective-permute-done.29.refs_7_ = bf16[72,1728]{1,0:T(8,128)(2,1)S(1)} collective-permute-done((bf16[72,1728]{1,0:T(8,128)(2,1)S(1)}, bf16[72,1728]{1,0:T(8,128)(2,1)S(1)}, u32[]{:S(2)}, u32[]{:S(2)}) %collective-permute-start.29) | collective-permute-done | bytes 248864 | tf_op jit(solution)/shard_map/ppermute | solution.py:369
  161.0 2.8 %grad_w.1 = f32[288,3456]{1,0:T(8,128)} custom-call(bf16[72,1728]{1,0:T(8,128)(2,1)S(1)} %sum_z.3.refs_0_, bf16[72,1728]{1,0:T(8,128)(2,1)S(1)} %collective-permute-done.23.refs_1_, bf16[72,1728]{1,0:T(8,128)(2,1)S(1)} %collective-permute-done.25.refs_2_, bf16[72,1728]{1,0:T(8,128)(2,1)S(1)} %collective-permute-done.26.refs_3_, ...), custom_call_target="tpu_custom_call" | custom-call | bytes 8388608 | tf_op jit(solution)/shard_map/grad_w/pallas_call | solution.py:486
  (61 shorter events, 20.6 us)
Async XLA Ops:
  2.2 3.2 %copy-start.6 = (s32[2]{0:T(128)S(1)}, s32[2]{0:T(128)}, u32[]{:S(2)}) copy-start(s32[2]{0:T(128)} %wi_ref.1) | copy-start | bytes 28
  2.4 43.0 %collective-permute-start.8 = (bf16[288,1728]{1,0:T(8,128)(2,1)S(1)}, bf16[288,1728]{1,0:T(8,128)(2,1)S(1)}, u32[]{:S(2)}, u32[]{:S(2)}) collective-permute-start(bf16[288,1728]{1,0:T(8,128)(2,1)S(1)} %w_half.1.refs_8_.refs_0_), channel_id=1, source_target_pairs={{0,2},{1,3},{2,0},{3,1},{4,6},{5,7},{6,4},{7,5},{8,10},{9,11},{10,... | collective-permute-start | bytes 2985992 | tf_op jit(solution)/shard_map/ppermute | solution.py:366
  10.4 13.9 %collective-permute-start.1 = (bf16[2,32,2304]{2,1,0:T(8,128)(2,1)S(1)}, bf16[2,32,2304]{2,1,0:T(8,128)(2,1)S(1)}, u32[]{:S(2)}, u32[]{:S(2)}) collective-permute-start(bf16[2,32,2304]{2,1,0:T(8,128)(2,1)S(1)} %get-tuple-element.35), channel_id=1, source_target_pairs={{0,8},{4,12},{8,0},{12,4},{16,24},{20,28},{24,16},{28,20},{1,9},{5... | collective-permute-start | bytes 884744 | tf_op jit(solution)/shard_map/ppermute | solution.py:372
  12.1 23.5 %collective-permute-start.2 = (bf16[2,32,2304]{2,1,0:T(8,128)(2,1)S(1)}, bf16[2,32,2304]{2,1,0:T(8,128)(2,1)S(1)}, u32[]{:S(2)}, u32[]{:S(2)}) collective-permute-start(bf16[2,32,2304]{2,1,0:T(8,128)(2,1)S(1)} %get-tuple-element.36), channel_id=1, source_target_pairs={{0,16},{4,20},{8,24},{12,28},{16,0},{20,4},{24,8},{28,12},{1,17},{... | collective-permute-start | bytes 884744 | tf_op jit(solution)/shard_map/ppermute | solution.py:372
  14.7 20.9 %collective-permute-start = (bf16[2,32,2304]{2,1,0:T(8,128)(2,1)S(1)}, bf16[2,32,2304]{2,1,0:T(8,128)(2,1)S(1)}, u32[]{:S(2)}, u32[]{:S(2)}) collective-permute-start(bf16[2,32,2304]{2,1,0:T(8,128)(2,1)S(1)} %get-tuple-element.34.refs_0_), channel_id=1, source_target_pairs={{0,4},{4,0},{8,12},{12,8},{16,20},{20,16},{24,28},{28,24},{1,5},{5... | collective-permute-start | bytes 884744 | tf_op jit(solution)/shard_map/ppermute | solution.py:369
  16.3 21.3 %collective-permute-start.3 = (bf16[2,32,2304]{2,1,0:T(8,128)(2,1)S(1)}, bf16[2,32,2304]{2,1,0:T(8,128)(2,1)S(1)}, u32[]{:S(2)}, u32[]{:S(2)}) collective-permute-start(bf16[2,32,2304]{2,1,0:T(8,128)(2,1)S(1)} %get-tuple-element.39), channel_id=1, source_target_pairs={{0,24},{4,28},{8,16},{12,20},{16,8},{20,12},{24,0},{28,4},{1,25},{... | collective-permute-start | bytes 884744 | tf_op jit(solution)/shard_map/ppermute | solution.py:372
  35.6 6.7 %collective-permute-start.4 = (bf16[2,32,2304]{2,1,0:T(8,128)(2,1)S(1)}, bf16[2,32,2304]{2,1,0:T(8,128)(2,1)S(1)}, u32[]{:S(2)}, u32[]{:S(2)}) collective-permute-start(bf16[2,32,2304]{2,1,0:T(8,128)(2,1)S(1)} %collective-permute-done.1.refs_1_), channel_id=1, source_target_pairs={{0,4},{4,0},{8,12},{12,8},{16,20},{20,16},{24,28},{28,24},{1,5},{5... | collective-permute-start | bytes 884744 | tf_op jit(solution)/shard_map/ppermute | solution.py:369
  37.2 8.3 %collective-permute-start.5 = (bf16[2,32,2304]{2,1,0:T(8,128)(2,1)S(1)}, bf16[2,32,2304]{2,1,0:T(8,128)(2,1)S(1)}, u32[]{:S(2)}, u32[]{:S(2)}) collective-permute-start(bf16[2,32,2304]{2,1,0:T(8,128)(2,1)S(1)} %collective-permute-done.2.refs_2_), channel_id=1, source_target_pairs={{0,4},{4,0},{8,12},{12,8},{16,20},{20,16},{24,28},{28,24},{1,5},{5... | collective-permute-start | bytes 884744 | tf_op jit(solution)/shard_map/ppermute | solution.py:369
  37.6 17.3 %collective-permute-start.7 = (bf16[288,1728]{1,0:T(8,128)(2,1)S(1)}, bf16[288,1728]{1,0:T(8,128)(2,1)S(1)}, u32[]{:S(2)}, u32[]{:S(2)}) collective-permute-start(bf16[288,1728]{1,0:T(8,128)(2,1)S(1)} %w_half.1.refs_8_.refs_0_), channel_id=1, source_target_pairs={{0,1},{1,0},{2,3},{3,2},{4,5},{5,4},{6,7},{7,6},{8,9},{9,8},{10,11... | collective-permute-start | bytes 2985992 | tf_op jit(solution)/shard_map/ppermute | solution.py:366
  45.4 9.4 %collective-permute-start.9 = (bf16[288,1728]{1,0:T(8,128)(2,1)S(1)}, bf16[288,1728]{1,0:T(8,128)(2,1)S(1)}, u32[]{:S(2)}, u32[]{:S(2)}) collective-permute-start(bf16[288,1728]{1,0:T(8,128)(2,1)S(1)} %collective-permute-done.8.refs_10_.refs_2_), channel_id=1, source_target_pairs={{0,1},{1,0},{2,3},{3,2},{4,5},{5,4},{6,7},{7,6},{8,9},{9,8},{10,11... | collective-permute-start | bytes 2985992 | tf_op jit(solution)/shard_map/ppermute | solution.py:366
  45.5 9.4 %collective-permute-start.6 = (bf16[2,32,2304]{2,1,0:T(8,128)(2,1)S(1)}, bf16[2,32,2304]{2,1,0:T(8,128)(2,1)S(1)}, u32[]{:S(2)}, u32[]{:S(2)}) collective-permute-start(bf16[2,32,2304]{2,1,0:T(8,128)(2,1)S(1)} %collective-permute-done.3.refs_3_), channel_id=1, source_target_pairs={{0,4},{4,0},{8,12},{12,8},{16,20},{20,16},{24,28},{28,24},{1,5},{5... | collective-permute-start | bytes 884744 | tf_op jit(solution)/shard_map/ppermute | solution.py:369
  66.1 4.4 %collective-permute-start.14 = (bf16[2,4,72,1728]{3,2,1,0:T(8,128)(2,1)S(1)}, bf16[2,4,72,1728]{3,2,1,0:T(8,128)(2,1)S(1)}, u32[]{:S(2)}, u32[]{:S(2)}) collective-permute-start(bf16[2,4,72,1728]{3,2,1,0:T(8,128)(2,1)S(1)} %get-tuple-element.50), channel_id=1, source_target_pairs={{0,1},{1,0},{2,3},{3,2},{4,5},{5,4},{6,7},{7,6},{8,9},{9,8},{10,11... | collective-permute-start | bytes 5971976 | tf_op jit(solution)/shard_map/ppermute | solution.py:366
  71.2 33.3 %collective-permute-start.15 = (bf16[4,72,1728]{2,1,0:T(8,128)(2,1)S(1)}, bf16[4,72,1728]{2,1,0:T(8,128)(2,1)S(1)}, u32[]{:S(2)}, u32[]{:S(2)}) collective-permute-start(bf16[4,72,1728]{2,1,0:T(8,128)(2,1)S(1)} %grad_w_rows.3), channel_id=1, source_target_pairs={{0,2},{1,3},{2,0},{3,1},{4,6},{5,7},{6,4},{7,5},{8,10},{9,11},{10,... | collective-permute-start | bytes 2985992 | tf_op jit(solution)/shard_map/ppermute | solution.py:366
  72.2 15.4 %collective-permute-start.10 = (bf16[4,2,32,1152]{3,2,1,0:T(8,128)(2,1)S(1)}, bf16[4,2,32,1152]{3,2,1,0:T(8,128)(2,1)S(1)}, u32[]{:S(2)}, u32[]{:S(2)}) collective-permute-start(bf16[4,2,32,1152]{3,2,1,0:T(8,128)(2,1)S(1)} %get-tuple-element.43), channel_id=1, source_target_pairs={{0,4},{4,0},{8,12},{12,8},{16,20},{20,16},{24,28},{28,24},{1,5},{5... | collective-permute-start | bytes 1769480 | tf_op jit(solution)/shard_map/ppermute | solution.py:369
  87.8 7.5 %collective-permute-start.11 = (bf16[2,32,1152]{2,1,0:T(8,128)(2,1)S(1)}, bf16[2,32,1152]{2,1,0:T(8,128)(2,1)S(1)}, u32[]{:S(2)}, u32[]{:S(2)}) collective-permute-start(bf16[2,32,1152]{2,1,0:T(8,128)(2,1)S(1)} %get-tuple-element.45), channel_id=1, source_target_pairs={{0,8},{4,12},{8,0},{12,4},{16,24},{20,28},{24,16},{28,20},{1,9},{5... | collective-permute-start | bytes 442376 | tf_op jit(solution)/shard_map/ppermute | solution.py:372
  87.9 14.1 %collective-permute-start.12 = (bf16[2,32,1152]{2,1,0:T(8,128)(2,1)S(1)}, bf16[2,32,1152]{2,1,0:T(8,128)(2,1)S(1)}, u32[]{:S(2)}, u32[]{:S(2)}) collective-permute-start(bf16[2,32,1152]{2,1,0:T(8,128)(2,1)S(1)} %get-tuple-element.46), channel_id=1, source_target_pairs={{0,16},{4,20},{8,24},{12,28},{16,0},{20,4},{24,8},{28,12},{1,17},{... | collective-permute-start | bytes 442376 | tf_op jit(solution)/shard_map/ppermute | solution.py:372
  90.9 11.0 %collective-permute-start.13 = (bf16[2,32,1152]{2,1,0:T(8,128)(2,1)S(1)}, bf16[2,32,1152]{2,1,0:T(8,128)(2,1)S(1)}, u32[]{:S(2)}, u32[]{:S(2)}) collective-permute-start(bf16[2,32,1152]{2,1,0:T(8,128)(2,1)S(1)} %get-tuple-element.47), channel_id=1, source_target_pairs={{0,24},{4,28},{8,16},{12,20},{16,8},{20,12},{24,0},{28,4},{1,25},{... | collective-permute-start | bytes 442376 | tf_op jit(solution)/shard_map/ppermute | solution.py:372
  104.7 7.3 %collective-permute-start.17 = (bf16[72,1728]{1,0:T(8,128)(2,1)S(1)}, bf16[72,1728]{1,0:T(8,128)(2,1)S(1)}, u32[]{:S(2)}, u32[]{:S(2)}) collective-permute-start(bf16[72,1728]{1,0:T(8,128)(2,1)S(1)} %get-tuple-element.57), channel_id=1, source_target_pairs={{0,8},{4,12},{8,0},{12,4},{16,24},{20,28},{24,16},{28,20},{1,9},{5... | collective-permute-start | bytes 746504 | tf_op jit(solution)/shard_map/ppermute | solution.py:372
  106.9 1.2 collective-permute-start.18
  108.2 3.8 %collective-permute-start.19 = (f32[2,2,1152]{2,1,0:T(2,128)S(1)}, f32[2,2,1152]{2,1,0:T(2,128)S(1)}, u32[]{:S(2)}, u32[]{:S(2)}) collective-permute-start(f32[2,2,1152]{2,1,0:T(2,128)S(1)} %add.15), channel_id=1, source_target_pairs={{0,2},{1,3},{2,0},{3,1},{4,6},{5,7},{6,4},{7,5},{8,10},{9,11},{10,... | collective-permute-start | bytes 55304 | tf_op jit(solution)/shard_map/ppermute | solution.py:366
  112.1 14.7 %collective-permute-start.20 = (bf16[72,1728]{1,0:T(8,128)(2,1)S(1)}, bf16[72,1728]{1,0:T(8,128)(2,1)S(1)}, u32[]{:S(2)}, u32[]{:S(2)}) collective-permute-start(bf16[72,1728]{1,0:T(8,128)(2,1)S(1)} %sum_z.2), channel_id=1, source_target_pairs={{0,16},{4,20},{8,24},{12,28},{16,0},{20,4},{24,8},{28,12},{1,17},{... | collective-permute-start | bytes 746504 | tf_op jit(solution)/shard_map/ppermute | solution.py:372
  114.9 11.8 %collective-permute-start.16 = (bf16[72,1728]{1,0:T(8,128)(2,1)S(1)}, bf16[72,1728]{1,0:T(8,128)(2,1)S(1)}, u32[]{:S(2)}, u32[]{:S(2)}) collective-permute-start(bf16[72,1728]{1,0:T(8,128)(2,1)S(1)} %get-tuple-element.55), channel_id=1, source_target_pairs={{0,8},{4,12},{8,0},{12,4},{16,24},{20,28},{24,16},{28,20},{1,9},{5... | collective-permute-start | bytes 746504 | tf_op jit(solution)/shard_map/ppermute | solution.py:372
  115.2 3.8 %collective-permute-start.21 = (f32[2,2,1152]{2,1,0:T(2,128)S(1)}, f32[2,2,1152]{2,1,0:T(2,128)S(1)}, u32[]{:S(2)}, u32[]{:S(2)}) collective-permute-start(f32[2,2,1152]{2,1,0:T(2,128)S(1)} %add.16), channel_id=1, source_target_pairs={{0,4},{4,0},{8,12},{12,8},{16,20},{20,16},{24,28},{28,24},{1,5},{5... | collective-permute-start | bytes 55304 | tf_op jit(solution)/shard_map/ppermute | solution.py:369
  119.0 7.8 %collective-permute-start.22 = (f32[2,2,1152]{2,1,0:T(2,128)S(1)}, f32[2,2,1152]{2,1,0:T(2,128)S(1)}, u32[]{:S(2)}, u32[]{:S(2)}) collective-permute-start(f32[2,2,1152]{2,1,0:T(2,128)S(1)} %add.17), channel_id=1, source_target_pairs={{0,8},{4,12},{8,0},{12,4},{16,24},{20,28},{24,16},{28,20},{1,9},{5... | collective-permute-start | bytes 55304 | tf_op jit(solution)/shard_map/ppermute | solution.py:372
  126.9 13.5 %collective-permute-start.25 = (bf16[72,1728]{1,0:T(8,128)(2,1)S(1)}, bf16[72,1728]{1,0:T(8,128)(2,1)S(1)}, u32[]{:S(2)}, u32[]{:S(2)}) collective-permute-start(bf16[72,1728]{1,0:T(8,128)(2,1)S(1)} %sum_z.3.refs_0_), channel_id=1, source_target_pairs={{0,16},{4,20},{8,24},{12,28},{16,0},{20,4},{24,8},{28,12},{1,17},{... | collective-permute-start | bytes 746504 | tf_op jit(solution)/shard_map/ppermute | solution.py:372
  127.0 13.4 %collective-permute-start.24 = (bf16[72,1728]{1,0:T(8,128)(2,1)S(1)}, bf16[72,1728]{1,0:T(8,128)(2,1)S(1)}, u32[]{:S(2)}, u32[]{:S(2)}) collective-permute-start(bf16[72,1728]{1,0:T(8,128)(2,1)S(1)} %sum_z.3.refs_0_), channel_id=1, source_target_pairs={{0,4},{4,0},{8,12},{12,8},{16,20},{20,16},{24,28},{28,24},{1,5},{5... | collective-permute-start | bytes 746504 | tf_op jit(solution)/shard_map/ppermute | solution.py:369
  128.5 15.4 %collective-permute-start.23 = (bf16[72,1728]{1,0:T(8,128)(2,1)S(1)}, bf16[72,1728]{1,0:T(8,128)(2,1)S(1)}, u32[]{:S(2)}, u32[]{:S(2)}) collective-permute-start(bf16[72,1728]{1,0:T(8,128)(2,1)S(1)} %sum_z.3.refs_0_), channel_id=1, source_target_pairs={{0,8},{4,12},{8,0},{12,4},{16,24},{20,28},{24,16},{28,20},{1,9},{5... | collective-permute-start | bytes 746504 | tf_op jit(solution)/shard_map/ppermute | solution.py:372
  140.4 8.5 %collective-permute-start.26 = (bf16[72,1728]{1,0:T(8,128)(2,1)S(1)}, bf16[72,1728]{1,0:T(8,128)(2,1)S(1)}, u32[]{:S(2)}, u32[]{:S(2)}) collective-permute-start(bf16[72,1728]{1,0:T(8,128)(2,1)S(1)} %collective-permute-done.25.refs_2_), channel_id=1, source_target_pairs={{0,8},{4,12},{8,0},{12,4},{16,24},{20,28},{24,16},{28,20},{1,9},{5... | collective-permute-start | bytes 746504 | tf_op jit(solution)/shard_map/ppermute | solution.py:372
  140.4 10.0 %collective-permute-start.30 = (f32[2,2,1152]{2,1,0:T(2,128)S(1)}, f32[2,2,1152]{2,1,0:T(2,128)S(1)}, u32[]{:S(2)}, u32[]{:S(2)}) collective-permute-start(f32[2,2,1152]{2,1,0:T(2,128)S(1)} %add.18), channel_id=1, source_target_pairs={{0,16},{4,20},{8,24},{12,28},{16,0},{20,4},{24,8},{28,12},{1,17},{... | collective-permute-start | bytes 55304 | tf_op jit(solution)/shard_map/ppermute | solution.py:372
  142.5 9.2 %collective-permute-start.28 = (bf16[72,1728]{1,0:T(8,128)(2,1)S(1)}, bf16[72,1728]{1,0:T(8,128)(2,1)S(1)}, u32[]{:S(2)}, u32[]{:S(2)}) collective-permute-start(bf16[72,1728]{1,0:T(8,128)(2,1)S(1)} %collective-permute-done.25.refs_2_), channel_id=1, source_target_pairs={{0,4},{4,0},{8,12},{12,8},{16,20},{20,16},{24,28},{28,24},{1,5},{5... | collective-permute-start | bytes 746504 | tf_op jit(solution)/shard_map/ppermute | solution.py:369
  144.0 13.2 %collective-permute-start.27 = (bf16[72,1728]{1,0:T(8,128)(2,1)S(1)}, bf16[72,1728]{1,0:T(8,128)(2,1)S(1)}, u32[]{:S(2)}, u32[]{:S(2)}) collective-permute-start(bf16[72,1728]{1,0:T(8,128)(2,1)S(1)} %collective-permute-done.23.refs_1_), channel_id=1, source_target_pairs={{0,4},{4,0},{8,12},{12,8},{16,20},{20,16},{24,28},{28,24},{1,5},{5... | collective-permute-start | bytes 746504 | tf_op jit(solution)/shard_map/ppermute | solution.py:369
  148.9 12.2 %collective-permute-start.29 = (bf16[72,1728]{1,0:T(8,128)(2,1)S(1)}, bf16[72,1728]{1,0:T(8,128)(2,1)S(1)}, u32[]{:S(2)}, u32[]{:S(2)}) collective-permute-start(bf16[72,1728]{1,0:T(8,128)(2,1)S(1)} %collective-permute-done.26.refs_3_), channel_id=1, source_target_pairs={{0,4},{4,0},{8,12},{12,8},{16,20},{20,16},{24,28},{28,24},{1,5},{5... | collective-permute-start | bytes 746504 | tf_op jit(solution)/shard_map/ppermute | solution.py:369
  (6 other events, 16.7 us)

commit v3 on v1

--- a/solution.py
+++ b/solution.py
@@ -16,14 +16,14 @@
 BF16 = jnp.bfloat16
 VMEM = pl.BlockSpec(memory_space=pltpu.VMEM)
 SMEM = pl.BlockSpec(memory_space=pltpu.SMEM)
-ANY = pl.BlockSpec(memory_space=pl.ANY)
+HBM = pl.BlockSpec(memory_space=pltpu.HBM)
 
 
 def cost(flops, moved):
     return pl.CostEstimate(flops=flops, bytes_accessed=moved, transcendentals=0)
 
 
-def call(kernel, name, out_shape, in_specs, scratch=(), flops=0, moved=1 << 20):
+def call(kernel, name, out_shape, in_specs, scratch=(), flops=0, moved=1 << 20, vmem=40):
     return pl.pallas_call(
         kernel,
         name=name,
@@ -32,7 +32,7 @@
         out_specs=jax.tree.map(lambda _: VMEM, out_shape),
         scratch_shapes=list(scratch),
         cost_estimate=cost(flops, moved),
-        compiler_params=pltpu.CompilerParams(vmem_limit_bytes=40 << 20),
+        compiler_params=pltpu.CompilerParams(vmem_limit_bytes=vmem << 20),
     )
 
 
@@ -50,6 +50,10 @@
 
 
 ROWS_ROWS = (((1,), (1,)), ((), ()))
+
+
+def after(x, *others):
+    return lax.optimization_barrier((x, *others))[0]
 
 
 def pick(cond, a, b):
@@ -82,25 +86,28 @@
     return centered * inverse_std, inverse_std
 
 
-def prep_kernel(groups, h_ref, c_ref, tab_ref, ts_ref, snr_ref, wi_ref, *rest):
-    send, keep = rest[:groups], rest[groups : 2 * groups]
-    mod_ref, scratch, sems = rest[2 * groups :]
-    z, y, _ = place()
-    clips, positions, width = h_ref.shape
-    chunk, half = positions // groups, width // 2
+def lookup_kernel(tab_ref, ts_ref, snr_ref, wi_ref, out_ref, scratch, sems):
+    clips = out_ref.shape[0]
     copies = [
         pltpu.make_async_copy(tab_ref.at[ts_ref[b]], scratch.at[b], sems.at[b])
         for b in range(clips)
     ]
     for copy in copies:
         copy.start()
-    for copy in copies:
+    for b in range(clips):
+        out_ref[b, 2:3, :] = jnp.full((1, out_ref.shape[2]), snr_ref[wi_ref[b]], F32)
+    for b, copy in enumerate(copies):
         copy.wait()
+        out_ref[b, 0:2, :] = scratch[b].astype(F32)
+
+
+def prep_kernel(groups, h_ref, c_ref, mod_ref, *outs):
+    send, keep = outs[:groups], outs[groups:]
+    z, y, _ = place()
+    clips, positions, width = h_ref.shape
+    chunk, half = positions // groups, width // 2
     for b in range(clips):
-        table = scratch[b].astype(F32)
-        mod_ref[b] = table
-        shift, scale = table[0:1], 1.0 + table[1:2]
-        weight = snr_ref[wi_ref[b]]
+        shift, scale, weight = mod_ref[b, 0:1, :], 1.0 + mod_ref[b, 1:2, :], mod_ref[b, 2:3, :]
         for k in range(groups):
             rows = pl.ds(pl.multiple_of((z ^ k) * chunk, chunk), chunk)
             normed, _ = layer_norm(h_ref[b, rows, :].astype(F32))
@@ -111,12 +118,12 @@
             keep[k][b] = pick(y == 0, low, high).astype(BF16)
 
 
-def main_kernel(groups, shares, others, *refs):
+def main_kernel(groups, shares, cuts, *refs):
     near, kept, far = refs[:groups], refs[groups : 2 * groups], refs[2 * groups : 3 * groups]
     weights = refs[3 * groups : 3 * groups + shares]
     rest = refs[3 * groups + shares :]
-    outs, scratches = rest[: 2 + (others > 0)], rest[2 + (others > 0) :]
-    grads, mod_t = outs[0], outs[1]
+    outs, scratches = rest[: 2 + len(cuts)], rest[2 + len(cuts) :]
+    grads, mod_t = outs[:2]
     w, mod, up, qw, kw, vw, dq, dk, dv, sems = scratches
     _, _, s = place()
     clips, chunk, _ = near[0].shape
@@ -198,30 +205,35 @@
         grads[rows, seam + LANES : 2 * half] = near_k[:, LANES:].astype(BF16)
         grads[rows, 2 * half :] = dv[:, :half].astype(BF16)
 
-    if others:
-        slices(outs[2], mod_t, grads, s ^ 1, share, others)
-
-
-def slices(out, mod_t, grads, first, share, count):
-    groups, rows = out.shape[1], out.shape[2]
-    for j in range(count):
-        start = pl.multiple_of((first ^ (2 * j)) * share, share)
-        total = dot(mod_t[pl.ds(start, share), :], grads[...])
-        for g in range(groups):
-            out[j, g] = total[g * rows : (g + 1) * rows].astype(out.dtype)
-
-
-def own_kernel(step, share, mod_t, grads, got, out):
+    for out, cut in zip(outs[2:], cuts):
+        for j in range(out.shape[0]):
+            start = pl.multiple_of((s ^ 1 ^ (2 * j)) * share, share)
+            total = dot(mod_t[pl.ds(start, share), :], grads[:, cut])
+            for g in range(groups):
+                out[j, g] = total[g * out.shape[2] : (g + 1) * out.shape[2]].astype(out.dtype)
+
+
+def unpack(out, total):
+    groups, clips, chunk, _ = out.shape
+    slabs = chunk // SLAB
+    for b in range(clips):
+        for i in range(slabs):
+            for k in range(groups):
+                start = ((b * slabs + i) * groups + k) * SLAB
+                out[k, b, i * SLAB : (i + 1) * SLAB, :] = total[start : start + SLAB].astype(out.dtype)
+
+
+def own_kernel(step, share, cut, mod_t, grads, got, out):
     _, _, s = place()
     groups, rows = out.shape[0], out.shape[1]
     start = pl.multiple_of((s ^ (2 * step)) * share, share)
-    total = dot(mod_t[pl.ds(start, share), :], grads[...])
+    total = dot(mod_t[pl.ds(start, share), :], grads[:, cut])
     for g in range(groups):
         out[g] = (total[g * rows : (g + 1) * rows] + got[step, g].astype(F32)).astype(out.dtype)
 
 
-def hidden_kernel(groups, shares, grads, *refs):
-    weights, (near, far, w, part, sems) = refs[:shares], refs[shares:]
+def hidden_kernel(shares, grads, *refs):
+    weights, (far, near, w, part, sems) = refs[:shares], refs[shares:]
     _, _, s = place()
     depth = w.shape[0]
     share = depth // shares
@@ -230,22 +242,16 @@
         rows = pl.ds(pl.multiple_of((s ^ k) * share, share), share) if shares > 1 else pl.ds(0, depth)
         copies.append(pltpu.make_async_copy(weights[k], w.at[rows], sems.at[k]))
         copies[-1].start()
-    _, clips, chunk, _ = near.shape
-    slabs = chunk // SLAB
-    block = 2 * groups * SLAB
-    side = block // 2
-    for copy in copies:
-        copy.wait()
+    groups, clips, chunk, _ = near.shape
+    side = groups * SLAB
     for which, out in ((1, far), (0, near)):
-        for n in range(clips * slabs):
-            start = n * block + which * side
+        for n in range(clips * (chunk // SLAB)):
+            start = (2 * n + which) * side
             part[n * side : (n + 1) * side, :] = grads[start : start + side, :]
-        total = dot(part[...], w[...], ROWS_ROWS)
-        for b in range(clips):
-            for i in range(slabs):
-                for k in range(groups):
-                    start = (b * slabs + i) * side + k * SLAB
-                    out[k, b, i * SLAB : (i + 1) * SLAB, :] = total[start : start + SLAB].astype(out.dtype)
+        if which:
+            for copy in copies:
+                copy.wait()
+        unpack(out, dot(part[...], w[...], ROWS_ROWS))
 
 
 def meet_kernel(near, got, *outs):
@@ -276,37 +282,79 @@
         sums_ref[b, 1:2, :] = scale_sum
 
 
-def spread_kernel(own, *refs):
-    groups = own.shape[0]
-    got, outs = refs[:-groups], refs[-groups:]
+def spread_kernel(own, got, keep, send):
     z, _, _ = place()
+    for k in range(own.shape[0]):
+        total = own[z ^ k] + got[z ^ k].astype(F32)
+        if k % 2:
+            send[k // 2] = total.astype(send.dtype)
+        else:
+            keep[k // 2] = total
+
+
+def fold_kernel(keep, got, own, send):
+    own[...] = keep[0] + got[0].astype(F32)
+    send[...] = (keep[1] + got[1].astype(F32)).astype(send.dtype)
+
+
+def add_kernel(*refs):
+    total = refs[0][...].astype(F32)
+    for other in refs[1:-1]:
+        total += other[...].astype(F32)
+    refs[-1][...] = total.astype(refs[-1].dtype)
+
+
+def stack_kernel(*refs):
+    for k, ref in enumerate(refs[:-1]):
+        refs[-1][k] = ref[...]
+
+
+def carry_kernel(own, got, sums, more, out):
+    rows, lanes = own.shape
+    out[:rows, :] = (own[...] + got[...].astype(F32)).astype(BF16)
+    values = jnp.concatenate([sums[b] + more[b] for b in range(sums.shape[0])], axis=0)
+    rest = values[:, lanes:]
+    gap = jnp.zeros((rest.shape[0], lanes - rest.shape[1]), F32)
+    values = jnp.concatenate([values[:, :lanes], jnp.concatenate([rest, gap], axis=1)], axis=0)
+    high = values.astype(BF16).astype(F32)
+    out[rows:, :] = jnp.concatenate([high, values - high], axis=0).astype(BF16)
+
+
+def weight_kernel(scale, *refs):
+    out, sums, scratch = refs[-3:]
+    z, y, _ = place()
+    rows, _ = refs[0].shape
+    groups = (len(refs) - 5) // 3
+    near_a, early = refs[:groups], refs[groups]
+    far_a = [early.at[k] for k in range(groups - 1)] + [refs[groups + 1]]
+    refs = refs[groups + 2 :]
+    count = scratch.shape[1]
     for k in range(groups):
-        total = own[z ^ k]
-        for other in got:
-            total += other[z ^ k].astype(F32)
-        outs[k][...] = total.astype(outs[k].dtype)
-
-
-def add_kernel(own, *refs):
-    total = own[...]
-    for other in refs[:-1]:
-        total += other[...].astype(F32)
-    refs[-1][...] = total.astype(BF16)
-
-
-def weight_kernel(groups, scale, *refs):
-    mine, other, out = refs[:groups], refs[groups : 2 * groups], refs[-1]
-    z, y, _ = place()
-    rows, wide = mine[0].shape
-    half = wide // 3
-    for k in range(groups):
-        a, b = mine[k][...].astype(F32) * scale, other[k][...].astype(F32) * scale
+        sides = []
+        for side, first in enumerate((near_a, far_a)):
+            second = refs[side * groups + k]
+            carried = second[rows:, :].astype(F32)
+            whole = carried[: 2 * count] + carried[2 * count :]
+            rest = scratch.shape[2] - whole.shape[1]
+            scratch[(z ^ k) * 2 + (y ^ side)] = jnp.concatenate([whole[:count], whole[count:, :rest]], axis=1)
+            sides.append(jnp.concatenate([first[k][...].astype(F32), second[:rows, :].astype(F32)], axis=1) * scale)
+        a, b = sides
+        half = a.shape[1] // 3
         low, high = pick(y == 0, a, b), pick(y == 0, b, a)
-        parts = []
+        whole = []
         for j in range(3):
             cut = slice(j * half, (j + 1) * half)
-            parts += [low[:, cut], high[:, cut]]
-        out[pl.ds(pl.multiple_of((z ^ k) * rows, rows), rows), :] = jnp.concatenate(parts, axis=1)
+            whole += [low[:, cut], high[:, cut]]
+        out[pl.ds(pl.multiple_of((z ^ k) * rows, rows), rows), :] = jnp.concatenate(whole, axis=1)
+    total = scratch[0]
+    for frame in range(1, scratch.shape[0]):
+        total += scratch[frame]
+    for b in range(sums.shape[0]):
+        sums[b] = total[2 * b : 2 * b + 2] * scale
+
+
+def together(*values):
+    return lax.optimization_barrier(values)
 
 
 def per_device(
@@ -322,7 +370,9 @@
     tokens = clips * frames * chunk
     block = frames * SLAB
     rows = share // groups
-    pieces = share % 16 == 0 and share % (8 * groups) == 0
+    pieces = groups == 4 and lines == 2 and share % 32 == 0
+    middle = -(-wide // 2 // LANES) * LANES
+    cuts = [slice(0, middle), slice(middle, wide)] if pieces else []
     shares = spaces if pieces else 1
     grad_scale_factor = float(clips * positions * frames * spaces) ** (-0.5)
 
@@ -338,40 +388,49 @@
     hidden = hidden_in.reshape(clips, positions, width)
     cotangent = attn_cotangent.reshape(clips, positions, width)
 
-    w_half = call(halves_kernel, "w_half", shape((share, wide)), [VMEM], moved=3 << 20)(w_qkv)
-    if pieces:
-        weights = [w_half, over_space(w_half, 1)]
-        for j in range(1, lines):
-            crossed = over_space(w_half, 2 * j)
-            weights += [crossed, over_space(crossed, 1)]
-    else:
-        weights = [lax.all_gather(w_half, "space", axis=0, tiled=True)]
-
+    modulation = call(
+        lookup_kernel,
+        "lookup",
+        shape((clips, 3, width), F32),
+        [HBM, SMEM, SMEM, SMEM],
+        [pltpu.VMEM((clips, 2, width), BF16), pltpu.SemaphoreType.DMA((clips,))],
+        vmem=60,
+    )(modulation_table, timestep, snr_table, weight_index)
     prep = call(
         functools.partial(prep_kernel, groups),
         "prep",
-        [shape((clips, chunk, width + half))] * groups
-        + [shape((clips, chunk, half))] * groups
-        + [shape((clips, 2, width), F32)],
-        [VMEM, VMEM, ANY, SMEM, SMEM, SMEM],
-        [pltpu.VMEM((clips, 2, width), BF16), pltpu.SemaphoreType.DMA((clips,))],
+        [shape((clips, chunk, width + half))] * groups + [shape((clips, chunk, half))] * groups,
+        [VMEM] * 3,
         moved=3 << 20,
-    )(hidden, cotangent, modulation_table, timestep, snr_table, weight_index)
-    send, keep, modulation = prep[:groups], prep[groups : 2 * groups], prep[-1]
+    )(hidden, cotangent, modulation)
+    send, keep = prep[:groups], prep[groups:]
+    w_half = call(halves_kernel, "w_half", shape((share, wide)), [VMEM], moved=3 << 20)(
+        after(w_qkv, send[0])
+    )
+    if pieces:
+        crossed = [over_space(w_half, 2 * j) for j in range(1, lines)]
     near = [send[0]] + [over_z(send[k], k) for k in range(1, groups)]
-    far = [over_y(x) for x in near]
+    far = [over_y(near[0])]
+    for k in range(1, groups):
+        near[k] = after(near[k], far[-1])
+        far.append(over_y(near[k]))
     kept = [keep[0]] + [over_z(keep[k], k) for k in range(1, groups)]
+    if pieces:
+        weights = [w_half, over_space(w_half, 1)]
+        for x in crossed:
+            weights += [x, over_space(after(x, *near[1:]), 1)]
+    else:
+        weights = [lax.all_gather(w_half, "space", axis=0, tiled=True)]
 
     pad = -(-half // LANES) * LANES
     outs = [shape((tokens, wide)), shape((width, tokens))]
-    if pieces:
-        outs.append(shape((lines, groups, rows, wide)))
+    outs += [shape((lines, groups, rows, cut.stop - cut.start)) for cut in cuts]
     w_scratch = pltpu.VMEM((width, wide), BF16)
     main = call(
-        functools.partial(main_kernel, groups, shares, lines if pieces else 0),
+        functools.partial(main_kernel, groups, shares, cuts),
         "attend",
         outs,
-        [VMEM] * (3 * groups) + [ANY] * shares,
+        [VMEM] * (3 * groups) + [HBM] * shares,
         [
             w_scratch,
             pltpu.VMEM((tokens, width), BF16),
@@ -389,51 +448,108 @@
     )(*near, *kept, *far, *weights)
     grads, mod_t = main[0], main[1]
 
-    near_hidden, far_hidden = call(
-        functools.partial(hidden_kernel, groups, shares),
+    far_hidden, near_hidden = call(
+        functools.partial(hidden_kernel, shares),
         "grad_hidden",
         [shape((groups, clips, chunk, width))] * 2,
-        [VMEM] + [ANY] * shares,
+        [VMEM] + [HBM] * shares,
         [w_scratch, pltpu.VMEM((tokens // 2, wide), BF16), pltpu.SemaphoreType.DMA((shares,))],
         flops=2 * tokens * width * wide,
         moved=8 << 20,
     )(grads, *weights)
 
+    def meet(came):
+        back = call(
+            meet_kernel, "meet", [shape((clips, chunk, width))] * groups, [VMEM] * 2, moved=2 << 20
+        )(near_hidden, came)
+        return [back[0]] + [over_z(back[k], k) for k in range(1, groups)]
+
+    def finish(back):
+        return call(
+            functools.partial(input_kernel, groups),
+            "grad_input",
+            [shape((clips, positions, width)), shape((clips, 2, width), F32)],
+            [VMEM] * (2 + groups),
+            moved=2 << 20,
+        )(hidden, modulation, *back)
+
     if pieces:
-        got = over_space(main[2], 1)
-
-        def own(step, kind):
+        def own(p, step, got, kind):
             return call(
-                functools.partial(own_kernel, step, share),
+                functools.partial(own_kernel, step, share, cuts[p]),
                 "grad_w_rows",
-                shape((groups, rows, wide), kind),
+                shape((groups, rows, cuts[p].stop - cuts[p].start), kind),
                 [VMEM] * 3,
-                flops=2 * tokens * share * wide,
-                moved=8 << 20,
             )(mod_t, grads, got)
 
-        crossed = [over_space(own(j, BF16), 2 * j) for j in range(1, lines)]
-        mine = own(0, F32)
-        spread = call(
-            spread_kernel,
-            "spread",
-            [shape((rows, wide), F32)] + [shape((rows, wide))] * (groups - 1),
-            [VMEM] * lines,
-            moved=4 << 20,
-        )(mine, *crossed)
-        summed = call(add_kernel, "sum_z", shape((rows, wide)), [VMEM] * groups)(
-            spread[0], *[over_z(spread[k], k) for k in range(1, groups)]
-        )
-        halves = [summed] + [over_z(summed, k) for k in range(1, groups)]
-        others = [over_y(x) for x in halves]
-        grad_weight = call(
-            functools.partial(weight_kernel, groups, grad_scale_factor),
+        def spread(p, mine, crossed):
+            dims = (groups // 2, rows, cuts[p].stop - cuts[p].start)
+            return call(spread_kernel, "spread", [shape(dims, F32), shape(dims)], [VMEM] * 2)(mine, crossed)
+
+        def fold(keep, got):
+            dims = keep.shape[1:]
+            return call(fold_kernel, "fold", [shape(dims, F32), shape(dims)], [VMEM] * 2)(keep, got)
+
+        def total(*terms):
+            return call(add_kernel, "sum_z", shape(terms[0].shape), [VMEM] * len(terms))(*terms)
+
+        core_a, core_b = (over_space(main[2 + p], 1) for p in range(2))
+        x_a = over_space(own(0, 1, core_a, BF16), 2)
+        x_b = over_space(own(1, 1, core_b, BF16), 2)
+        mine = [own(0, 0, core_a, F32), own(1, 0, core_b, F32)]
+        came = over_y(far_hidden)
+
+        keep_a, send_a = spread(0, mine[0], x_a)
+        next_a = over_z(send_a, 1)
+        next_a, came = together(next_a, came)
+        own_a, send_a = fold(keep_a, next_a)
+        over_a = over_z(send_a, 2)
+        back = meet(came)
+        x_b, over_a, back[1] = together(x_b, over_a, back[1])
+        keep_b, send_b = spread(1, mine[1], x_b)
+        next_b = over_z(send_b, 1)
+        next_b, back[2], back[3] = together(next_b, back[2], back[3])
+        sum_a = total(own_a, over_a)
+        own_b, send_b = fold(keep_b, next_b)
+        grad_input, sums = finish(back)
+        over_b = over_z(send_b, 2)
+        a2, a1 = over_z(sum_a, 2), over_z(sum_a, 1)
+        sums = sums + over_space(sums, 1)
+        got = over_space(sums, 2)
+        over_b, a2, a1, got = together(over_b, a2, a1, got)
+        sum_b = call(
+            carry_kernel,
+            "sum_z",
+            shape((rows + 4 * 2 * clips, own_b.shape[1])),
+            [VMEM] * 4,
+        )(own_b, over_b, sums, got)
+        a3 = over_z(a2, 1)
+        c2, c1, d0 = over_z(sum_b, 2), over_z(sum_b, 1), over_y(sum_b)
+        early = call(stack_kernel, "stack", shape((groups - 1, *sum_a.shape)), [VMEM] * (groups - 1))(sum_a, a1, a2)
+        early = over_y(early)
+        a3, c2, c1, d0, early = together(a3, c2, c1, d0, early)
+        b3, c3, d1, d2 = over_y(a3), over_z(c2, 1), over_y(c1), over_y(c2)
+        c3, b3 = together(c3, b3)
+        d3 = over_y(c3)
+        grad_weight, sums = call(
+            functools.partial(weight_kernel, grad_scale_factor),
             "grad_w",
-            shape((share, 2 * wide), F32),
-            [VMEM] * (2 * groups),
-            moved=8 << 20,
-        )(*halves, *others)
+            [shape((share, 2 * wide), F32), shape((clips, 2, width), F32)],
+            [VMEM] * (2 + 3 * groups),
+            [pltpu.VMEM((frames, 2 * clips, width), F32)],
+        )(sum_a, a1, a2, a3, early, b3, sum_b, c1, c2, c3, d0, d1, d2, d3)
     else:
+        grad_input, sums = finish(meet(over_y(far_hidden)))
+        step = 1
+        while step < spaces:
+            sums += over_space(sums, step)
+            step *= 2
+        sums += over_y(sums)
+        step = 1
+        while step < groups:
+            sums += over_z(sums, step)
+            step *= 2
+        sums *= grad_scale_factor
         partial = jnp.dot(mod_t, grads, preferred_element_type=F32).astype(BF16)
         summed = lax.psum_scatter(partial, "space", scatter_dimension=0, tiled=True)
         sides = [list(range(side, frames, 2)) for side in range(2)]
@@ -445,27 +561,7 @@
         grad_weight = jnp.concatenate([low, high], axis=2).reshape(share, 2 * wide)
         grad_weight = grad_weight.astype(F32) * grad_scale_factor
 
-    back = call(
-        meet_kernel, "meet", [shape((clips, chunk, width))] * groups, [VMEM] * 2, moved=2 << 20
-    )(near_hidden, over_y(far_hidden))
-    back = [back[0]] + [over_z(back[k], k) for k in range(1, groups)]
-    grad_input, sums = call(
-        functools.partial(input_kernel, groups),
-        "grad_input",
-        [shape((clips, positions, width)), shape((clips, 2, width), F32)],
-        [VMEM] * (2 + groups),
-        moved=2 << 20,
-    )(hidden, modulation, *back)
-    step = 1
-    while step < spaces:
-        sums += over_space(sums, step)
-        step *= 2
-    sums += over_y(sums)
-    step = 1
-    while step < groups:
-        sums += over_z(sums, step)
-        step *= 2
-    return (grad_input.reshape(hidden_in.shape), grad_weight, sums * grad_scale_factor)
+    return (grad_input.reshape(hidden_in.shape), grad_weight, sums)
 
 
 def solution(mesh):

time: 224 us -> 152 us (0.68)
  waiting for transfers between devices: 134 us -> 72.6 us
  starting transfers between devices: 60 us -> 50.7 us
  local copies, waits for them, and re-layouts: 3.87 us -> 0.78 us
  Pallas kernels: 24.3 us -> 26.7 us
    ppermute x7 -> x9, waiting for transfers between devices: 47 us -> 11.7 us  [over_space(): return lax.ppermute(x, 'space', [(i, i ^ step) for i in range(spaces)])]
    ppermute x17 -> x19, waiting for transfers between devices: 55.1 us -> 41 us  [over_z(): return lax.ppermute(x, 'frame', [(i, i ^ 2 * step) for i in range(frames)])]
    ppermute x10 -> x11, waiting for transfers between devices: 32 us -> 19.9 us  [over_y(): return lax.ppermute(x, 'frame', [(i, i ^ 1) for i in range(frames)])]
    ppermute x17 -> x19, starting transfers between devices: 41 us -> 29.7 us  [over_z(): return lax.ppermute(x, 'frame', [(i, i ^ 2 * step) for i in range(frames)])]
    pallas_call x9 -> x17, Pallas kernels: 21.9 us -> 25 us  [the longest x1 11.5 us: per_device(): call(functools.partial(main_kernel, groups, shares, cuts), 'attend', outs...]
    unnamed x14 -> x10, local copies, waits for them, and re-layouts: 3.87 us -> 0.78 us
    ppermute x10 -> x11, starting transfers between devices: 12.7 us -> 14.2 us  [over_y(): return lax.ppermute(x, 'frame', [(i, i ^ 1) for i in range(frames)])]
    ppermute x7 -> x9, starting transfers between devices: 6.26 us -> 6.74 us  [over_space(): return lax.ppermute(x, 'space', [(i, i ^ step) for i in range(spaces)])]
  transfers between devices with their start and end apart: 34 -> 39, of which waited for: 20 -> 19; matrix products, arithmetic and copies ran while one was open for 0% -> 0% of each run, Pallas kernels for 4% -> 5%
where the time goes in v3:
time: 152 us
  waiting for transfers between devices  72.6 us (48%)
  starting transfers between devices  50.7 us (33%)
  Pallas kernels  26.7 us (18%)
    ppermute x19, waiting for transfers between devices, over_z(): return lax.ppermute(x, 'frame', [(i, i ^ 2 * step) for i in range(frames)])  41 us
    ppermute x19, starting transfers between devices, over_z(): return lax.ppermute(x, 'frame', [(i, i ^ 2 * step) for i in range(frames)])  29.7 us
    ppermute x11, waiting for transfers between devices, over_y(): return lax.ppermute(x, 'frame', [(i, i ^ 1) for i in range(frames)])  19.9 us
    ppermute x11, starting transfers between devices, over_y(): return lax.ppermute(x, 'frame', [(i, i ^ 1) for i in range(frames)])  14.2 us
    ppermute x9, waiting for transfers between devices, over_space(): return lax.ppermute(x, 'space', [(i, i ^ step) for i in range(spaces)])  11.7 us
    pallas_call x1, Pallas kernels, per_device(): call(functools.partial(main_kernel, groups, shares, cuts), 'attend', outs...  11.5 us
    ppermute x9, starting transfers between devices, over_space(): return lax.ppermute(x, 'space', [(i, i ^ step) for i in range(spaces)])  6.74 us
    pallas_call x1, Pallas kernels, per_device(): call(functools.partial(hidden_kernel, shares), 'grad_hidden', [shape((gro...  4.15 us
  transfers between devices with their start and end apart: 39, of which 19 were waited for; matrix products, arithmetic and copies ran while one was open for 0% of the time, Pallas kernels for 5%

profile of v3, /device:TPU:0, one launch (start us, length us, event | category | flops | bytes accessed | tf_op | source)
XLA Modules:
  0.0 151.7 jit_solution(5200487207253554258)
XLA Ops:
  0.7 2.3 %lookup.1.mod_ref = f32[2,3,1152]{2,1,0:T(4,128)} custom-call(bf16[1000,2,1152]{2,1,0:T(2,128)(2,1)} %tab_ref.1, s32[2]{0:T(128)} %ts_ref.1, f32[1000]{0:T(1024)} %snr_ref.1, s32[2]{0:T(128)} %wi_ref.1), custom_call_target="tpu_custom_call" | custom-call | bytes 1048576 | tf_op jit(solution)/shard_map/lookup/pallas_call | solution.py:391
  5.5 3.0 %collective-permute-start.11 = (bf16[288,1728]{1,0:T(8,128)(2,1)S(1)}, bf16[288,1728]{1,0:T(8,128)(2,1)S(1)}, u32[]{:S(2)}, u32[]{:S(2)}) collective-permute-start(bf16[288,1728]{1,0:T(8,128)(2,1)S(1)} %w_half.1.refs_12_.refs_0_), channel_id=1, source_target_pairs={{0,2},{1,3},{2,0},{3,1},{4,6},{5,7},{6,4},{7,5},{8,10},{9,11},{10,... | collective-permute-start | bytes 2985992 | tf_op jit(solution)/shard_map/ppermute | solution.py:380
  11.7 2.6 %collective-permute-start.2 = (bf16[2,32,1728]{2,1,0:T(8,128)(2,1)S(1)}, bf16[2,32,1728]{2,1,0:T(8,128)(2,1)S(1)}, u32[]{:S(2)}, u32[]{:S(2)}) collective-permute-start(bf16[2,32,1728]{2,1,0:T(8,128)(2,1)S(1)} %get-tuple-element.60), channel_id=1, source_target_pairs={{0,16},{4,20},{8,24},{12,28},{16,0},{20,4},{24,8},{28,12},{1,17},{... | collective-permute-start | bytes 663560 | tf_op jit(solution)/shard_map/ppermute | solution.py:386
  14.3 4.5 %collective-permute-done.refs_1_ = bf16[2,32,1728]{2,1,0:T(8,128)(2,1)S(1)} collective-permute-done((bf16[2,32,1728]{2,1,0:T(8,128)(2,1)S(1)}, bf16[2,32,1728]{2,1,0:T(8,128)(2,1)S(1)}, u32[]{:S(2)}, u32[]{:S(2)}) %collective-permute-start) | collective-permute-done | bytes 221216 | tf_op jit(solution)/shard_map/ppermute | solution.py:386
  18.8 3.0 %collective-permute-start.3 = (bf16[2,32,1728]{2,1,0:T(8,128)(2,1)S(1)}, bf16[2,32,1728]{2,1,0:T(8,128)(2,1)S(1)}, u32[]{:S(2)}, u32[]{:S(2)}) collective-permute-start(bf16[2,32,1728]{2,1,0:T(8,128)(2,1)S(1)} %collective-permute-done.refs_1_), channel_id=1, source_target_pairs={{0,4},{4,0},{8,12},{12,8},{16,20},{20,16},{24,28},{28,24},{1,5},{5... | collective-permute-start | bytes 663560 | tf_op jit(solution)/shard_map/ppermute | solution.py:383
  21.8 2.5 %collective-permute-start.4 = (bf16[2,32,1728]{2,1,0:T(8,128)(2,1)S(1)}, bf16[2,32,1728]{2,1,0:T(8,128)(2,1)S(1)}, u32[]{:S(2)}, u32[]{:S(2)}) collective-permute-start(bf16[2,32,1728]{2,1,0:T(8,128)(2,1)S(1)} %get-tuple-element.62), channel_id=1, source_target_pairs={{0,24},{4,28},{8,16},{12,20},{16,8},{20,12},{24,0},{28,4},{1,25},{... | collective-permute-start | bytes 663560 | tf_op jit(solution)/shard_map/ppermute | solution.py:386
  24.3 6.0 %collective-permute-done.2.refs_2_ = bf16[2,32,1728]{2,1,0:T(8,128)(2,1)S(1)} collective-permute-done((bf16[2,32,1728]{2,1,0:T(8,128)(2,1)S(1)}, bf16[2,32,1728]{2,1,0:T(8,128)(2,1)S(1)}, u32[]{:S(2)}, u32[]{:S(2)}) %collective-permute-start.2) | collective-permute-done | bytes 221216 | tf_op jit(solution)/shard_map/ppermute | solution.py:386
  30.4 6.0 %collective-permute-done.5.refs_10_ = bf16[2,32,1728]{2,1,0:T(8,128)(2,1)S(1)} collective-permute-done((bf16[2,32,1728]{2,1,0:T(8,128)(2,1)S(1)}, bf16[2,32,1728]{2,1,0:T(8,128)(2,1)S(1)}, u32[]{:S(2)}, u32[]{:S(2)}) %collective-permute-start.5) | collective-permute-done | bytes 221216 | tf_op jit(solution)/shard_map/ppermute | solution.py:383
  36.5 3.3 %collective-permute-start.7 = (bf16[2,32,576]{2,1,0:T(8,128)(2,1)S(1)}, bf16[2,32,576]{2,1,0:T(8,128)(2,1)S(1)}, u32[]{:S(2)}, u32[]{:S(2)}) collective-permute-start(bf16[2,32,576]{2,1,0:T(8,128)(2,1)S(1)} %get-tuple-element.66), channel_id=1, source_target_pairs={{0,16},{4,20},{8,24},{12,28},{16,0},{20,4},{24,8},{28,12},{1,17},{... | collective-permute-start | bytes 221192 | tf_op jit(solution)/shard_map/ppermute | solution.py:386
  39.7 3.0 %collective-permute-done.6.refs_5_ = bf16[2,32,576]{2,1,0:T(8,128)(2,1)S(1)} collective-permute-done((bf16[2,32,576]{2,1,0:T(8,128)(2,1)S(1)}, bf16[2,32,576]{2,1,0:T(8,128)(2,1)S(1)}, u32[]{:S(2)}, u32[]{:S(2)}) %collective-permute-start.6) | collective-permute-done | bytes 73760 | tf_op jit(solution)/shard_map/ppermute | solution.py:386
  42.8 2.3 %collective-permute-start.8 = (bf16[2,32,576]{2,1,0:T(8,128)(2,1)S(1)}, bf16[2,32,576]{2,1,0:T(8,128)(2,1)S(1)}, u32[]{:S(2)}, u32[]{:S(2)}) collective-permute-start(bf16[2,32,576]{2,1,0:T(8,128)(2,1)S(1)} %get-tuple-element.67), channel_id=1, source_target_pairs={{0,24},{4,28},{8,16},{12,20},{16,8},{20,12},{24,0},{28,4},{1,25},{... | collective-permute-start | bytes 221192 | tf_op jit(solution)/shard_map/ppermute | solution.py:386
  45.1 3.9 %collective-permute-done.8.refs_7_ = bf16[2,32,576]{2,1,0:T(8,128)(2,1)S(1)} collective-permute-done((bf16[2,32,576]{2,1,0:T(8,128)(2,1)S(1)}, bf16[2,32,576]{2,1,0:T(8,128)(2,1)S(1)}, u32[]{:S(2)}, u32[]{:S(2)}) %collective-permute-start.8) | collective-permute-done | bytes 73760 | tf_op jit(solution)/shard_map/ppermute | solution.py:386
  49.0 11.5 %attend.1 = (bf16[512,1728]{1,0:T(8,128)(2,1)S(1)}, bf16[1152,512]{1,0:T(8,128)(2,1)S(1)}, bf16[2,4,72,896]{3,2,1,0:T(8,128)(2,1)S(1)}, bf16[2,4,72,832]{3,2,1,0:T(8,128)(2,1)S(1)}) custom-call(bf16[2,32,1728]{2,1,0:T(8,128)(2,1)S(1)} %get-tuple-element.57.refs_0_, bf16[2,32,1728]{2,1,0:T(8,128)(2,1)S(1)} %collective-permute-done.refs_1_, ...), custom_call_target="tpu_custom_call" | custom-call | flops 6115295232 | bytes 20971520 | tf_op jit(solution)/shard_map/attend/pallas_call | solution.py:429
  61.1 2.1 %collective-permute-done.13.got = bf16[2,4,72,896]{3,2,1,0:T(8,128)(2,1)S(1)} collective-permute-done((bf16[2,4,72,896]{3,2,1,0:T(8,128)(2,1)S(1)}, bf16[2,4,72,896]{3,2,1,0:T(8,128)(2,1)S(1)}, u32[]{:S(2)}, u32[]{:S(2)}) %collective-permute-start.13) | collective-permute-done | bytes 1032224 | tf_op jit(solution)/shard_map/ppermute | solution.py:380
  64.3 4.2 %grad_hidden.1 = (bf16[4,2,32,1152]{3,2,1,0:T(8,128)(2,1)S(1)}, bf16[4,2,32,1152]{3,2,1,0:T(8,128)(2,1)S(1)}) custom-call(bf16[512,1728]{1,0:T(8,128)(2,1)S(1)} %get-tuple-element.70.grads, bf16[288,1728]{1,0:T(8,128)(2,1)S(1)} %w_half.1.refs_12_.refs_0_, bf16[288,1728]{1,0:T(8,128)(2,1)S(1)} %collective-permute-done.10.refs_13_.refs_1_, ...), custom_call_target="tpu_custom_call" | custom-call | flops 2038431744 | bytes 8388608 | tf_op jit(solution)/shard_map/grad_hidden/pallas_call | solution.py:451
  72.8 5.6 %collective-permute-done.14.got = bf16[4,72,896]{2,1,0:T(8,128)(2,1)S(1)} collective-permute-done((bf16[4,72,896]{2,1,0:T(8,128)(2,1)S(1)}, bf16[4,72,896]{2,1,0:T(8,128)(2,1)S(1)}, u32[]{:S(2)}, u32[]{:S(2)}) %collective-permute-start.14) | collective-permute-done | bytes 516128 | tf_op jit(solution)/shard_map/ppermute | solution.py:380
  78.5 5.1 %collective-permute-done.16.got = bf16[4,2,32,1152]{3,2,1,0:T(8,128)(2,1)S(1)} collective-permute-done((bf16[4,2,32,1152]{3,2,1,0:T(8,128)(2,1)S(1)}, bf16[4,2,32,1152]{3,2,1,0:T(8,128)(2,1)S(1)}, u32[]{:S(2)}, u32[]{:S(2)}) %collective-permute-start.16) | collective-permute-done | bytes 589856 | tf_op jit(solution)/shard_map/ppermute | solution.py:383
  85.7 2.7 %collective-permute-start.19 = (bf16[72,896]{1,0:T(8,128)(2,1)S(1)}, bf16[72,896]{1,0:T(8,128)(2,1)S(1)}, u32[]{:S(2)}, u32[]{:S(2)}) collective-permute-start(bf16[72,896]{1,0:T(8,128)(2,1)S(1)} %get-tuple-element.81), channel_id=1, source_target_pairs={{0,16},{4,20},{8,24},{12,28},{16,0},{20,4},{24,8},{28,12},{1,17},{... | collective-permute-start | bytes 387080 | tf_op jit(solution)/shard_map/ppermute | solution.py:386
  88.9 4.3 %collective-permute-done.19.refs_1_ = bf16[72,896]{1,0:T(8,128)(2,1)S(1)} collective-permute-done((bf16[72,896]{1,0:T(8,128)(2,1)S(1)}, bf16[72,896]{1,0:T(8,128)(2,1)S(1)}, u32[]{:S(2)}, u32[]{:S(2)}) %collective-permute-start.19) | collective-permute-done | bytes 129056 | tf_op jit(solution)/shard_map/ppermute | solution.py:386
  93.6 2.0 %collective-permute-start.22 = (bf16[2,32,1152]{2,1,0:T(8,128)(2,1)S(1)}, bf16[2,32,1152]{2,1,0:T(8,128)(2,1)S(1)}, u32[]{:S(2)}, u32[]{:S(2)}) collective-permute-start(bf16[2,32,1152]{2,1,0:T(8,128)(2,1)S(1)} %get-tuple-element.86), channel_id=1, source_target_pairs={{0,16},{4,20},{8,24},{12,28},{16,0},{20,4},{24,8},{28,12},{1,17},{... | collective-permute-start | bytes 442376 | tf_op jit(solution)/shard_map/ppermute | solution.py:386
  95.6 2.1 %collective-permute-start.23 = (bf16[2,32,1152]{2,1,0:T(8,128)(2,1)S(1)}, bf16[2,32,1152]{2,1,0:T(8,128)(2,1)S(1)}, u32[]{:S(2)}, u32[]{:S(2)}) collective-permute-start(bf16[2,32,1152]{2,1,0:T(8,128)(2,1)S(1)} %get-tuple-element.87), channel_id=1, source_target_pairs={{0,24},{4,28},{8,16},{12,20},{16,8},{20,12},{24,0},{28,4},{1,25},{... | collective-permute-start | bytes 442376 | tf_op jit(solution)/shard_map/ppermute | solution.py:386
  97.8 2.3 %collective-permute-start.25 = (bf16[72,896]{1,0:T(8,128)(2,1)S(1)}, bf16[72,896]{1,0:T(8,128)(2,1)S(1)}, u32[]{:S(2)}, u32[]{:S(2)}) collective-permute-start(bf16[72,896]{1,0:T(8,128)(2,1)S(1)} %sum_z.2.refs_0_), channel_id=1, source_target_pairs={{0,16},{4,20},{8,24},{12,28},{16,0},{20,4},{24,8},{28,12},{1,17},{... | collective-permute-start | bytes 387080 | tf_op jit(solution)/shard_map/ppermute | solution.py:386
  100.1 3.4 %collective-permute-done.22.refs_2_ = bf16[2,32,1152]{2,1,0:T(8,128)(2,1)S(1)} collective-permute-done((bf16[2,32,1152]{2,1,0:T(8,128)(2,1)S(1)}, bf16[2,32,1152]{2,1,0:T(8,128)(2,1)S(1)}, u32[]{:S(2)}, u32[]{:S(2)}) %collective-permute-start.22) | collective-permute-done | bytes 147488 | tf_op jit(solution)/shard_map/ppermute | solution.py:386
  103.5 5.7 %collective-permute-done.23.refs_3_ = bf16[2,32,1152]{2,1,0:T(8,128)(2,1)S(1)} collective-permute-done((bf16[2,32,1152]{2,1,0:T(8,128)(2,1)S(1)}, bf16[2,32,1152]{2,1,0:T(8,128)(2,1)S(1)}, u32[]{:S(2)}, u32[]{:S(2)}) %collective-permute-start.23) | collective-permute-done | bytes 147488 | tf_op jit(solution)/shard_map/ppermute | solution.py:386
  109.3 5.3 %collective-permute-start.24 = (bf16[72,832]{1,0:T(8,128)(2,1)S(1)}, bf16[72,832]{1,0:T(8,128)(2,1)S(1)}, u32[]{:S(2)}, u32[]{:S(2)}) collective-permute-start(bf16[72,832]{1,0:T(8,128)(2,1)S(1)} %get-tuple-element.95), channel_id=1, source_target_pairs={{0,16},{4,20},{8,24},{12,28},{16,0},{20,4},{24,8},{28,12},{1,17},{... | collective-permute-start | bytes 359432 | tf_op jit(solution)/shard_map/ppermute | solution.py:386
  118.6 2.8 %collective-permute-done.28.more = f32[2,2,1152]{2,1,0:T(2,128)S(1)} collective-permute-done((f32[2,2,1152]{2,1,0:T(2,128)S(1)}, f32[2,2,1152]{2,1,0:T(2,128)S(1)}, u32[]{:S(2)}, u32[]{:S(2)}) %collective-permute-start.28) | collective-permute-done | bytes 18464 | tf_op jit(solution)/shard_map/ppermute | solution.py:380
  121.5 1.9 %collective-permute-start.33 = (bf16[3,72,896]{2,1,0:T(8,128)(2,1)S(1)}, bf16[3,72,896]{2,1,0:T(8,128)(2,1)S(1)}, u32[]{:S(2)}, u32[]{:S(2)}) collective-permute-start(bf16[3,72,896]{2,1,0:T(8,128)(2,1)S(1)} %stack.1), channel_id=1, source_target_pairs={{0,4},{4,0},{8,12},{12,8},{16,20},{20,16},{24,28},{28,24},{1,5},{5... | collective-permute-start | bytes 1161224 | tf_op jit(solution)/shard_map/ppermute | solution.py:383
  125.7 8.6 %collective-permute-done.29.refs_3_ = bf16[72,896]{1,0:T(8,128)(2,1)S(1)} collective-permute-done((bf16[72,896]{1,0:T(8,128)(2,1)S(1)}, bf16[72,896]{1,0:T(8,128)(2,1)S(1)}, u32[]{:S(2)}, u32[]{:S(2)}) %collective-permute-start.29) | collective-permute-done | bytes 129056 | tf_op jit(solution)/shard_map/ppermute | solution.py:386
  135.0 1.8 %collective-permute-start.35 = (bf16[72,896]{1,0:T(8,128)(2,1)S(1)}, bf16[72,896]{1,0:T(8,128)(2,1)S(1)}, u32[]{:S(2)}, u32[]{:S(2)}) collective-permute-start(bf16[72,896]{1,0:T(8,128)(2,1)S(1)} %collective-permute-done.29.refs_3_), channel_id=1, source_target_pairs={{0,4},{4,0},{8,12},{12,8},{16,20},{20,16},{24,28},{28,24},{1,5},{5... | collective-permute-start | bytes 387080 | tf_op jit(solution)/shard_map/ppermute | solution.py:383
  138.8 2.6 %collective-permute-done.35.refs_5_ = bf16[72,896]{1,0:T(8,128)(2,1)S(1)} collective-permute-done((bf16[72,896]{1,0:T(8,128)(2,1)S(1)}, bf16[72,896]{1,0:T(8,128)(2,1)S(1)}, u32[]{:S(2)}, u32[]{:S(2)}) %collective-permute-start.35) | collective-permute-done | bytes 129056 | tf_op jit(solution)/shard_map/ppermute | solution.py:383
  143.2 4.1 %collective-permute-done.36.refs_11_ = bf16[88,832]{1,0:T(8,128)(2,1)S(1)} collective-permute-done((bf16[88,832]{1,0:T(8,128)(2,1)S(1)}, bf16[88,832]{1,0:T(8,128)(2,1)S(1)}, u32[]{:S(2)}, u32[]{:S(2)}) %collective-permute-start.36) | collective-permute-done | bytes 146464 | tf_op jit(solution)/shard_map/ppermute | solution.py:383
  148.9 2.8 %grad_w.1 = (f32[288,3456]{1,0:T(8,128)}, f32[2,2,1152]{2,1,0:T(2,128)}) custom-call(bf16[72,896]{1,0:T(8,128)(2,1)S(1)} %sum_z.2.refs_0_, bf16[72,896]{1,0:T(8,128)(2,1)S(1)} %collective-permute-done.26.refs_1_, bf16[72,896]{1,0:T(8,128)(2,1)S(1)} %collective-permute-done.25.refs_2_, bf16[72,896]{1,0:T(8,128)(2,1)S(1)} %collective-permute-done.29.refs_3_, ...), custom_call_target="tpu_custom_call" | custom-call | bytes 1048576 | tf_op jit(solution)/shard_map/grad_w/pallas_call | solution.py:534
  (76 shorter events, 27.7 us)
Async XLA Ops:
  5.5 30.9 %collective-permute-start.11 = (bf16[288,1728]{1,0:T(8,128)(2,1)S(1)}, bf16[288,1728]{1,0:T(8,128)(2,1)S(1)}, u32[]{:S(2)}, u32[]{:S(2)}) collective-permute-start(bf16[288,1728]{1,0:T(8,128)(2,1)S(1)} %w_half.1.refs_12_.refs_0_), channel_id=1, source_target_pairs={{0,2},{1,3},{2,0},{3,1},{4,6},{5,7},{6,4},{7,5},{8,10},{9,11},{10,... | collective-permute-start | bytes 2985992 | tf_op jit(solution)/shard_map/ppermute | solution.py:380
  8.5 10.3 %collective-permute-start = (bf16[2,32,1728]{2,1,0:T(8,128)(2,1)S(1)}, bf16[2,32,1728]{2,1,0:T(8,128)(2,1)S(1)}, u32[]{:S(2)}, u32[]{:S(2)}) collective-permute-start(bf16[2,32,1728]{2,1,0:T(8,128)(2,1)S(1)} %get-tuple-element.58), channel_id=1, source_target_pairs={{0,8},{4,12},{8,0},{12,4},{16,24},{20,28},{24,16},{28,20},{1,9},{5... | collective-permute-start | bytes 663560 | tf_op jit(solution)/shard_map/ppermute | solution.py:386
  10.1 8.7 %collective-permute-start.1 = (bf16[2,32,1728]{2,1,0:T(8,128)(2,1)S(1)}, bf16[2,32,1728]{2,1,0:T(8,128)(2,1)S(1)}, u32[]{:S(2)}, u32[]{:S(2)}) collective-permute-start(bf16[2,32,1728]{2,1,0:T(8,128)(2,1)S(1)} %get-tuple-element.57.refs_0_), channel_id=1, source_target_pairs={{0,4},{4,0},{8,12},{12,8},{16,20},{20,16},{24,28},{28,24},{1,5},{5... | collective-permute-start | bytes 663560 | tf_op jit(solution)/shard_map/ppermute | solution.py:383
  11.7 18.7 %collective-permute-start.2 = (bf16[2,32,1728]{2,1,0:T(8,128)(2,1)S(1)}, bf16[2,32,1728]{2,1,0:T(8,128)(2,1)S(1)}, u32[]{:S(2)}, u32[]{:S(2)}) collective-permute-start(bf16[2,32,1728]{2,1,0:T(8,128)(2,1)S(1)} %get-tuple-element.60), channel_id=1, source_target_pairs={{0,16},{4,20},{8,24},{12,28},{16,0},{20,4},{24,8},{28,12},{1,17},{... | collective-permute-start | bytes 663560 | tf_op jit(solution)/shard_map/ppermute | solution.py:386
  18.8 11.6 %collective-permute-start.3 = (bf16[2,32,1728]{2,1,0:T(8,128)(2,1)S(1)}, bf16[2,32,1728]{2,1,0:T(8,128)(2,1)S(1)}, u32[]{:S(2)}, u32[]{:S(2)}) collective-permute-start(bf16[2,32,1728]{2,1,0:T(8,128)(2,1)S(1)} %collective-permute-done.refs_1_), channel_id=1, source_target_pairs={{0,4},{4,0},{8,12},{12,8},{16,20},{20,16},{24,28},{28,24},{1,5},{5... | collective-permute-start | bytes 663560 | tf_op jit(solution)/shard_map/ppermute | solution.py:383
  21.8 8.5 %collective-permute-start.4 = (bf16[2,32,1728]{2,1,0:T(8,128)(2,1)S(1)}, bf16[2,32,1728]{2,1,0:T(8,128)(2,1)S(1)}, u32[]{:S(2)}, u32[]{:S(2)}) collective-permute-start(bf16[2,32,1728]{2,1,0:T(8,128)(2,1)S(1)} %get-tuple-element.62), channel_id=1, source_target_pairs={{0,24},{4,28},{8,16},{12,20},{16,8},{20,12},{24,0},{28,4},{1,25},{... | collective-permute-start | bytes 663560 | tf_op jit(solution)/shard_map/ppermute | solution.py:386
  30.3 18.7 %collective-permute-start.10 = (bf16[288,1728]{1,0:T(8,128)(2,1)S(1)}, bf16[288,1728]{1,0:T(8,128)(2,1)S(1)}, u32[]{:S(2)}, u32[]{:S(2)}) collective-permute-start(bf16[288,1728]{1,0:T(8,128)(2,1)S(1)} %w_half.1.refs_12_.refs_0_), channel_id=1, source_target_pairs={{0,1},{1,0},{2,3},{3,2},{4,5},{5,4},{6,7},{7,6},{8,9},{9,8},{10,11... | collective-permute-start | bytes 2985992 | tf_op jit(solution)/shard_map/ppermute | solution.py:380
  36.4 12.6 %collective-permute-start.12 = (bf16[288,1728]{1,0:T(8,128)(2,1)S(1)}, bf16[288,1728]{1,0:T(8,128)(2,1)S(1)}, u32[]{:S(2)}, u32[]{:S(2)}) collective-permute-start(bf16[288,1728]{1,0:T(8,128)(2,1)S(1)} %collective-permute-done.11.refs_14_.refs_2_), channel_id=1, source_target_pairs={{0,1},{1,0},{2,3},{3,2},{4,5},{5,4},{6,7},{7,6},{8,9},{9,8},{10,11... | collective-permute-start | bytes 2985992 | tf_op jit(solution)/shard_map/ppermute | solution.py:380
  36.4 12.6 %collective-permute-start.9 = (bf16[2,32,1728]{2,1,0:T(8,128)(2,1)S(1)}, bf16[2,32,1728]{2,1,0:T(8,128)(2,1)S(1)}, u32[]{:S(2)}, u32[]{:S(2)}) collective-permute-start(bf16[2,32,1728]{2,1,0:T(8,128)(2,1)S(1)} %collective-permute-done.4.refs_3_), channel_id=1, source_target_pairs={{0,4},{4,0},{8,12},{12,8},{16,20},{20,16},{24,28},{28,24},{1,5},{5... | collective-permute-start | bytes 663560 | tf_op jit(solution)/shard_map/ppermute | solution.py:383
  36.5 8.6 %collective-permute-start.7 = (bf16[2,32,576]{2,1,0:T(8,128)(2,1)S(1)}, bf16[2,32,576]{2,1,0:T(8,128)(2,1)S(1)}, u32[]{:S(2)}, u32[]{:S(2)}) collective-permute-start(bf16[2,32,576]{2,1,0:T(8,128)(2,1)S(1)} %get-tuple-element.66), channel_id=1, source_target_pairs={{0,16},{4,20},{8,24},{12,28},{16,0},{20,4},{24,8},{28,12},{1,17},{... | collective-permute-start | bytes 221192 | tf_op jit(solution)/shard_map/ppermute | solution.py:386
  60.6 9.7 %collective-permute-start.17 = (bf16[2,4,72,832]{3,2,1,0:T(8,128)(2,1)S(1)}, bf16[2,4,72,832]{3,2,1,0:T(8,128)(2,1)S(1)}, u32[]{:S(2)}, u32[]{:S(2)}) collective-permute-start(bf16[2,4,72,832]{3,2,1,0:T(8,128)(2,1)S(1)} %get-tuple-element.78), channel_id=1, source_target_pairs={{0,1},{1,0},{2,3},{3,2},{4,5},{5,4},{6,7},{7,6},{8,9},{9,8},{10,11... | collective-permute-start | bytes 2875400 | tf_op jit(solution)/shard_map/ppermute | solution.py:380
  63.7 14.7 %collective-permute-start.14 = (bf16[4,72,896]{2,1,0:T(8,128)(2,1)S(1)}, bf16[4,72,896]{2,1,0:T(8,128)(2,1)S(1)}, u32[]{:S(2)}, u32[]{:S(2)}) collective-permute-start(bf16[4,72,896]{2,1,0:T(8,128)(2,1)S(1)} %grad_w_rows.5), channel_id=1, source_target_pairs={{0,2},{1,3},{2,0},{3,1},{4,6},{5,7},{6,4},{7,5},{8,10},{9,11},{10,... | collective-permute-start | bytes 1548296 | tf_op jit(solution)/shard_map/ppermute | solution.py:380
  68.5 15.2 %collective-permute-start.16 = (bf16[4,2,32,1152]{3,2,1,0:T(8,128)(2,1)S(1)}, bf16[4,2,32,1152]{3,2,1,0:T(8,128)(2,1)S(1)}, u32[]{:S(2)}, u32[]{:S(2)}) collective-permute-start(bf16[4,2,32,1152]{3,2,1,0:T(8,128)(2,1)S(1)} %get-tuple-element.75), channel_id=1, source_target_pairs={{0,4},{4,0},{8,12},{12,8},{16,20},{20,16},{24,28},{28,24},{1,5},{5... | collective-permute-start | bytes 1769480 | tf_op jit(solution)/shard_map/ppermute | solution.py:383
  70.7 18.1 %collective-permute-start.18 = (bf16[4,72,832]{2,1,0:T(8,128)(2,1)S(1)}, bf16[4,72,832]{2,1,0:T(8,128)(2,1)S(1)}, u32[]{:S(2)}, u32[]{:S(2)}) collective-permute-start(bf16[4,72,832]{2,1,0:T(8,128)(2,1)S(1)} %grad_w_rows.6), channel_id=1, source_target_pairs={{0,2},{1,3},{2,0},{3,1},{4,6},{5,7},{6,4},{7,5},{8,10},{9,11},{10,... | collective-permute-start | bytes 1437704 | tf_op jit(solution)/shard_map/ppermute | solution.py:380
  78.5 6.7 %collective-permute-start.15 = (bf16[2,72,896]{2,1,0:T(8,128)(2,1)S(1)}, bf16[2,72,896]{2,1,0:T(8,128)(2,1)S(1)}, u32[]{:S(2)}, u32[]{:S(2)}) collective-permute-start(bf16[2,72,896]{2,1,0:T(8,128)(2,1)S(1)} %get-tuple-element.74), channel_id=1, source_target_pairs={{0,8},{4,12},{8,0},{12,4},{16,24},{20,28},{24,16},{28,20},{1,9},{5... | collective-permute-start | bytes 774152 | tf_op jit(solution)/shard_map/ppermute | solution.py:386
  85.3 7.9 %collective-permute-start.20 = (bf16[2,32,1152]{2,1,0:T(8,128)(2,1)S(1)}, bf16[2,32,1152]{2,1,0:T(8,128)(2,1)S(1)}, u32[]{:S(2)}, u32[]{:S(2)}) collective-permute-start(bf16[2,32,1152]{2,1,0:T(8,128)(2,1)S(1)} %get-tuple-element.82), channel_id=1, source_target_pairs={{0,8},{4,12},{8,0},{12,4},{16,24},{20,28},{24,16},{28,20},{1,9},{5... | collective-permute-start | bytes 442376 | tf_op jit(solution)/shard_map/ppermute | solution.py:386
  85.7 7.4 %collective-permute-start.19 = (bf16[72,896]{1,0:T(8,128)(2,1)S(1)}, bf16[72,896]{1,0:T(8,128)(2,1)S(1)}, u32[]{:S(2)}, u32[]{:S(2)}) collective-permute-start(bf16[72,896]{1,0:T(8,128)(2,1)S(1)} %get-tuple-element.81), channel_id=1, source_target_pairs={{0,16},{4,20},{8,24},{12,28},{16,0},{20,4},{24,8},{28,12},{1,17},{... | collective-permute-start | bytes 387080 | tf_op jit(solution)/shard_map/ppermute | solution.py:386
  93.3 15.9 %collective-permute-start.21 = (bf16[2,72,832]{2,1,0:T(8,128)(2,1)S(1)}, bf16[2,72,832]{2,1,0:T(8,128)(2,1)S(1)}, u32[]{:S(2)}, u32[]{:S(2)}) collective-permute-start(bf16[2,72,832]{2,1,0:T(8,128)(2,1)S(1)} %get-tuple-element.85), channel_id=1, source_target_pairs={{0,8},{4,12},{8,0},{12,4},{16,24},{20,28},{24,16},{28,20},{1,9},{5... | collective-permute-start | bytes 718856 | tf_op jit(solution)/shard_map/ppermute | solution.py:386
  93.6 9.9 %collective-permute-start.22 = (bf16[2,32,1152]{2,1,0:T(8,128)(2,1)S(1)}, bf16[2,32,1152]{2,1,0:T(8,128)(2,1)S(1)}, u32[]{:S(2)}, u32[]{:S(2)}) collective-permute-start(bf16[2,32,1152]{2,1,0:T(8,128)(2,1)S(1)} %get-tuple-element.86), channel_id=1, source_target_pairs={{0,16},{4,20},{8,24},{12,28},{16,0},{20,4},{24,8},{28,12},{1,17},{... | collective-permute-start | bytes 442376 | tf_op jit(solution)/shard_map/ppermute | solution.py:386
  95.6 13.5 %collective-permute-start.23 = (bf16[2,32,1152]{2,1,0:T(8,128)(2,1)S(1)}, bf16[2,32,1152]{2,1,0:T(8,128)(2,1)S(1)}, u32[]{:S(2)}, u32[]{:S(2)}) collective-permute-start(bf16[2,32,1152]{2,1,0:T(8,128)(2,1)S(1)} %get-tuple-element.87), channel_id=1, source_target_pairs={{0,24},{4,28},{8,16},{12,20},{16,8},{20,12},{24,0},{28,4},{1,25},{... | collective-permute-start | bytes 442376 | tf_op jit(solution)/shard_map/ppermute | solution.py:386
  97.8 20.8 %collective-permute-start.26 = (bf16[72,896]{1,0:T(8,128)(2,1)S(1)}, bf16[72,896]{1,0:T(8,128)(2,1)S(1)}, u32[]{:S(2)}, u32[]{:S(2)}) collective-permute-start(bf16[72,896]{1,0:T(8,128)(2,1)S(1)} %sum_z.2.refs_0_), channel_id=1, source_target_pairs={{0,8},{4,12},{8,0},{12,4},{16,24},{20,28},{24,16},{28,20},{1,9},{5... | collective-permute-start | bytes 387080 | tf_op jit(solution)/shard_map/ppermute | solution.py:386
  97.8 20.8 %collective-permute-start.25 = (bf16[72,896]{1,0:T(8,128)(2,1)S(1)}, bf16[72,896]{1,0:T(8,128)(2,1)S(1)}, u32[]{:S(2)}, u32[]{:S(2)}) collective-permute-start(bf16[72,896]{1,0:T(8,128)(2,1)S(1)} %sum_z.2.refs_0_), channel_id=1, source_target_pairs={{0,16},{4,20},{8,24},{12,28},{16,0},{20,4},{24,8},{28,12},{1,17},{... | collective-permute-start | bytes 387080 | tf_op jit(solution)/shard_map/ppermute | solution.py:386
  109.3 12.2 %collective-permute-start.24 = (bf16[72,832]{1,0:T(8,128)(2,1)S(1)}, bf16[72,832]{1,0:T(8,128)(2,1)S(1)}, u32[]{:S(2)}, u32[]{:S(2)}) collective-permute-start(bf16[72,832]{1,0:T(8,128)(2,1)S(1)} %get-tuple-element.95), channel_id=1, source_target_pairs={{0,16},{4,20},{8,24},{12,28},{16,0},{20,4},{24,8},{28,12},{1,17},{... | collective-permute-start | bytes 359432 | tf_op jit(solution)/shard_map/ppermute | solution.py:386
  121.5 13.4 %collective-permute-start.33 = (bf16[3,72,896]{2,1,0:T(8,128)(2,1)S(1)}, bf16[3,72,896]{2,1,0:T(8,128)(2,1)S(1)}, u32[]{:S(2)}, u32[]{:S(2)}) collective-permute-start(bf16[3,72,896]{2,1,0:T(8,128)(2,1)S(1)} %stack.1), channel_id=1, source_target_pairs={{0,4},{4,0},{8,12},{12,8},{16,20},{20,16},{24,28},{28,24},{1,5},{5... | collective-permute-start | bytes 1161224 | tf_op jit(solution)/shard_map/ppermute | solution.py:383
  123.4 11.5 %collective-permute-start.32 = (bf16[88,832]{1,0:T(8,128)(2,1)S(1)}, bf16[88,832]{1,0:T(8,128)(2,1)S(1)}, u32[]{:S(2)}, u32[]{:S(2)}) collective-permute-start(bf16[88,832]{1,0:T(8,128)(2,1)S(1)} %sum_z.3.refs_6_), channel_id=1, source_target_pairs={{0,4},{4,0},{8,12},{12,8},{16,20},{20,16},{24,28},{28,24},{1,5},{5... | collective-permute-start | bytes 439304 | tf_op jit(solution)/shard_map/ppermute | solution.py:383
  123.7 11.2 %collective-permute-start.31 = (bf16[88,832]{1,0:T(8,128)(2,1)S(1)}, bf16[88,832]{1,0:T(8,128)(2,1)S(1)}, u32[]{:S(2)}, u32[]{:S(2)}) collective-permute-start(bf16[88,832]{1,0:T(8,128)(2,1)S(1)} %sum_z.3.refs_6_), channel_id=1, source_target_pairs={{0,8},{4,12},{8,0},{12,4},{16,24},{20,28},{24,16},{28,20},{1,9},{5... | collective-permute-start | bytes 439304 | tf_op jit(solution)/shard_map/ppermute | solution.py:386
  123.7 11.2 %collective-permute-start.30 = (bf16[88,832]{1,0:T(8,128)(2,1)S(1)}, bf16[88,832]{1,0:T(8,128)(2,1)S(1)}, u32[]{:S(2)}, u32[]{:S(2)}) collective-permute-start(bf16[88,832]{1,0:T(8,128)(2,1)S(1)} %sum_z.3.refs_6_), channel_id=1, source_target_pairs={{0,16},{4,20},{8,24},{12,28},{16,0},{20,4},{24,8},{28,12},{1,17},{... | collective-permute-start | bytes 439304 | tf_op jit(solution)/shard_map/ppermute | solution.py:386
  125.5 8.9 %collective-permute-start.29 = (bf16[72,896]{1,0:T(8,128)(2,1)S(1)}, bf16[72,896]{1,0:T(8,128)(2,1)S(1)}, u32[]{:S(2)}, u32[]{:S(2)}) collective-permute-start(bf16[72,896]{1,0:T(8,128)(2,1)S(1)} %collective-permute-done.25.refs_2_), channel_id=1, source_target_pairs={{0,8},{4,12},{8,0},{12,4},{16,24},{20,28},{24,16},{28,20},{1,9},{5... | collective-permute-start | bytes 387080 | tf_op jit(solution)/shard_map/ppermute | solution.py:386
  134.9 6.5 %collective-permute-start.34 = (bf16[88,832]{1,0:T(8,128)(2,1)S(1)}, bf16[88,832]{1,0:T(8,128)(2,1)S(1)}, u32[]{:S(2)}, u32[]{:S(2)}) collective-permute-start(bf16[88,832]{1,0:T(8,128)(2,1)S(1)} %collective-permute-done.30.refs_8_), channel_id=1, source_target_pairs={{0,8},{4,12},{8,0},{12,4},{16,24},{20,28},{24,16},{28,20},{1,9},{5... | collective-permute-start | bytes 439304 | tf_op jit(solution)/shard_map/ppermute | solution.py:386
  136.8 10.5 %collective-permute-start.37 = (bf16[88,832]{1,0:T(8,128)(2,1)S(1)}, bf16[88,832]{1,0:T(8,128)(2,1)S(1)}, u32[]{:S(2)}, u32[]{:S(2)}) collective-permute-start(bf16[88,832]{1,0:T(8,128)(2,1)S(1)} %collective-permute-done.30.refs_8_), channel_id=1, source_target_pairs={{0,4},{4,0},{8,12},{12,8},{16,20},{20,16},{24,28},{28,24},{1,5},{5... | collective-permute-start | bytes 439304 | tf_op jit(solution)/shard_map/ppermute | solution.py:383
  137.0 10.2 %collective-permute-start.36 = (bf16[88,832]{1,0:T(8,128)(2,1)S(1)}, bf16[88,832]{1,0:T(8,128)(2,1)S(1)}, u32[]{:S(2)}, u32[]{:S(2)}) collective-permute-start(bf16[88,832]{1,0:T(8,128)(2,1)S(1)} %collective-permute-done.31.refs_7_), channel_id=1, source_target_pairs={{0,4},{4,0},{8,12},{12,8},{16,20},{20,16},{24,28},{28,24},{1,5},{5... | collective-permute-start | bytes 439304 | tf_op jit(solution)/shard_map/ppermute | solution.py:383
  141.4 7.6 %collective-permute-start.38 = (bf16[88,832]{1,0:T(8,128)(2,1)S(1)}, bf16[88,832]{1,0:T(8,128)(2,1)S(1)}, u32[]{:S(2)}, u32[]{:S(2)}) collective-permute-start(bf16[88,832]{1,0:T(8,128)(2,1)S(1)} %collective-permute-done.34.refs_9_), channel_id=1, source_target_pairs={{0,4},{4,0},{8,12},{12,8},{16,20},{20,16},{24,28},{28,24},{1,5},{5... | collective-permute-start | bytes 439304 | tf_op jit(solution)/shard_map/ppermute | solution.py:383
  (12 other events, 68.5 us)

commit v4 on v3

--- a/solution.py
+++ b/solution.py
@@ -23,7 +23,7 @@
     return pl.CostEstimate(flops=flops, bytes_accessed=moved, transcendentals=0)
 
 
-def call(kernel, name, out_shape, in_specs, scratch=(), flops=0, moved=1 << 20, vmem=40):
+def call(kernel, name, out_shape, in_specs, scratch=(), flops=0, moved=1 << 20, vmem=24):
     return pl.pallas_call(
         kernel,
         name=name,
@@ -101,18 +101,17 @@
         out_ref[b, 0:2, :] = scratch[b].astype(F32)
 
 
-def prep_kernel(groups, h_ref, c_ref, mod_ref, *outs):
+def prep_kernel(groups, h_ref, c_ref, *outs):
     send, keep = outs[:groups], outs[groups:]
     z, y, _ = place()
     clips, positions, width = h_ref.shape
     chunk, half = positions // groups, width // 2
     for b in range(clips):
-        shift, scale, weight = mod_ref[b, 0:1, :], 1.0 + mod_ref[b, 1:2, :], mod_ref[b, 2:3, :]
         for k in range(groups):
             rows = pl.ds(pl.multiple_of((z ^ k) * chunk, chunk), chunk)
             normed, _ = layer_norm(h_ref[b, rows, :].astype(F32))
-            send[k][b, :, :width] = (normed * scale + shift).astype(BF16)
-            up = c_ref[b, rows, :].astype(F32) * weight
+            send[k][b, :, :width] = normed.astype(BF16)
+            up = c_ref[b, rows, :].astype(F32)
             low, high = up[:, :half], up[:, half:]
             send[k][b, :, width:] = pick(y == 0, high, low).astype(BF16)
             keep[k][b] = pick(y == 0, low, high).astype(BF16)
@@ -121,9 +120,9 @@
 def main_kernel(groups, shares, cuts, *refs):
     near, kept, far = refs[:groups], refs[groups : 2 * groups], refs[2 * groups : 3 * groups]
     weights = refs[3 * groups : 3 * groups + shares]
-    rest = refs[3 * groups + shares :]
-    outs, scratches = rest[: 2 + len(cuts)], rest[2 + len(cuts) :]
-    grads, mod_t = outs[:2]
+    table, *rest = refs[3 * groups + shares :]
+    outs, scratches = rest[: 3 + len(cuts[:1])], rest[3 + len(cuts[:1]) :]
+    grads, mod_t, normed = outs[:3]
     w, mod, up, qw, kw, vw, dq, dk, dv, sems = scratches
     _, _, s = place()
     clips, chunk, _ = near[0].shape
@@ -140,16 +139,19 @@
         copies.append(pltpu.make_async_copy(weights[k], w.at[rows], sems.at[k]))
         copies[-1].start()
     for b in range(clips):
-        for i in range(slabs):
-            base = (b * slabs + i) * block
-            take = slice(i * SLAB, (i + 1) * SLAB)
-            for k in range(groups):
-                own = slice(base + k * SLAB, base + (k + 1) * SLAB)
-                mod[own, :] = near[k][b, take, :depth]
-                up[own, :half] = kept[k][b, take, :]
-                its = slice(base + (groups + k) * SLAB, base + (groups + k + 1) * SLAB)
-                mod[its, :] = far[k][b, take, :depth]
-                up[its, :half] = far[k][b, take, depth:]
+        shift, scale, loss = table[b, 0:1, :], 1.0 + table[b, 1:2, :], table[b, 2:3, :half]
+        for k in range(groups):
+            for at, ref, tangent in (
+                (k, near[k], kept[k][b]),
+                (groups + k, far[k], far[k][b, :, depth:]),
+            ):
+                modulated = (ref[b, :, :depth].astype(F32) * scale + shift).astype(BF16)
+                upstream = (tangent.astype(F32) * loss).astype(BF16)
+                for i in range(slabs):
+                    base = (b * slabs + i) * block + at * SLAB
+                    normed[base : base + SLAB, :] = ref[b, i * SLAB : (i + 1) * SLAB, :depth]
+                    mod[base : base + SLAB, :] = modulated[i * SLAB : (i + 1) * SLAB]
+                    up[base : base + SLAB, :half] = upstream[i * SLAB : (i + 1) * SLAB]
     up[:, half:] = jnp.zeros((up.shape[0], pad - half), BF16)
     vw[:, half:] = jnp.zeros((block, pad - half), BF16)
     for copy in copies:
@@ -205,22 +207,18 @@
         grads[rows, seam + LANES : 2 * half] = near_k[:, LANES:].astype(BF16)
         grads[rows, 2 * half :] = dv[:, :half].astype(BF16)
 
-    for out, cut in zip(outs[2:], cuts):
-        for j in range(out.shape[0]):
-            start = pl.multiple_of((s ^ 1 ^ (2 * j)) * share, share)
-            total = dot(mod_t[pl.ds(start, share), :], grads[:, cut])
-            for g in range(groups):
-                out[j, g] = total[g * out.shape[2] : (g + 1) * out.shape[2]].astype(out.dtype)
-
-
-def unpack(out, total):
-    groups, clips, chunk, _ = out.shape
-    slabs = chunk // SLAB
-    for b in range(clips):
-        for i in range(slabs):
-            for k in range(groups):
-                start = ((b * slabs + i) * groups + k) * SLAB
-                out[k, b, i * SLAB : (i + 1) * SLAB, :] = total[start : start + SLAB].astype(out.dtype)
+    if cuts:
+        other_kernel(share, cuts[0], mod_t, grads, outs[3])
+
+
+def other_kernel(share, cut, mod_t, grads, out):
+    _, _, s = place()
+    count, groups, rows, _ = out.shape
+    for j in range(count):
+        start = pl.multiple_of((s ^ 1 ^ (2 * j)) * share, share)
+        total = dot(mod_t[pl.ds(start, share), :], grads[:, cut])
+        for g in range(groups):
+            out[j, g] = total[g * rows : (g + 1) * rows].astype(out.dtype)
 
 
 def own_kernel(step, share, cut, mod_t, grads, got, out):
@@ -232,8 +230,8 @@
         out[g] = (total[g * rows : (g + 1) * rows] + got[step, g].astype(F32)).astype(out.dtype)
 
 
-def hidden_kernel(shares, grads, *refs):
-    weights, (far, near, w, part, sems) = refs[:shares], refs[shares:]
+def hidden_kernel(shares, grads, normed, *refs):
+    weights, (far_hidden, near_hidden, sums, w, part, sems) = refs[:shares], refs[shares:]
     _, _, s = place()
     depth = w.shape[0]
     share = depth // shares
@@ -242,16 +240,28 @@
         rows = pl.ds(pl.multiple_of((s ^ k) * share, share), share) if shares > 1 else pl.ds(0, depth)
         copies.append(pltpu.make_async_copy(weights[k], w.at[rows], sems.at[k]))
         copies[-1].start()
-    groups, clips, chunk, _ = near.shape
+    groups, clips, chunk, _ = near_hidden.shape
+    slabs = chunk // SLAB
     side = groups * SLAB
-    for which, out in ((1, far), (0, near)):
-        for n in range(clips * (chunk // SLAB)):
+    sums[...] = jnp.zeros_like(sums)
+    for which, out in ((1, far_hidden), (0, near_hidden)):
+        for n in range(clips * slabs):
             start = (2 * n + which) * side
             part[n * side : (n + 1) * side, :] = grads[start : start + side, :]
         if which:
             for copy in copies:
                 copy.wait()
-        unpack(out, dot(part[...], w[...], ROWS_ROWS))
+        total = dot(part[...], w[...], ROWS_ROWS)
+        for b in range(clips):
+            for i in range(slabs):
+                n = b * slabs + i
+                mine = total[n * side : (n + 1) * side]
+                start = (2 * n + which) * side
+                scaled = mine * normed[start : start + side, :].astype(F32)
+                sums[b, 0:1, :] += jnp.sum(mine, axis=0, keepdims=True)
+                sums[b, 1:2, :] += jnp.sum(scaled, axis=0, keepdims=True)
+                for k in range(groups):
+                    out[k, b, i * SLAB : (i + 1) * SLAB, :] = mine[k * SLAB : (k + 1) * SLAB].astype(out.dtype)
 
 
 def meet_kernel(near, got, *outs):
@@ -260,26 +270,19 @@
 
 
 def input_kernel(groups, h_ref, mod_ref, *refs):
-    parts, (out_ref, sums_ref) = refs[:groups], refs[groups:]
+    parts, out_ref = refs[:groups], refs[groups]
     z, _, _ = place()
     clips, positions, _ = h_ref.shape
     chunk = positions // groups
     for b in range(clips):
-        scale = 1.0 + mod_ref[b][1:2]
-        shift_sum, scale_sum = 0.0, 0.0
+        scale = 1.0 + mod_ref[b, 1:2, :]
         for k in range(groups):
             rows = pl.ds(pl.multiple_of((z ^ k) * chunk, chunk), chunk)
             normed, inverse_std = layer_norm(h_ref[b, rows, :].astype(F32))
-            grad_hidden = parts[k][b].astype(F32)
-            by_normed = grad_hidden * normed
-            shift_sum += jnp.sum(grad_hidden, axis=0, keepdims=True)
-            scale_sum += jnp.sum(by_normed, axis=0, keepdims=True)
-            grad_normed = grad_hidden * scale
+            grad_normed = parts[k][b].astype(F32) * scale
             first = jnp.mean(grad_normed, axis=-1, keepdims=True)
-            second = jnp.mean(by_normed * scale, axis=-1, keepdims=True)
+            second = jnp.mean(grad_normed * normed, axis=-1, keepdims=True)
             out_ref[b, rows, :] = ((grad_normed - first - normed * second) * inverse_std).astype(BF16)
-        sums_ref[b, 0:1, :] = shift_sum
-        sums_ref[b, 1:2, :] = scale_sum
 
 
 def spread_kernel(own, got, keep, send):
@@ -326,7 +329,7 @@
     rows, _ = refs[0].shape
     groups = (len(refs) - 5) // 3
     near_a, early = refs[:groups], refs[groups]
-    far_a = [early.at[k] for k in range(groups - 1)] + [refs[groups + 1]]
+    far_a = [refs[groups + 1]] + [early.at[k] for k in range(groups - 1)]
     refs = refs[groups + 2 :]
     count = scratch.shape[1]
     for k in range(groups):
@@ -396,19 +399,19 @@
         [pltpu.VMEM((clips, 2, width), BF16), pltpu.SemaphoreType.DMA((clips,))],
         vmem=60,
     )(modulation_table, timestep, snr_table, weight_index)
+    w_half = call(halves_kernel, "w_half", shape((share, wide)), [VMEM], moved=3 << 20)(
+        after(w_qkv, modulation)
+    )
+    if pieces:
+        crossed = [over_space(w_half, 2 * j) for j in range(1, lines)]
     prep = call(
         functools.partial(prep_kernel, groups),
         "prep",
         [shape((clips, chunk, width + half))] * groups + [shape((clips, chunk, half))] * groups,
-        [VMEM] * 3,
+        [VMEM] * 2,
         moved=3 << 20,
-    )(hidden, cotangent, modulation)
+    )(after(hidden, w_half), cotangent)
     send, keep = prep[:groups], prep[groups:]
-    w_half = call(halves_kernel, "w_half", shape((share, wide)), [VMEM], moved=3 << 20)(
-        after(w_qkv, send[0])
-    )
-    if pieces:
-        crossed = [over_space(w_half, 2 * j) for j in range(1, lines)]
     near = [send[0]] + [over_z(send[k], k) for k in range(1, groups)]
     far = [over_y(near[0])]
     for k in range(1, groups):
@@ -423,14 +426,15 @@
         weights = [lax.all_gather(w_half, "space", axis=0, tiled=True)]
 
     pad = -(-half // LANES) * LANES
-    outs = [shape((tokens, wide)), shape((width, tokens))]
-    outs += [shape((lines, groups, rows, cut.stop - cut.start)) for cut in cuts]
+    outs = [shape((tokens, wide)), shape((width, tokens)), shape((tokens, width))]
+    other_rows = [shape((lines, groups, rows, cut.stop - cut.start)) for cut in cuts]
+    outs += other_rows[:1]
     w_scratch = pltpu.VMEM((width, wide), BF16)
     main = call(
         functools.partial(main_kernel, groups, shares, cuts),
         "attend",
         outs,
-        [VMEM] * (3 * groups) + [HBM] * shares,
+        [VMEM] * (3 * groups) + [HBM] * shares + [VMEM],
         [
             w_scratch,
             pltpu.VMEM((tokens, width), BF16),
@@ -445,18 +449,18 @@
         ],
         flops=2 * tokens * width * wide * 3,
         moved=20 << 20,
-    )(*near, *kept, *far, *weights)
-    grads, mod_t = main[0], main[1]
-
-    far_hidden, near_hidden = call(
+    )(*near, *kept, *far, *weights, modulation)
+    grads, mod_t, normed = main[:3]
+
+    far_hidden, near_hidden, sums = call(
         functools.partial(hidden_kernel, shares),
         "grad_hidden",
-        [shape((groups, clips, chunk, width))] * 2,
-        [VMEM] + [HBM] * shares,
+        [shape((groups, clips, chunk, width))] * 2 + [shape((clips, 2, width), F32)],
+        [VMEM] * 2 + [HBM] * shares,
         [w_scratch, pltpu.VMEM((tokens // 2, wide), BF16), pltpu.SemaphoreType.DMA((shares,))],
         flops=2 * tokens * width * wide,
         moved=8 << 20,
-    )(grads, *weights)
+    )(grads, normed, *weights)
 
     def meet(came):
         back = call(
@@ -468,7 +472,7 @@
         return call(
             functools.partial(input_kernel, groups),
             "grad_input",
-            [shape((clips, positions, width)), shape((clips, 2, width), F32)],
+            shape((clips, positions, width)),
             [VMEM] * (2 + groups),
             moved=2 << 20,
         )(hidden, modulation, *back)
@@ -493,7 +497,11 @@
         def total(*terms):
             return call(add_kernel, "sum_z", shape(terms[0].shape), [VMEM] * len(terms))(*terms)
 
-        core_a, core_b = (over_space(main[2 + p], 1) for p in range(2))
+        core_a = over_space(main[3], 1)
+        other_b = call(
+            functools.partial(other_kernel, share, cuts[1]), "grad_w_other", other_rows[1], [VMEM] * 2
+        )(mod_t, grads)
+        core_b = over_space(other_b, 1)
         x_a = over_space(own(0, 1, core_a, BF16), 2)
         x_b = over_space(own(1, 1, core_b, BF16), 2)
         mine = [own(0, 0, core_a, F32), own(1, 0, core_b, F32)]
@@ -505,31 +513,30 @@
         own_a, send_a = fold(keep_a, next_a)
         over_a = over_z(send_a, 2)
         back = meet(came)
-        x_b, over_a, back[1] = together(x_b, over_a, back[1])
+        x_b, over_a = together(x_b, over_a)
         keep_b, send_b = spread(1, mine[1], x_b)
         next_b = over_z(send_b, 1)
-        next_b, back[2], back[3] = together(next_b, back[2], back[3])
         sum_a = total(own_a, over_a)
+        a2, a1, b0 = over_z(sum_a, 2), over_z(sum_a, 1), over_y(sum_a)
         own_b, send_b = fold(keep_b, next_b)
-        grad_input, sums = finish(back)
         over_b = over_z(send_b, 2)
-        a2, a1 = over_z(sum_a, 2), over_z(sum_a, 1)
-        sums = sums + over_space(sums, 1)
-        got = over_space(sums, 2)
-        over_b, a2, a1, got = together(over_b, a2, a1, got)
+        a2 = after(a2, own_b)
+        a3 = over_z(a2, 1)
+        sums = sums + over_space(after(sums, own_b), 1)
+        more = over_space(sums, 2)
+        over_b, a3, a1, b0, more = together(over_b, a3, a1, b0, more)
         sum_b = call(
             carry_kernel,
             "sum_z",
             shape((rows + 4 * 2 * clips, own_b.shape[1])),
             [VMEM] * 4,
-        )(own_b, over_b, sums, got)
-        a3 = over_z(a2, 1)
+        )(own_b, over_b, sums, more)
         c2, c1, d0 = over_z(sum_b, 2), over_z(sum_b, 1), over_y(sum_b)
-        early = call(stack_kernel, "stack", shape((groups - 1, *sum_a.shape)), [VMEM] * (groups - 1))(sum_a, a1, a2)
+        early = call(stack_kernel, "stack", shape((groups - 1, *sum_a.shape)), [VMEM] * (groups - 1))(a1, a2, a3)
         early = over_y(early)
-        a3, c2, c1, d0, early = together(a3, c2, c1, d0, early)
-        b3, c3, d1, d2 = over_y(a3), over_z(c2, 1), over_y(c1), over_y(c2)
-        c3, b3 = together(c3, b3)
+        c2, c1, d0, early = together(c2, c1, d0, early)
+        c3, d1, d2 = over_z(c2, 1), over_y(c1), over_y(c2)
+        grad_input = finish(back)
         d3 = over_y(c3)
         grad_weight, sums = call(
             functools.partial(weight_kernel, grad_scale_factor),
@@ -537,9 +544,9 @@
             [shape((share, 2 * wide), F32), shape((clips, 2, width), F32)],
             [VMEM] * (2 + 3 * groups),
             [pltpu.VMEM((frames, 2 * clips, width), F32)],
-        )(sum_a, a1, a2, a3, early, b3, sum_b, c1, c2, c3, d0, d1, d2, d3)
+        )(sum_a, a1, a2, a3, early, b0, sum_b, c1, c2, c3, d0, d1, d2, d3)
     else:
-        grad_input, sums = finish(meet(over_y(far_hidden)))
+        grad_input = finish(meet(over_y(far_hidden)))
         step = 1
         while step < spaces:
             sums += over_space(sums, step)

time: 152 us -> 143 us (0.941)
  waiting for transfers between devices: 72.6 us -> 66 us
  starting transfers between devices: 50.7 us -> 48.3 us
    ppermute x19, waiting for transfers between devices: 41 us -> 34.1 us  [over_z(): return lax.ppermute(x, 'frame', [(i, i ^ 2 * step) for i in range(frames)])]
    ppermute x19, starting transfers between devices: 29.7 us -> 27.2 us  [over_z(): return lax.ppermute(x, 'frame', [(i, i ^ 2 * step) for i in range(frames)])]
  transfers between devices with their start and end apart: 39 -> 39, of which waited for: 19 -> 17; matrix products, arithmetic and copies ran while one was open for 0% -> 0% of each run, Pallas kernels for 5% -> 7%
where the time goes in v4:
time: 143 us; the launch traced here: 142 us
  waiting for transfers between devices  66 us (46%)
  starting transfers between devices  48.3 us (34%)
  Pallas kernels  27 us (19%)
    ppermute x19, waiting for transfers between devices, over_z(): return lax.ppermute(x, 'frame', [(i, i ^ 2 * step) for i in range(frames)])  34.1 us
    ppermute x19, starting transfers between devices, over_z(): return lax.ppermute(x, 'frame', [(i, i ^ 2 * step) for i in range(frames)])  27.2 us
    ppermute x11, waiting for transfers between devices, over_y(): return lax.ppermute(x, 'frame', [(i, i ^ 1) for i in range(frames)])  19.7 us
    ppermute x11, starting transfers between devices, over_y(): return lax.ppermute(x, 'frame', [(i, i ^ 1) for i in range(frames)])  14.3 us
    ppermute x9, waiting for transfers between devices, over_space(): return lax.ppermute(x, 'space', [(i, i ^ step) for i in range(spaces)])  12.2 us
    pallas_call x1, Pallas kernels, per_device(): call(functools.partial(main_kernel, groups, shares, cuts), 'attend', outs...  11.2 us
    ppermute x9, starting transfers between devices, over_space(): return lax.ppermute(x, 'space', [(i, i ^ step) for i in range(spaces)])  6.86 us
    pallas_call x1, Pallas kernels, per_device(): call(functools.partial(hidden_kernel, shares), 'grad_hidden', [shape((gro...  4.26 us
  transfers between devices with their start and end apart: 39, of which 17 were waited for; matrix products, arithmetic and copies ran while one was open for 0% of the time, Pallas kernels for 7%

profile of v4, /device:TPU:0, one launch (start us, length us, event | category | flops | bytes accessed | tf_op | source)
XLA Modules:
  0.0 142.3 jit_solution(14787719631842452172)
XLA Ops:
  0.6 2.2 %lookup.1.refs_16_.mod_ref = f32[2,3,1152]{2,1,0:T(4,128)} custom-call(bf16[1000,2,1152]{2,1,0:T(2,128)(2,1)} %tab_ref.1, s32[2]{0:T(128)} %ts_ref.1, f32[1000]{0:T(1024)} %snr_ref.1, s32[2]{0:T(128)} %wi_ref.1), custom_call_target="tpu_custom_call" | custom-call | bytes 1048576 | tf_op jit(solution)/shard_map/lookup/pallas_call | solution.py:394
  3.1 3.0 %collective-permute-start.11 = (bf16[288,1728]{1,0:T(8,128)(2,1)S(1)}, bf16[288,1728]{1,0:T(8,128)(2,1)S(1)}, u32[]{:S(2)}, u32[]{:S(2)}) collective-permute-start(bf16[288,1728]{1,0:T(8,128)(2,1)S(1)} %w_half.1.refs_12_.refs_0_), channel_id=1, source_target_pairs={{0,2},{1,3},{2,0},{3,1},{4,6},{5,7},{6,4},{7,5},{8,10},{9,11},{10,... | collective-permute-start | bytes 2985992 | tf_op jit(solution)/shard_map/ppermute | solution.py:383
  10.9 2.6 %collective-permute-start.2 = (bf16[2,32,1728]{2,1,0:T(8,128)(2,1)S(1)}, bf16[2,32,1728]{2,1,0:T(8,128)(2,1)S(1)}, u32[]{:S(2)}, u32[]{:S(2)}) collective-permute-start(bf16[2,32,1728]{2,1,0:T(8,128)(2,1)S(1)} %get-tuple-element.58), channel_id=1, source_target_pairs={{0,16},{4,20},{8,24},{12,28},{16,0},{20,4},{24,8},{28,12},{1,17},{... | collective-permute-start | bytes 663560 | tf_op jit(solution)/shard_map/ppermute | solution.py:389
  13.5 4.5 %collective-permute-done.refs_1_ = bf16[2,32,1728]{2,1,0:T(8,128)(2,1)S(1)} collective-permute-done((bf16[2,32,1728]{2,1,0:T(8,128)(2,1)S(1)}, bf16[2,32,1728]{2,1,0:T(8,128)(2,1)S(1)}, u32[]{:S(2)}, u32[]{:S(2)}) %collective-permute-start) | collective-permute-done | bytes 221216 | tf_op jit(solution)/shard_map/ppermute | solution.py:389
  18.0 3.0 %collective-permute-start.3 = (bf16[2,32,1728]{2,1,0:T(8,128)(2,1)S(1)}, bf16[2,32,1728]{2,1,0:T(8,128)(2,1)S(1)}, u32[]{:S(2)}, u32[]{:S(2)}) collective-permute-start(bf16[2,32,1728]{2,1,0:T(8,128)(2,1)S(1)} %collective-permute-done.refs_1_), channel_id=1, source_target_pairs={{0,4},{4,0},{8,12},{12,8},{16,20},{20,16},{24,28},{28,24},{1,5},{5... | collective-permute-start | bytes 663560 | tf_op jit(solution)/shard_map/ppermute | solution.py:386
  21.0 2.5 %collective-permute-start.4 = (bf16[2,32,1728]{2,1,0:T(8,128)(2,1)S(1)}, bf16[2,32,1728]{2,1,0:T(8,128)(2,1)S(1)}, u32[]{:S(2)}, u32[]{:S(2)}) collective-permute-start(bf16[2,32,1728]{2,1,0:T(8,128)(2,1)S(1)} %get-tuple-element.60), channel_id=1, source_target_pairs={{0,24},{4,28},{8,16},{12,20},{16,8},{20,12},{24,0},{28,4},{1,25},{... | collective-permute-start | bytes 663560 | tf_op jit(solution)/shard_map/ppermute | solution.py:389
  23.5 6.0 %collective-permute-done.2.refs_2_ = bf16[2,32,1728]{2,1,0:T(8,128)(2,1)S(1)} collective-permute-done((bf16[2,32,1728]{2,1,0:T(8,128)(2,1)S(1)}, bf16[2,32,1728]{2,1,0:T(8,128)(2,1)S(1)}, u32[]{:S(2)}, u32[]{:S(2)}) %collective-permute-start.2) | collective-permute-done | bytes 221216 | tf_op jit(solution)/shard_map/ppermute | solution.py:389
  29.6 6.0 %collective-permute-done.5.refs_10_ = bf16[2,32,1728]{2,1,0:T(8,128)(2,1)S(1)} collective-permute-done((bf16[2,32,1728]{2,1,0:T(8,128)(2,1)S(1)}, bf16[2,32,1728]{2,1,0:T(8,128)(2,1)S(1)}, u32[]{:S(2)}, u32[]{:S(2)}) %collective-permute-start.5) | collective-permute-done | bytes 221216 | tf_op jit(solution)/shard_map/ppermute | solution.py:386
  35.6 3.3 %collective-permute-start.7 = (bf16[2,32,576]{2,1,0:T(8,128)(2,1)S(1)}, bf16[2,32,576]{2,1,0:T(8,128)(2,1)S(1)}, u32[]{:S(2)}, u32[]{:S(2)}) collective-permute-start(bf16[2,32,576]{2,1,0:T(8,128)(2,1)S(1)} %get-tuple-element.64), channel_id=1, source_target_pairs={{0,16},{4,20},{8,24},{12,28},{16,0},{20,4},{24,8},{28,12},{1,17},{... | collective-permute-start | bytes 221192 | tf_op jit(solution)/shard_map/ppermute | solution.py:389
  38.9 3.0 %collective-permute-done.6.refs_5_ = bf16[2,32,576]{2,1,0:T(8,128)(2,1)S(1)} collective-permute-done((bf16[2,32,576]{2,1,0:T(8,128)(2,1)S(1)}, bf16[2,32,576]{2,1,0:T(8,128)(2,1)S(1)}, u32[]{:S(2)}, u32[]{:S(2)}) %collective-permute-start.6) | collective-permute-done | bytes 73760 | tf_op jit(solution)/shard_map/ppermute | solution.py:389
  41.9 2.3 %collective-permute-start.8 = (bf16[2,32,576]{2,1,0:T(8,128)(2,1)S(1)}, bf16[2,32,576]{2,1,0:T(8,128)(2,1)S(1)}, u32[]{:S(2)}, u32[]{:S(2)}) collective-permute-start(bf16[2,32,576]{2,1,0:T(8,128)(2,1)S(1)} %get-tuple-element.65), channel_id=1, source_target_pairs={{0,24},{4,28},{8,16},{12,20},{16,8},{20,12},{24,0},{28,4},{1,25},{... | collective-permute-start | bytes 221192 | tf_op jit(solution)/shard_map/ppermute | solution.py:389
  44.3 3.9 %collective-permute-done.8.refs_7_ = bf16[2,32,576]{2,1,0:T(8,128)(2,1)S(1)} collective-permute-done((bf16[2,32,576]{2,1,0:T(8,128)(2,1)S(1)}, bf16[2,32,576]{2,1,0:T(8,128)(2,1)S(1)}, u32[]{:S(2)}, u32[]{:S(2)}) %collective-permute-start.8) | collective-permute-done | bytes 73760 | tf_op jit(solution)/shard_map/ppermute | solution.py:389
  48.2 11.2 %attend.1 = (bf16[512,1728]{1,0:T(8,128)(2,1)S(1)}, bf16[1152,512]{1,0:T(8,128)(2,1)S(1)}, bf16[512,1152]{1,0:T(8,128)(2,1)S(1)}, bf16[2,4,72,896]{3,2,1,0:T(8,128)(2,1)S(1)}) custom-call(bf16[2,32,1728]{2,1,0:T(8,128)(2,1)S(1)} %get-tuple-element.55.refs_0_, bf16[2,32,1728]{2,1,0:T(8,128)(2,1)S(1)} %collective-permute-done.refs_1_, ...), custom_call_target="tpu_custom_call" | custom-call | flops 6115295232 | bytes 20971520 | tf_op jit(solution)/shard_map/attend/pallas_call | solution.py:433
  63.6 4.3 %grad_hidden.1 = (bf16[4,2,32,1152]{3,2,1,0:T(8,128)(2,1)S(1)}, bf16[4,2,32,1152]{3,2,1,0:T(8,128)(2,1)S(1)}, f32[2,2,1152]{2,1,0:T(2,128)S(1)}) custom-call(bf16[512,1728]{1,0:T(8,128)(2,1)S(1)} %get-tuple-element.67.grads, bf16[512,1152]{1,0:T(8,128)(2,1)S(1)} %get-tuple-element.68.normed, bf16[288,1728]{1,0:T(8,128)(2,1)S(1)} %w_half.1.refs_12_.refs_0_, ...), custom_call_target="tpu_custom_call" | custom-call | flops 2038431744 | bytes 8388608 | tf_op jit(solution)/shard_map/grad_hidden/pallas_call | solution.py:455
  67.8 1.9 %collective-permute-start.16 = (bf16[4,2,32,1152]{3,2,1,0:T(8,128)(2,1)S(1)}, bf16[4,2,32,1152]{3,2,1,0:T(8,128)(2,1)S(1)}, u32[]{:S(2)}, u32[]{:S(2)}) collective-permute-start(bf16[4,2,32,1152]{3,2,1,0:T(8,128)(2,1)S(1)} %get-tuple-element.73), channel_id=1, source_target_pairs={{0,4},{4,0},{8,12},{12,8},{16,20},{20,16},{24,28},{28,24},{1,5},{5... | collective-permute-start | bytes 1769480 | tf_op jit(solution)/shard_map/ppermute | solution.py:386
  71.8 5.5 %collective-permute-done.14.got = bf16[4,72,896]{2,1,0:T(8,128)(2,1)S(1)} collective-permute-done((bf16[4,72,896]{2,1,0:T(8,128)(2,1)S(1)}, bf16[4,72,896]{2,1,0:T(8,128)(2,1)S(1)}, u32[]{:S(2)}, u32[]{:S(2)}) %collective-permute-start.14) | collective-permute-done | bytes 516128 | tf_op jit(solution)/shard_map/ppermute | solution.py:383
  77.4 5.7 %collective-permute-done.16.got = bf16[4,2,32,1152]{3,2,1,0:T(8,128)(2,1)S(1)} collective-permute-done((bf16[4,2,32,1152]{3,2,1,0:T(8,128)(2,1)S(1)}, bf16[4,2,32,1152]{3,2,1,0:T(8,128)(2,1)S(1)}, u32[]{:S(2)}, u32[]{:S(2)}) %collective-permute-start.16) | collective-permute-done | bytes 589856 | tf_op jit(solution)/shard_map/ppermute | solution.py:386
  87.5 3.7 %collective-permute-done.22.refs_1_ = bf16[72,896]{1,0:T(8,128)(2,1)S(1)} collective-permute-done((bf16[72,896]{1,0:T(8,128)(2,1)S(1)}, bf16[72,896]{1,0:T(8,128)(2,1)S(1)}, u32[]{:S(2)}, u32[]{:S(2)}) %collective-permute-start.22) | collective-permute-done | bytes 129056 | tf_op jit(solution)/shard_map/ppermute | solution.py:389
  91.4 3.0 %collective-permute-start.25 = (bf16[72,896]{1,0:T(8,128)(2,1)S(1)}, bf16[72,896]{1,0:T(8,128)(2,1)S(1)}, u32[]{:S(2)}, u32[]{:S(2)}) collective-permute-start(bf16[72,896]{1,0:T(8,128)(2,1)S(1)} %sum_z.2.refs_0_), channel_id=1, source_target_pairs={{0,16},{4,20},{8,24},{12,28},{16,0},{20,4},{24,8},{28,12},{1,17},{... | collective-permute-start | bytes 387080 | tf_op jit(solution)/shard_map/ppermute | solution.py:389
  94.4 1.7 %collective-permute-start.28 = (bf16[72,896]{1,0:T(8,128)(2,1)S(1)}, bf16[72,896]{1,0:T(8,128)(2,1)S(1)}, u32[]{:S(2)}, u32[]{:S(2)}) collective-permute-start(bf16[72,896]{1,0:T(8,128)(2,1)S(1)} %sum_z.2.refs_0_), channel_id=1, source_target_pairs={{0,4},{4,0},{8,12},{12,8},{16,20},{20,16},{24,28},{28,24},{1,5},{5... | collective-permute-start | bytes 387080 | tf_op jit(solution)/shard_map/ppermute | solution.py:386
  96.1 7.1 %collective-permute-done.23.got = bf16[2,72,832]{2,1,0:T(8,128)(2,1)S(1)} collective-permute-done((bf16[2,72,832]{2,1,0:T(8,128)(2,1)S(1)}, bf16[2,72,832]{2,1,0:T(8,128)(2,1)S(1)}, u32[]{:S(2)}, u32[]{:S(2)}) %collective-permute-start.23) | collective-permute-done | bytes 239648 | tf_op jit(solution)/shard_map/ppermute | solution.py:389
  103.4 2.9 %collective-permute-start.24 = (bf16[72,832]{1,0:T(8,128)(2,1)S(1)}, bf16[72,832]{1,0:T(8,128)(2,1)S(1)}, u32[]{:S(2)}, u32[]{:S(2)}) collective-permute-start(bf16[72,832]{1,0:T(8,128)(2,1)S(1)} %get-tuple-element.87), channel_id=1, source_target_pairs={{0,16},{4,20},{8,24},{12,28},{16,0},{20,4},{24,8},{28,12},{1,17},{... | collective-permute-start | bytes 359432 | tf_op jit(solution)/shard_map/ppermute | solution.py:389
  108.7 2.6 %collective-permute-done.30.more = f32[2,2,1152]{2,1,0:T(2,128)S(1)} collective-permute-done((f32[2,2,1152]{2,1,0:T(2,128)S(1)}, f32[2,2,1152]{2,1,0:T(2,128)S(1)}, u32[]{:S(2)}, u32[]{:S(2)}) %collective-permute-start.30) | collective-permute-done | bytes 18464 | tf_op jit(solution)/shard_map/ppermute | solution.py:383
  111.4 1.8 %collective-permute-start.34 = (bf16[3,72,896]{2,1,0:T(8,128)(2,1)S(1)}, bf16[3,72,896]{2,1,0:T(8,128)(2,1)S(1)}, u32[]{:S(2)}, u32[]{:S(2)}) collective-permute-start(bf16[3,72,896]{2,1,0:T(8,128)(2,1)S(1)} %stack.1), channel_id=1, source_target_pairs={{0,4},{4,0},{8,12},{12,8},{16,20},{20,16},{24,28},{28,24},{1,5},{5... | collective-permute-start | bytes 1161224 | tf_op jit(solution)/shard_map/ppermute | solution.py:386
  113.7 1.9 %collective-permute-start.31 = (bf16[88,832]{1,0:T(8,128)(2,1)S(1)}, bf16[88,832]{1,0:T(8,128)(2,1)S(1)}, u32[]{:S(2)}, u32[]{:S(2)}) collective-permute-start(bf16[88,832]{1,0:T(8,128)(2,1)S(1)} %sum_z.3.refs_6_), channel_id=1, source_target_pairs={{0,16},{4,20},{8,24},{12,28},{16,0},{20,4},{24,8},{28,12},{1,17},{... | collective-permute-start | bytes 439304 | tf_op jit(solution)/shard_map/ppermute | solution.py:389
  116.7 8.0 %collective-permute-done.33.refs_10_ = bf16[88,832]{1,0:T(8,128)(2,1)S(1)} collective-permute-done((bf16[88,832]{1,0:T(8,128)(2,1)S(1)}, bf16[88,832]{1,0:T(8,128)(2,1)S(1)}, u32[]{:S(2)}, u32[]{:S(2)}) %collective-permute-start.33) | collective-permute-done | bytes 146464 | tf_op jit(solution)/shard_map/ppermute | solution.py:386
  125.2 1.9 %collective-permute-start.18 = (bf16[2,32,1152]{2,1,0:T(8,128)(2,1)S(1)}, bf16[2,32,1152]{2,1,0:T(8,128)(2,1)S(1)}, u32[]{:S(2)}, u32[]{:S(2)}) collective-permute-start(bf16[2,32,1152]{2,1,0:T(8,128)(2,1)S(1)} %get-tuple-element.77), channel_id=1, source_target_pairs={{0,16},{4,20},{8,24},{12,28},{16,0},{20,4},{24,8},{28,12},{1,17},{... | collective-permute-start | bytes 442376 | tf_op jit(solution)/shard_map/ppermute | solution.py:389
  127.2 2.1 %collective-permute-start.19 = (bf16[2,32,1152]{2,1,0:T(8,128)(2,1)S(1)}, bf16[2,32,1152]{2,1,0:T(8,128)(2,1)S(1)}, u32[]{:S(2)}, u32[]{:S(2)}) collective-permute-start(bf16[2,32,1152]{2,1,0:T(8,128)(2,1)S(1)} %get-tuple-element.78), channel_id=1, source_target_pairs={{0,24},{4,28},{8,16},{12,20},{16,8},{20,12},{24,0},{28,4},{1,25},{... | collective-permute-start | bytes 442376 | tf_op jit(solution)/shard_map/ppermute | solution.py:389
  129.2 1.7 %collective-permute-start.37 = (bf16[88,832]{1,0:T(8,128)(2,1)S(1)}, bf16[88,832]{1,0:T(8,128)(2,1)S(1)}, u32[]{:S(2)}, u32[]{:S(2)}) collective-permute-start(bf16[88,832]{1,0:T(8,128)(2,1)S(1)} %collective-permute-done.31.refs_8_), channel_id=1, source_target_pairs={{0,4},{4,0},{8,12},{12,8},{16,20},{20,16},{24,28},{28,24},{1,5},{5... | collective-permute-start | bytes 439304 | tf_op jit(solution)/shard_map/ppermute | solution.py:386
  131.9 1.8 %collective-permute-start.38 = (bf16[88,832]{1,0:T(8,128)(2,1)S(1)}, bf16[88,832]{1,0:T(8,128)(2,1)S(1)}, u32[]{:S(2)}, u32[]{:S(2)}) collective-permute-start(bf16[88,832]{1,0:T(8,128)(2,1)S(1)} %collective-permute-done.35.refs_9_), channel_id=1, source_target_pairs={{0,4},{4,0},{8,12},{12,8},{16,20},{20,16},{24,28},{28,24},{1,5},{5... | collective-permute-start | bytes 439304 | tf_op jit(solution)/shard_map/ppermute | solution.py:386
  133.7 4.2 %collective-permute-done.18.refs_2_ = bf16[2,32,1152]{2,1,0:T(8,128)(2,1)S(1)} collective-permute-done((bf16[2,32,1152]{2,1,0:T(8,128)(2,1)S(1)}, bf16[2,32,1152]{2,1,0:T(8,128)(2,1)S(1)}, u32[]{:S(2)}, u32[]{:S(2)}) %collective-permute-start.18) | collective-permute-done | bytes 147488 | tf_op jit(solution)/shard_map/ppermute | solution.py:389
  139.5 2.8 %grad_w.1 = (f32[288,3456]{1,0:T(8,128)}, f32[2,2,1152]{2,1,0:T(2,128)}) custom-call(bf16[72,896]{1,0:T(8,128)(2,1)S(1)} %sum_z.2.refs_0_, bf16[72,896]{1,0:T(8,128)(2,1)S(1)} %collective-permute-done.27.refs_0_.refs_1_, bf16[72,896]{1,0:T(8,128)(2,1)S(1)} %collective-permute-done.25.refs_1_.refs_2_, ...), custom_call_target="tpu_custom_call" | custom-call | bytes 1048576 | tf_op jit(solution)/shard_map/grad_w/pallas_call | solution.py:541
  (75 shorter events, 23.1 us)
Async XLA Ops:
  3.1 32.5 %collective-permute-start.11 = (bf16[288,1728]{1,0:T(8,128)(2,1)S(1)}, bf16[288,1728]{1,0:T(8,128)(2,1)S(1)}, u32[]{:S(2)}, u32[]{:S(2)}) collective-permute-start(bf16[288,1728]{1,0:T(8,128)(2,1)S(1)} %w_half.1.refs_12_.refs_0_), channel_id=1, source_target_pairs={{0,2},{1,3},{2,0},{3,1},{4,6},{5,7},{6,4},{7,5},{8,10},{9,11},{10,... | collective-permute-start | bytes 2985992 | tf_op jit(solution)/shard_map/ppermute | solution.py:383
  7.6 10.4 %collective-permute-start = (bf16[2,32,1728]{2,1,0:T(8,128)(2,1)S(1)}, bf16[2,32,1728]{2,1,0:T(8,128)(2,1)S(1)}, u32[]{:S(2)}, u32[]{:S(2)}) collective-permute-start(bf16[2,32,1728]{2,1,0:T(8,128)(2,1)S(1)} %get-tuple-element.56), channel_id=1, source_target_pairs={{0,8},{4,12},{8,0},{12,4},{16,24},{20,28},{24,16},{28,20},{1,9},{5... | collective-permute-start | bytes 663560 | tf_op jit(solution)/shard_map/ppermute | solution.py:389
  9.3 8.7 %collective-permute-start.1 = (bf16[2,32,1728]{2,1,0:T(8,128)(2,1)S(1)}, bf16[2,32,1728]{2,1,0:T(8,128)(2,1)S(1)}, u32[]{:S(2)}, u32[]{:S(2)}) collective-permute-start(bf16[2,32,1728]{2,1,0:T(8,128)(2,1)S(1)} %get-tuple-element.55.refs_0_), channel_id=1, source_target_pairs={{0,4},{4,0},{8,12},{12,8},{16,20},{20,16},{24,28},{28,24},{1,5},{5... | collective-permute-start | bytes 663560 | tf_op jit(solution)/shard_map/ppermute | solution.py:386
  10.9 18.7 %collective-permute-start.2 = (bf16[2,32,1728]{2,1,0:T(8,128)(2,1)S(1)}, bf16[2,32,1728]{2,1,0:T(8,128)(2,1)S(1)}, u32[]{:S(2)}, u32[]{:S(2)}) collective-permute-start(bf16[2,32,1728]{2,1,0:T(8,128)(2,1)S(1)} %get-tuple-element.58), channel_id=1, source_target_pairs={{0,16},{4,20},{8,24},{12,28},{16,0},{20,4},{24,8},{28,12},{1,17},{... | collective-permute-start | bytes 663560 | tf_op jit(solution)/shard_map/ppermute | solution.py:389
  18.0 11.6 %collective-permute-start.3 = (bf16[2,32,1728]{2,1,0:T(8,128)(2,1)S(1)}, bf16[2,32,1728]{2,1,0:T(8,128)(2,1)S(1)}, u32[]{:S(2)}, u32[]{:S(2)}) collective-permute-start(bf16[2,32,1728]{2,1,0:T(8,128)(2,1)S(1)} %collective-permute-done.refs_1_), channel_id=1, source_target_pairs={{0,4},{4,0},{8,12},{12,8},{16,20},{20,16},{24,28},{28,24},{1,5},{5... | collective-permute-start | bytes 663560 | tf_op jit(solution)/shard_map/ppermute | solution.py:386
  21.0 8.5 %collective-permute-start.4 = (bf16[2,32,1728]{2,1,0:T(8,128)(2,1)S(1)}, bf16[2,32,1728]{2,1,0:T(8,128)(2,1)S(1)}, u32[]{:S(2)}, u32[]{:S(2)}) collective-permute-start(bf16[2,32,1728]{2,1,0:T(8,128)(2,1)S(1)} %get-tuple-element.60), channel_id=1, source_target_pairs={{0,24},{4,28},{8,16},{12,20},{16,8},{20,12},{24,0},{28,4},{1,25},{... | collective-permute-start | bytes 663560 | tf_op jit(solution)/shard_map/ppermute | solution.py:389
  29.5 18.7 %collective-permute-start.10 = (bf16[288,1728]{1,0:T(8,128)(2,1)S(1)}, bf16[288,1728]{1,0:T(8,128)(2,1)S(1)}, u32[]{:S(2)}, u32[]{:S(2)}) collective-permute-start(bf16[288,1728]{1,0:T(8,128)(2,1)S(1)} %w_half.1.refs_12_.refs_0_), channel_id=1, source_target_pairs={{0,1},{1,0},{2,3},{3,2},{4,5},{5,4},{6,7},{7,6},{8,9},{9,8},{10,11... | collective-permute-start | bytes 2985992 | tf_op jit(solution)/shard_map/ppermute | solution.py:383
  35.6 12.6 %collective-permute-start.12 = (bf16[288,1728]{1,0:T(8,128)(2,1)S(1)}, bf16[288,1728]{1,0:T(8,128)(2,1)S(1)}, u32[]{:S(2)}, u32[]{:S(2)}) collective-permute-start(bf16[288,1728]{1,0:T(8,128)(2,1)S(1)} %collective-permute-done.11.refs_14_.refs_2_), channel_id=1, source_target_pairs={{0,1},{1,0},{2,3},{3,2},{4,5},{5,4},{6,7},{7,6},{8,9},{9,8},{10,11... | collective-permute-start | bytes 2985992 | tf_op jit(solution)/shard_map/ppermute | solution.py:383
  35.6 12.6 %collective-permute-start.9 = (bf16[2,32,1728]{2,1,0:T(8,128)(2,1)S(1)}, bf16[2,32,1728]{2,1,0:T(8,128)(2,1)S(1)}, u32[]{:S(2)}, u32[]{:S(2)}) collective-permute-start(bf16[2,32,1728]{2,1,0:T(8,128)(2,1)S(1)} %collective-permute-done.4.refs_3_), channel_id=1, source_target_pairs={{0,4},{4,0},{8,12},{12,8},{16,20},{20,16},{24,28},{28,24},{1,5},{5... | collective-permute-start | bytes 663560 | tf_op jit(solution)/shard_map/ppermute | solution.py:386
  35.6 8.6 %collective-permute-start.7 = (bf16[2,32,576]{2,1,0:T(8,128)(2,1)S(1)}, bf16[2,32,576]{2,1,0:T(8,128)(2,1)S(1)}, u32[]{:S(2)}, u32[]{:S(2)}) collective-permute-start(bf16[2,32,576]{2,1,0:T(8,128)(2,1)S(1)} %get-tuple-element.64), channel_id=1, source_target_pairs={{0,16},{4,20},{8,24},{12,28},{16,0},{20,4},{24,8},{28,12},{1,17},{... | collective-permute-start | bytes 221192 | tf_op jit(solution)/shard_map/ppermute | solution.py:389
  60.3 9.5 %collective-permute-start.20 = (bf16[2,4,72,832]{3,2,1,0:T(8,128)(2,1)S(1)}, bf16[2,4,72,832]{3,2,1,0:T(8,128)(2,1)S(1)}, u32[]{:S(2)}, u32[]{:S(2)}) collective-permute-start(bf16[2,4,72,832]{3,2,1,0:T(8,128)(2,1)S(1)} %grad_w_other.1), channel_id=1, source_target_pairs={{0,1},{1,0},{2,3},{3,2},{4,5},{5,4},{6,7},{7,6},{8,9},{9,8},{10,11... | collective-permute-start | bytes 2875400 | tf_op jit(solution)/shard_map/ppermute | solution.py:383
  62.6 14.7 %collective-permute-start.14 = (bf16[4,72,896]{2,1,0:T(8,128)(2,1)S(1)}, bf16[4,72,896]{2,1,0:T(8,128)(2,1)S(1)}, u32[]{:S(2)}, u32[]{:S(2)}) collective-permute-start(bf16[4,72,896]{2,1,0:T(8,128)(2,1)S(1)} %grad_w_rows.5), channel_id=1, source_target_pairs={{0,2},{1,3},{2,0},{3,1},{4,6},{5,7},{6,4},{7,5},{8,10},{9,11},{10,... | collective-permute-start | bytes 1548296 | tf_op jit(solution)/shard_map/ppermute | solution.py:383
  67.8 15.3 %collective-permute-start.16 = (bf16[4,2,32,1152]{3,2,1,0:T(8,128)(2,1)S(1)}, bf16[4,2,32,1152]{3,2,1,0:T(8,128)(2,1)S(1)}, u32[]{:S(2)}, u32[]{:S(2)}) collective-permute-start(bf16[4,2,32,1152]{3,2,1,0:T(8,128)(2,1)S(1)} %get-tuple-element.73), channel_id=1, source_target_pairs={{0,4},{4,0},{8,12},{12,8},{16,20},{20,16},{24,28},{28,24},{1,5},{5... | collective-permute-start | bytes 1769480 | tf_op jit(solution)/shard_map/ppermute | solution.py:386
  70.3 17.2 %collective-permute-start.21 = (bf16[4,72,832]{2,1,0:T(8,128)(2,1)S(1)}, bf16[4,72,832]{2,1,0:T(8,128)(2,1)S(1)}, u32[]{:S(2)}, u32[]{:S(2)}) collective-permute-start(bf16[4,72,832]{2,1,0:T(8,128)(2,1)S(1)} %grad_w_rows.6), channel_id=1, source_target_pairs={{0,2},{1,3},{2,0},{3,1},{4,6},{5,7},{6,4},{7,5},{8,10},{9,11},{10,... | collective-permute-start | bytes 1437704 | tf_op jit(solution)/shard_map/ppermute | solution.py:383
  84.1 7.0 %collective-permute-start.22 = (bf16[72,896]{1,0:T(8,128)(2,1)S(1)}, bf16[72,896]{1,0:T(8,128)(2,1)S(1)}, u32[]{:S(2)}, u32[]{:S(2)}) collective-permute-start(bf16[72,896]{1,0:T(8,128)(2,1)S(1)} %get-tuple-element.82), channel_id=1, source_target_pairs={{0,16},{4,20},{8,24},{12,28},{16,0},{20,4},{24,8},{28,12},{1,17},{... | collective-permute-start | bytes 387080 | tf_op jit(solution)/shard_map/ppermute | solution.py:389
  91.3 12.0 %collective-permute-start.23 = (bf16[2,72,832]{2,1,0:T(8,128)(2,1)S(1)}, bf16[2,72,832]{2,1,0:T(8,128)(2,1)S(1)}, u32[]{:S(2)}, u32[]{:S(2)}) collective-permute-start(bf16[2,72,832]{2,1,0:T(8,128)(2,1)S(1)} %get-tuple-element.86), channel_id=1, source_target_pairs={{0,8},{4,12},{8,0},{12,4},{16,24},{20,28},{24,16},{28,20},{1,9},{5... | collective-permute-start | bytes 718856 | tf_op jit(solution)/shard_map/ppermute | solution.py:389
  91.4 11.9 %collective-permute-start.25 = (bf16[72,896]{1,0:T(8,128)(2,1)S(1)}, bf16[72,896]{1,0:T(8,128)(2,1)S(1)}, u32[]{:S(2)}, u32[]{:S(2)}) collective-permute-start(bf16[72,896]{1,0:T(8,128)(2,1)S(1)} %sum_z.2.refs_0_), channel_id=1, source_target_pairs={{0,16},{4,20},{8,24},{12,28},{16,0},{20,4},{24,8},{28,12},{1,17},{... | collective-permute-start | bytes 387080 | tf_op jit(solution)/shard_map/ppermute | solution.py:389
  94.4 14.3 %collective-permute-start.28 = (bf16[72,896]{1,0:T(8,128)(2,1)S(1)}, bf16[72,896]{1,0:T(8,128)(2,1)S(1)}, u32[]{:S(2)}, u32[]{:S(2)}) collective-permute-start(bf16[72,896]{1,0:T(8,128)(2,1)S(1)} %sum_z.2.refs_0_), channel_id=1, source_target_pairs={{0,4},{4,0},{8,12},{12,8},{16,20},{20,16},{24,28},{28,24},{1,5},{5... | collective-permute-start | bytes 387080 | tf_op jit(solution)/shard_map/ppermute | solution.py:386
  96.1 12.6 %collective-permute-start.27 = (bf16[72,896]{1,0:T(8,128)(2,1)S(1)}, bf16[72,896]{1,0:T(8,128)(2,1)S(1)}, u32[]{:S(2)}, u32[]{:S(2)}) collective-permute-start(bf16[72,896]{1,0:T(8,128)(2,1)S(1)} %sum_z.2.refs_0_), channel_id=1, source_target_pairs={{0,8},{4,12},{8,0},{12,4},{16,24},{20,28},{24,16},{28,20},{1,9},{5... | collective-permute-start | bytes 387080 | tf_op jit(solution)/shard_map/ppermute | solution.py:389
  103.3 8.0 %collective-permute-start.26 = (bf16[72,896]{1,0:T(8,128)(2,1)S(1)}, bf16[72,896]{1,0:T(8,128)(2,1)S(1)}, u32[]{:S(2)}, u32[]{:S(2)}) collective-permute-start(bf16[72,896]{1,0:T(8,128)(2,1)S(1)} %collective-permute-done.25.refs_1_.refs_2_), channel_id=1, source_target_pairs={{0,8},{4,12},{8,0},{12,4},{16,24},{20,28},{24,16},{28,20},{1,9},{5... | collective-permute-start | bytes 387080 | tf_op jit(solution)/shard_map/ppermute | solution.py:389
  103.4 8.0 %collective-permute-start.24 = (bf16[72,832]{1,0:T(8,128)(2,1)S(1)}, bf16[72,832]{1,0:T(8,128)(2,1)S(1)}, u32[]{:S(2)}, u32[]{:S(2)}) collective-permute-start(bf16[72,832]{1,0:T(8,128)(2,1)S(1)} %get-tuple-element.87), channel_id=1, source_target_pairs={{0,16},{4,20},{8,24},{12,28},{16,0},{20,4},{24,8},{28,12},{1,17},{... | collective-permute-start | bytes 359432 | tf_op jit(solution)/shard_map/ppermute | solution.py:389
  111.4 13.4 %collective-permute-start.34 = (bf16[3,72,896]{2,1,0:T(8,128)(2,1)S(1)}, bf16[3,72,896]{2,1,0:T(8,128)(2,1)S(1)}, u32[]{:S(2)}, u32[]{:S(2)}) collective-permute-start(bf16[3,72,896]{2,1,0:T(8,128)(2,1)S(1)} %stack.1), channel_id=1, source_target_pairs={{0,4},{4,0},{8,12},{12,8},{16,20},{20,16},{24,28},{28,24},{1,5},{5... | collective-permute-start | bytes 1161224 | tf_op jit(solution)/shard_map/ppermute | solution.py:386
  113.3 11.5 %collective-permute-start.33 = (bf16[88,832]{1,0:T(8,128)(2,1)S(1)}, bf16[88,832]{1,0:T(8,128)(2,1)S(1)}, u32[]{:S(2)}, u32[]{:S(2)}) collective-permute-start(bf16[88,832]{1,0:T(8,128)(2,1)S(1)} %sum_z.3.refs_6_), channel_id=1, source_target_pairs={{0,4},{4,0},{8,12},{12,8},{16,20},{20,16},{24,28},{28,24},{1,5},{5... | collective-permute-start | bytes 439304 | tf_op jit(solution)/shard_map/ppermute | solution.py:386
  113.6 11.1 %collective-permute-start.32 = (bf16[88,832]{1,0:T(8,128)(2,1)S(1)}, bf16[88,832]{1,0:T(8,128)(2,1)S(1)}, u32[]{:S(2)}, u32[]{:S(2)}) collective-permute-start(bf16[88,832]{1,0:T(8,128)(2,1)S(1)} %sum_z.3.refs_6_), channel_id=1, source_target_pairs={{0,8},{4,12},{8,0},{12,4},{16,24},{20,28},{24,16},{28,20},{1,9},{5... | collective-permute-start | bytes 439304 | tf_op jit(solution)/shard_map/ppermute | solution.py:389
  113.7 11.1 %collective-permute-start.31 = (bf16[88,832]{1,0:T(8,128)(2,1)S(1)}, bf16[88,832]{1,0:T(8,128)(2,1)S(1)}, u32[]{:S(2)}, u32[]{:S(2)}) collective-permute-start(bf16[88,832]{1,0:T(8,128)(2,1)S(1)} %sum_z.3.refs_6_), channel_id=1, source_target_pairs={{0,16},{4,20},{8,24},{12,28},{16,0},{20,4},{24,8},{28,12},{1,17},{... | collective-permute-start | bytes 439304 | tf_op jit(solution)/shard_map/ppermute | solution.py:389
  115.8 15.2 %collective-permute-start.17 = (bf16[2,32,1152]{2,1,0:T(8,128)(2,1)S(1)}, bf16[2,32,1152]{2,1,0:T(8,128)(2,1)S(1)}, u32[]{:S(2)}, u32[]{:S(2)}) collective-permute-start(bf16[2,32,1152]{2,1,0:T(8,128)(2,1)S(1)} %get-tuple-element.76), channel_id=1, source_target_pairs={{0,8},{4,12},{8,0},{12,4},{16,24},{20,28},{24,16},{28,20},{1,9},{5... | collective-permute-start | bytes 442376 | tf_op jit(solution)/shard_map/ppermute | solution.py:389
  124.8 7.1 %collective-permute-start.35 = (bf16[88,832]{1,0:T(8,128)(2,1)S(1)}, bf16[88,832]{1,0:T(8,128)(2,1)S(1)}, u32[]{:S(2)}, u32[]{:S(2)}) collective-permute-start(bf16[88,832]{1,0:T(8,128)(2,1)S(1)} %collective-permute-done.31.refs_8_), channel_id=1, source_target_pairs={{0,8},{4,12},{8,0},{12,4},{16,24},{20,28},{24,16},{28,20},{1,9},{5... | collective-permute-start | bytes 439304 | tf_op jit(solution)/shard_map/ppermute | solution.py:389
  125.2 12.7 %collective-permute-start.18 = (bf16[2,32,1152]{2,1,0:T(8,128)(2,1)S(1)}, bf16[2,32,1152]{2,1,0:T(8,128)(2,1)S(1)}, u32[]{:S(2)}, u32[]{:S(2)}) collective-permute-start(bf16[2,32,1152]{2,1,0:T(8,128)(2,1)S(1)} %get-tuple-element.77), channel_id=1, source_target_pairs={{0,16},{4,20},{8,24},{12,28},{16,0},{20,4},{24,8},{28,12},{1,17},{... | collective-permute-start | bytes 442376 | tf_op jit(solution)/shard_map/ppermute | solution.py:389
  127.2 10.7 %collective-permute-start.19 = (bf16[2,32,1152]{2,1,0:T(8,128)(2,1)S(1)}, bf16[2,32,1152]{2,1,0:T(8,128)(2,1)S(1)}, u32[]{:S(2)}, u32[]{:S(2)}) collective-permute-start(bf16[2,32,1152]{2,1,0:T(8,128)(2,1)S(1)} %get-tuple-element.78), channel_id=1, source_target_pairs={{0,24},{4,28},{8,16},{12,20},{16,8},{20,12},{24,0},{28,4},{1,25},{... | collective-permute-start | bytes 442376 | tf_op jit(solution)/shard_map/ppermute | solution.py:389
  129.2 10.2 %collective-permute-start.37 = (bf16[88,832]{1,0:T(8,128)(2,1)S(1)}, bf16[88,832]{1,0:T(8,128)(2,1)S(1)}, u32[]{:S(2)}, u32[]{:S(2)}) collective-permute-start(bf16[88,832]{1,0:T(8,128)(2,1)S(1)} %collective-permute-done.31.refs_8_), channel_id=1, source_target_pairs={{0,4},{4,0},{8,12},{12,8},{16,20},{20,16},{24,28},{28,24},{1,5},{5... | collective-permute-start | bytes 439304 | tf_op jit(solution)/shard_map/ppermute | solution.py:386
  131.0 8.5 %collective-permute-start.36 = (bf16[88,832]{1,0:T(8,128)(2,1)S(1)}, bf16[88,832]{1,0:T(8,128)(2,1)S(1)}, u32[]{:S(2)}, u32[]{:S(2)}) collective-permute-start(bf16[88,832]{1,0:T(8,128)(2,1)S(1)} %collective-permute-done.32.refs_7_), channel_id=1, source_target_pairs={{0,4},{4,0},{8,12},{12,8},{16,20},{20,16},{24,28},{28,24},{1,5},{5... | collective-permute-start | bytes 439304 | tf_op jit(solution)/shard_map/ppermute | solution.py:386
  131.9 7.6 %collective-permute-start.38 = (bf16[88,832]{1,0:T(8,128)(2,1)S(1)}, bf16[88,832]{1,0:T(8,128)(2,1)S(1)}, u32[]{:S(2)}, u32[]{:S(2)}) collective-permute-start(bf16[88,832]{1,0:T(8,128)(2,1)S(1)} %collective-permute-done.35.refs_9_), channel_id=1, source_target_pairs={{0,4},{4,0},{8,12},{12,8},{16,20},{20,16},{24,28},{28,24},{1,5},{5... | collective-permute-start | bytes 439304 | tf_op jit(solution)/shard_map/ppermute | solution.py:386
  (11 other events, 87.0 us)

commit v5 on v4

--- a/solution.py
+++ b/solution.py
@@ -534,7 +534,7 @@
         c2, c1, d0 = over_z(sum_b, 2), over_z(sum_b, 1), over_y(sum_b)
         early = call(stack_kernel, "stack", shape((groups - 1, *sum_a.shape)), [VMEM] * (groups - 1))(a1, a2, a3)
         early = over_y(early)
-        c2, c1, d0, early = together(c2, c1, d0, early)
+        d0, c1, c2 = together(d0, c1, c2)
         c3, d1, d2 = over_z(c2, 1), over_y(c1), over_y(c2)
         grad_input = finish(back)
         d3 = over_y(c3)

time: 143 us -> 142 us (level)
    ppermute x11, waiting for transfers between devices: 19.7 us -> 13.6 us  [over_y(): return lax.ppermute(x, 'frame', [(i, i ^ 1) for i in range(frames)])]
    ppermute x19, waiting for transfers between devices: 34.1 us -> 39.6 us  [over_z(): return lax.ppermute(x, 'frame', [(i, i ^ 2 * step) for i in range(frames)])]
    ppermute x19, starting transfers between devices: 27.2 us -> 25.7 us  [over_z(): return lax.ppermute(x, 'frame', [(i, i ^ 2 * step) for i in range(frames)])]
  transfers between devices with their start and end apart: 39 -> 39, of which waited for: 17 -> 20; matrix products, arithmetic and copies ran while one was open for 0% -> 0% of each run, Pallas kernels for 7% -> 7%
where the time goes in v5:
time: 142 us
  waiting for transfers between devices  65.5 us (46%)
  starting transfers between devices  48.2 us (34%)
  Pallas kernels  27 us (19%)
    ppermute x19, waiting for transfers between devices, over_z(): return lax.ppermute(x, 'frame', [(i, i ^ 2 * step) for i in range(frames)])  39.6 us
    ppermute x19, starting transfers between devices, over_z(): return lax.ppermute(x, 'frame', [(i, i ^ 2 * step) for i in range(frames)])  25.7 us
    ppermute x11, starting transfers between devices, over_y(): return lax.ppermute(x, 'frame', [(i, i ^ 1) for i in range(frames)])  15.7 us
    ppermute x11, waiting for transfers between devices, over_y(): return lax.ppermute(x, 'frame', [(i, i ^ 1) for i in range(frames)])  13.6 us
    ppermute x9, waiting for transfers between devices, over_space(): return lax.ppermute(x, 'space', [(i, i ^ step) for i in range(spaces)])  12.2 us
    pallas_call x1, Pallas kernels, per_device(): call(functools.partial(main_kernel, groups, shares, cuts), 'attend', outs...  11.2 us
    ppermute x9, starting transfers between devices, over_space(): return lax.ppermute(x, 'space', [(i, i ^ step) for i in range(spaces)])  6.86 us
    pallas_call x1, Pallas kernels, per_device(): call(functools.partial(hidden_kernel, shares), 'grad_hidden', [shape((gro...  4.26 us
  transfers between devices with their start and end apart: 39, of which 20 were waited for; matrix products, arithmetic and copies ran while one was open for 0% of the time, Pallas kernels for 7%

profile of v5, /device:TPU:0, one launch (start us, length us, event | category | flops | bytes accessed | tf_op | source)
XLA Modules:
  0.0 141.7 jit_solution(229836327922979698)
XLA Ops:
  0.6 2.2 %lookup.1.refs_16_.mod_ref = f32[2,3,1152]{2,1,0:T(4,128)} custom-call(bf16[1000,2,1152]{2,1,0:T(2,128)(2,1)} %tab_ref.1, s32[2]{0:T(128)} %ts_ref.1, f32[1000]{0:T(1024)} %snr_ref.1, s32[2]{0:T(128)} %wi_ref.1), custom_call_target="tpu_custom_call" | custom-call | bytes 1048576 | tf_op jit(solution)/shard_map/lookup/pallas_call | solution.py:394
  3.1 3.0 %collective-permute-start.11 = (bf16[288,1728]{1,0:T(8,128)(2,1)S(1)}, bf16[288,1728]{1,0:T(8,128)(2,1)S(1)}, u32[]{:S(2)}, u32[]{:S(2)}) collective-permute-start(bf16[288,1728]{1,0:T(8,128)(2,1)S(1)} %w_half.1.refs_12_.refs_0_), channel_id=1, source_target_pairs={{0,2},{1,3},{2,0},{3,1},{4,6},{5,7},{6,4},{7,5},{8,10},{9,11},{10,... | collective-permute-start | bytes 2985992 | tf_op jit(solution)/shard_map/ppermute | solution.py:383
  10.9 2.6 %collective-permute-start.2 = (bf16[2,32,1728]{2,1,0:T(8,128)(2,1)S(1)}, bf16[2,32,1728]{2,1,0:T(8,128)(2,1)S(1)}, u32[]{:S(2)}, u32[]{:S(2)}) collective-permute-start(bf16[2,32,1728]{2,1,0:T(8,128)(2,1)S(1)} %get-tuple-element.57), channel_id=1, source_target_pairs={{0,16},{4,20},{8,24},{12,28},{16,0},{20,4},{24,8},{28,12},{1,17},{... | collective-permute-start | bytes 663560 | tf_op jit(solution)/shard_map/ppermute | solution.py:389
  13.5 4.5 %collective-permute-done.refs_1_ = bf16[2,32,1728]{2,1,0:T(8,128)(2,1)S(1)} collective-permute-done((bf16[2,32,1728]{2,1,0:T(8,128)(2,1)S(1)}, bf16[2,32,1728]{2,1,0:T(8,128)(2,1)S(1)}, u32[]{:S(2)}, u32[]{:S(2)}) %collective-permute-start) | collective-permute-done | bytes 221216 | tf_op jit(solution)/shard_map/ppermute | solution.py:389
  18.0 3.0 %collective-permute-start.3 = (bf16[2,32,1728]{2,1,0:T(8,128)(2,1)S(1)}, bf16[2,32,1728]{2,1,0:T(8,128)(2,1)S(1)}, u32[]{:S(2)}, u32[]{:S(2)}) collective-permute-start(bf16[2,32,1728]{2,1,0:T(8,128)(2,1)S(1)} %collective-permute-done.refs_1_), channel_id=1, source_target_pairs={{0,4},{4,0},{8,12},{12,8},{16,20},{20,16},{24,28},{28,24},{1,5},{5... | collective-permute-start | bytes 663560 | tf_op jit(solution)/shard_map/ppermute | solution.py:386
  21.0 2.5 %collective-permute-start.4 = (bf16[2,32,1728]{2,1,0:T(8,128)(2,1)S(1)}, bf16[2,32,1728]{2,1,0:T(8,128)(2,1)S(1)}, u32[]{:S(2)}, u32[]{:S(2)}) collective-permute-start(bf16[2,32,1728]{2,1,0:T(8,128)(2,1)S(1)} %get-tuple-element.59), channel_id=1, source_target_pairs={{0,24},{4,28},{8,16},{12,20},{16,8},{20,12},{24,0},{28,4},{1,25},{... | collective-permute-start | bytes 663560 | tf_op jit(solution)/shard_map/ppermute | solution.py:389
  23.5 6.0 %collective-permute-done.2.refs_2_ = bf16[2,32,1728]{2,1,0:T(8,128)(2,1)S(1)} collective-permute-done((bf16[2,32,1728]{2,1,0:T(8,128)(2,1)S(1)}, bf16[2,32,1728]{2,1,0:T(8,128)(2,1)S(1)}, u32[]{:S(2)}, u32[]{:S(2)}) %collective-permute-start.2) | collective-permute-done | bytes 221216 | tf_op jit(solution)/shard_map/ppermute | solution.py:389
  29.6 6.0 %collective-permute-done.5.refs_10_ = bf16[2,32,1728]{2,1,0:T(8,128)(2,1)S(1)} collective-permute-done((bf16[2,32,1728]{2,1,0:T(8,128)(2,1)S(1)}, bf16[2,32,1728]{2,1,0:T(8,128)(2,1)S(1)}, u32[]{:S(2)}, u32[]{:S(2)}) %collective-permute-start.5) | collective-permute-done | bytes 221216 | tf_op jit(solution)/shard_map/ppermute | solution.py:386
  35.6 3.3 %collective-permute-start.7 = (bf16[2,32,576]{2,1,0:T(8,128)(2,1)S(1)}, bf16[2,32,576]{2,1,0:T(8,128)(2,1)S(1)}, u32[]{:S(2)}, u32[]{:S(2)}) collective-permute-start(bf16[2,32,576]{2,1,0:T(8,128)(2,1)S(1)} %get-tuple-element.63), channel_id=1, source_target_pairs={{0,16},{4,20},{8,24},{12,28},{16,0},{20,4},{24,8},{28,12},{1,17},{... | collective-permute-start | bytes 221192 | tf_op jit(solution)/shard_map/ppermute | solution.py:389
  38.9 3.0 %collective-permute-done.6.refs_5_ = bf16[2,32,576]{2,1,0:T(8,128)(2,1)S(1)} collective-permute-done((bf16[2,32,576]{2,1,0:T(8,128)(2,1)S(1)}, bf16[2,32,576]{2,1,0:T(8,128)(2,1)S(1)}, u32[]{:S(2)}, u32[]{:S(2)}) %collective-permute-start.6) | collective-permute-done | bytes 73760 | tf_op jit(solution)/shard_map/ppermute | solution.py:389
  41.9 2.3 %collective-permute-start.8 = (bf16[2,32,576]{2,1,0:T(8,128)(2,1)S(1)}, bf16[2,32,576]{2,1,0:T(8,128)(2,1)S(1)}, u32[]{:S(2)}, u32[]{:S(2)}) collective-permute-start(bf16[2,32,576]{2,1,0:T(8,128)(2,1)S(1)} %get-tuple-element.64), channel_id=1, source_target_pairs={{0,24},{4,28},{8,16},{12,20},{16,8},{20,12},{24,0},{28,4},{1,25},{... | collective-permute-start | bytes 221192 | tf_op jit(solution)/shard_map/ppermute | solution.py:389
  44.3 3.9 %collective-permute-done.8.refs_7_ = bf16[2,32,576]{2,1,0:T(8,128)(2,1)S(1)} collective-permute-done((bf16[2,32,576]{2,1,0:T(8,128)(2,1)S(1)}, bf16[2,32,576]{2,1,0:T(8,128)(2,1)S(1)}, u32[]{:S(2)}, u32[]{:S(2)}) %collective-permute-start.8) | collective-permute-done | bytes 73760 | tf_op jit(solution)/shard_map/ppermute | solution.py:389
  48.2 11.2 %attend.1 = (bf16[512,1728]{1,0:T(8,128)(2,1)S(1)}, bf16[1152,512]{1,0:T(8,128)(2,1)S(1)}, bf16[512,1152]{1,0:T(8,128)(2,1)S(1)}, bf16[2,4,72,896]{3,2,1,0:T(8,128)(2,1)S(1)}) custom-call(bf16[2,32,1728]{2,1,0:T(8,128)(2,1)S(1)} %get-tuple-element.54.refs_0_, bf16[2,32,1728]{2,1,0:T(8,128)(2,1)S(1)} %collective-permute-done.refs_1_, ...), custom_call_target="tpu_custom_call" | custom-call | flops 6115295232 | bytes 20971520 | tf_op jit(solution)/shard_map/attend/pallas_call | solution.py:433
  63.6 4.3 %grad_hidden.1 = (bf16[4,2,32,1152]{3,2,1,0:T(8,128)(2,1)S(1)}, bf16[4,2,32,1152]{3,2,1,0:T(8,128)(2,1)S(1)}, f32[2,2,1152]{2,1,0:T(2,128)S(1)}) custom-call(bf16[512,1728]{1,0:T(8,128)(2,1)S(1)} %get-tuple-element.66.grads, bf16[512,1152]{1,0:T(8,128)(2,1)S(1)} %get-tuple-element.67.normed, bf16[288,1728]{1,0:T(8,128)(2,1)S(1)} %w_half.1.refs_12_.refs_0_, ...), custom_call_target="tpu_custom_call" | custom-call | flops 2038431744 | bytes 8388608 | tf_op jit(solution)/shard_map/grad_hidden/pallas_call | solution.py:455
  67.8 1.9 %collective-permute-start.16 = (bf16[4,2,32,1152]{3,2,1,0:T(8,128)(2,1)S(1)}, bf16[4,2,32,1152]{3,2,1,0:T(8,128)(2,1)S(1)}, u32[]{:S(2)}, u32[]{:S(2)}) collective-permute-start(bf16[4,2,32,1152]{3,2,1,0:T(8,128)(2,1)S(1)} %get-tuple-element.72), channel_id=1, source_target_pairs={{0,4},{4,0},{8,12},{12,8},{16,20},{20,16},{24,28},{28,24},{1,5},{5... | collective-permute-start | bytes 1769480 | tf_op jit(solution)/shard_map/ppermute | solution.py:386
  71.8 5.5 %collective-permute-done.14.got = bf16[4,72,896]{2,1,0:T(8,128)(2,1)S(1)} collective-permute-done((bf16[4,72,896]{2,1,0:T(8,128)(2,1)S(1)}, bf16[4,72,896]{2,1,0:T(8,128)(2,1)S(1)}, u32[]{:S(2)}, u32[]{:S(2)}) %collective-permute-start.14) | collective-permute-done | bytes 516128 | tf_op jit(solution)/shard_map/ppermute | solution.py:383
  77.4 5.7 %collective-permute-done.16.got = bf16[4,2,32,1152]{3,2,1,0:T(8,128)(2,1)S(1)} collective-permute-done((bf16[4,2,32,1152]{3,2,1,0:T(8,128)(2,1)S(1)}, bf16[4,2,32,1152]{3,2,1,0:T(8,128)(2,1)S(1)}, u32[]{:S(2)}, u32[]{:S(2)}) %collective-permute-start.16) | collective-permute-done | bytes 589856 | tf_op jit(solution)/shard_map/ppermute | solution.py:386
  87.5 3.7 %collective-permute-done.22.refs_1_ = bf16[72,896]{1,0:T(8,128)(2,1)S(1)} collective-permute-done((bf16[72,896]{1,0:T(8,128)(2,1)S(1)}, bf16[72,896]{1,0:T(8,128)(2,1)S(1)}, u32[]{:S(2)}, u32[]{:S(2)}) %collective-permute-start.22) | collective-permute-done | bytes 129056 | tf_op jit(solution)/shard_map/ppermute | solution.py:389
  91.4 3.0 %collective-permute-start.25 = (bf16[72,896]{1,0:T(8,128)(2,1)S(1)}, bf16[72,896]{1,0:T(8,128)(2,1)S(1)}, u32[]{:S(2)}, u32[]{:S(2)}) collective-permute-start(bf16[72,896]{1,0:T(8,128)(2,1)S(1)} %sum_z.2.refs_0_), channel_id=1, source_target_pairs={{0,16},{4,20},{8,24},{12,28},{16,0},{20,4},{24,8},{28,12},{1,17},{... | collective-permute-start | bytes 387080 | tf_op jit(solution)/shard_map/ppermute | solution.py:389
  94.4 1.7 %collective-permute-start.28 = (bf16[72,896]{1,0:T(8,128)(2,1)S(1)}, bf16[72,896]{1,0:T(8,128)(2,1)S(1)}, u32[]{:S(2)}, u32[]{:S(2)}) collective-permute-start(bf16[72,896]{1,0:T(8,128)(2,1)S(1)} %sum_z.2.refs_0_), channel_id=1, source_target_pairs={{0,4},{4,0},{8,12},{12,8},{16,20},{20,16},{24,28},{28,24},{1,5},{5... | collective-permute-start | bytes 387080 | tf_op jit(solution)/shard_map/ppermute | solution.py:386
  96.1 7.1 %collective-permute-done.23.got = bf16[2,72,832]{2,1,0:T(8,128)(2,1)S(1)} collective-permute-done((bf16[2,72,832]{2,1,0:T(8,128)(2,1)S(1)}, bf16[2,72,832]{2,1,0:T(8,128)(2,1)S(1)}, u32[]{:S(2)}, u32[]{:S(2)}) %collective-permute-start.23) | collective-permute-done | bytes 239648 | tf_op jit(solution)/shard_map/ppermute | solution.py:389
  103.4 2.9 %collective-permute-start.24 = (bf16[72,832]{1,0:T(8,128)(2,1)S(1)}, bf16[72,832]{1,0:T(8,128)(2,1)S(1)}, u32[]{:S(2)}, u32[]{:S(2)}) collective-permute-start(bf16[72,832]{1,0:T(8,128)(2,1)S(1)} %get-tuple-element.86), channel_id=1, source_target_pairs={{0,16},{4,20},{8,24},{12,28},{16,0},{20,4},{24,8},{28,12},{1,17},{... | collective-permute-start | bytes 359432 | tf_op jit(solution)/shard_map/ppermute | solution.py:389
  108.7 2.6 %collective-permute-done.30.more = f32[2,2,1152]{2,1,0:T(2,128)S(1)} collective-permute-done((f32[2,2,1152]{2,1,0:T(2,128)S(1)}, f32[2,2,1152]{2,1,0:T(2,128)S(1)}, u32[]{:S(2)}, u32[]{:S(2)}) %collective-permute-start.30) | collective-permute-done | bytes 18464 | tf_op jit(solution)/shard_map/ppermute | solution.py:383
  113.5 1.7 %collective-permute-start.32 = (bf16[88,832]{1,0:T(8,128)(2,1)S(1)}, bf16[88,832]{1,0:T(8,128)(2,1)S(1)}, u32[]{:S(2)}, u32[]{:S(2)}) collective-permute-start(bf16[88,832]{1,0:T(8,128)(2,1)S(1)} %sum_z.3.refs_6_), channel_id=1, source_target_pairs={{0,4},{4,0},{8,12},{12,8},{16,20},{20,16},{24,28},{28,24},{1,5},{5... | collective-permute-start | bytes 439304 | tf_op jit(solution)/shard_map/ppermute | solution.py:386
  116.7 4.0 %collective-permute-done.34.refs_8_ = bf16[88,832]{1,0:T(8,128)(2,1)S(1)} collective-permute-done((bf16[88,832]{1,0:T(8,128)(2,1)S(1)}, bf16[88,832]{1,0:T(8,128)(2,1)S(1)}, u32[]{:S(2)}, u32[]{:S(2)}) %collective-permute-start.34) | collective-permute-done | bytes 146464 | tf_op jit(solution)/shard_map/ppermute | solution.py:389
  122.6 2.5 %collective-permute-start.19 = (bf16[2,32,1152]{2,1,0:T(8,128)(2,1)S(1)}, bf16[2,32,1152]{2,1,0:T(8,128)(2,1)S(1)}, u32[]{:S(2)}, u32[]{:S(2)}) collective-permute-start(bf16[2,32,1152]{2,1,0:T(8,128)(2,1)S(1)} %get-tuple-element.77), channel_id=1, source_target_pairs={{0,24},{4,28},{8,16},{12,20},{16,8},{20,12},{24,0},{28,4},{1,25},{... | collective-permute-start | bytes 442376 | tf_op jit(solution)/shard_map/ppermute | solution.py:389
  125.2 1.7 %collective-permute-start.36 = (bf16[88,832]{1,0:T(8,128)(2,1)S(1)}, bf16[88,832]{1,0:T(8,128)(2,1)S(1)}, u32[]{:S(2)}, u32[]{:S(2)}) collective-permute-start(bf16[88,832]{1,0:T(8,128)(2,1)S(1)} %collective-permute-done.33.refs_7_), channel_id=1, source_target_pairs={{0,4},{4,0},{8,12},{12,8},{16,20},{20,16},{24,28},{28,24},{1,5},{5... | collective-permute-start | bytes 439304 | tf_op jit(solution)/shard_map/ppermute | solution.py:386
  126.9 4.4 %collective-permute-done.18.refs_2_ = bf16[2,32,1152]{2,1,0:T(8,128)(2,1)S(1)} collective-permute-done((bf16[2,32,1152]{2,1,0:T(8,128)(2,1)S(1)}, bf16[2,32,1152]{2,1,0:T(8,128)(2,1)S(1)}, u32[]{:S(2)}, u32[]{:S(2)}) %collective-permute-start.18) | collective-permute-done | bytes 147488 | tf_op jit(solution)/shard_map/ppermute | solution.py:389
  131.3 1.7 %collective-permute-start.37 = (bf16[88,832]{1,0:T(8,128)(2,1)S(1)}, bf16[88,832]{1,0:T(8,128)(2,1)S(1)}, u32[]{:S(2)}, u32[]{:S(2)}) collective-permute-start(bf16[88,832]{1,0:T(8,128)(2,1)S(1)} %collective-permute-done.34.refs_8_), channel_id=1, source_target_pairs={{0,4},{4,0},{8,12},{12,8},{16,20},{20,16},{24,28},{28,24},{1,5},{5... | collective-permute-start | bytes 439304 | tf_op jit(solution)/shard_map/ppermute | solution.py:386
  133.6 1.7 %collective-permute-start.38 = (bf16[88,832]{1,0:T(8,128)(2,1)S(1)}, bf16[88,832]{1,0:T(8,128)(2,1)S(1)}, u32[]{:S(2)}, u32[]{:S(2)}) collective-permute-start(bf16[88,832]{1,0:T(8,128)(2,1)S(1)} %collective-permute-done.35.refs_9_), channel_id=1, source_target_pairs={{0,4},{4,0},{8,12},{12,8},{16,20},{20,16},{24,28},{28,24},{1,5},{5... | collective-permute-start | bytes 439304 | tf_op jit(solution)/shard_map/ppermute | solution.py:386
  137.0 1.9 %collective-permute-done.38.refs_13_ = bf16[88,832]{1,0:T(8,128)(2,1)S(1)} collective-permute-done((bf16[88,832]{1,0:T(8,128)(2,1)S(1)}, bf16[88,832]{1,0:T(8,128)(2,1)S(1)}, u32[]{:S(2)}, u32[]{:S(2)}) %collective-permute-start.38) | collective-permute-done | bytes 146464 | tf_op jit(solution)/shard_map/ppermute | solution.py:386
  138.9 2.8 %grad_w.1 = (f32[288,3456]{1,0:T(8,128)}, f32[2,2,1152]{2,1,0:T(2,128)}) custom-call(bf16[72,896]{1,0:T(8,128)(2,1)S(1)} %sum_z.2.refs_0_, bf16[72,896]{1,0:T(8,128)(2,1)S(1)} %collective-permute-done.27.refs_0_.refs_1_, bf16[72,896]{1,0:T(8,128)(2,1)S(1)} %collective-permute-done.25.refs_1_.refs_2_, ...), custom_call_target="tpu_custom_call" | custom-call | bytes 1048576 | tf_op jit(solution)/shard_map/grad_w/pallas_call | solution.py:541
  (75 shorter events, 26.2 us)
Async XLA Ops:
  3.1 32.5 %collective-permute-start.11 = (bf16[288,1728]{1,0:T(8,128)(2,1)S(1)}, bf16[288,1728]{1,0:T(8,128)(2,1)S(1)}, u32[]{:S(2)}, u32[]{:S(2)}) collective-permute-start(bf16[288,1728]{1,0:T(8,128)(2,1)S(1)} %w_half.1.refs_12_.refs_0_), channel_id=1, source_target_pairs={{0,2},{1,3},{2,0},{3,1},{4,6},{5,7},{6,4},{7,5},{8,10},{9,11},{10,... | collective-permute-start | bytes 2985992 | tf_op jit(solution)/shard_map/ppermute | solution.py:383
  7.6 10.4 %collective-permute-start = (bf16[2,32,1728]{2,1,0:T(8,128)(2,1)S(1)}, bf16[2,32,1728]{2,1,0:T(8,128)(2,1)S(1)}, u32[]{:S(2)}, u32[]{:S(2)}) collective-permute-start(bf16[2,32,1728]{2,1,0:T(8,128)(2,1)S(1)} %get-tuple-element.55), channel_id=1, source_target_pairs={{0,8},{4,12},{8,0},{12,4},{16,24},{20,28},{24,16},{28,20},{1,9},{5... | collective-permute-start | bytes 663560 | tf_op jit(solution)/shard_map/ppermute | solution.py:389
  9.3 8.7 %collective-permute-start.1 = (bf16[2,32,1728]{2,1,0:T(8,128)(2,1)S(1)}, bf16[2,32,1728]{2,1,0:T(8,128)(2,1)S(1)}, u32[]{:S(2)}, u32[]{:S(2)}) collective-permute-start(bf16[2,32,1728]{2,1,0:T(8,128)(2,1)S(1)} %get-tuple-element.54.refs_0_), channel_id=1, source_target_pairs={{0,4},{4,0},{8,12},{12,8},{16,20},{20,16},{24,28},{28,24},{1,5},{5... | collective-permute-start | bytes 663560 | tf_op jit(solution)/shard_map/ppermute | solution.py:386
  10.9 18.7 %collective-permute-start.2 = (bf16[2,32,1728]{2,1,0:T(8,128)(2,1)S(1)}, bf16[2,32,1728]{2,1,0:T(8,128)(2,1)S(1)}, u32[]{:S(2)}, u32[]{:S(2)}) collective-permute-start(bf16[2,32,1728]{2,1,0:T(8,128)(2,1)S(1)} %get-tuple-element.57), channel_id=1, source_target_pairs={{0,16},{4,20},{8,24},{12,28},{16,0},{20,4},{24,8},{28,12},{1,17},{... | collective-permute-start | bytes 663560 | tf_op jit(solution)/shard_map/ppermute | solution.py:389
  18.0 11.6 %collective-permute-start.3 = (bf16[2,32,1728]{2,1,0:T(8,128)(2,1)S(1)}, bf16[2,32,1728]{2,1,0:T(8,128)(2,1)S(1)}, u32[]{:S(2)}, u32[]{:S(2)}) collective-permute-start(bf16[2,32,1728]{2,1,0:T(8,128)(2,1)S(1)} %collective-permute-done.refs_1_), channel_id=1, source_target_pairs={{0,4},{4,0},{8,12},{12,8},{16,20},{20,16},{24,28},{28,24},{1,5},{5... | collective-permute-start | bytes 663560 | tf_op jit(solution)/shard_map/ppermute | solution.py:386
  21.0 8.5 %collective-permute-start.4 = (bf16[2,32,1728]{2,1,0:T(8,128)(2,1)S(1)}, bf16[2,32,1728]{2,1,0:T(8,128)(2,1)S(1)}, u32[]{:S(2)}, u32[]{:S(2)}) collective-permute-start(bf16[2,32,1728]{2,1,0:T(8,128)(2,1)S(1)} %get-tuple-element.59), channel_id=1, source_target_pairs={{0,24},{4,28},{8,16},{12,20},{16,8},{20,12},{24,0},{28,4},{1,25},{... | collective-permute-start | bytes 663560 | tf_op jit(solution)/shard_map/ppermute | solution.py:389
  29.5 18.7 %collective-permute-start.10 = (bf16[288,1728]{1,0:T(8,128)(2,1)S(1)}, bf16[288,1728]{1,0:T(8,128)(2,1)S(1)}, u32[]{:S(2)}, u32[]{:S(2)}) collective-permute-start(bf16[288,1728]{1,0:T(8,128)(2,1)S(1)} %w_half.1.refs_12_.refs_0_), channel_id=1, source_target_pairs={{0,1},{1,0},{2,3},{3,2},{4,5},{5,4},{6,7},{7,6},{8,9},{9,8},{10,11... | collective-permute-start | bytes 2985992 | tf_op jit(solution)/shard_map/ppermute | solution.py:383
  35.6 12.6 %collective-permute-start.12 = (bf16[288,1728]{1,0:T(8,128)(2,1)S(1)}, bf16[288,1728]{1,0:T(8,128)(2,1)S(1)}, u32[]{:S(2)}, u32[]{:S(2)}) collective-permute-start(bf16[288,1728]{1,0:T(8,128)(2,1)S(1)} %collective-permute-done.11.refs_14_.refs_2_), channel_id=1, source_target_pairs={{0,1},{1,0},{2,3},{3,2},{4,5},{5,4},{6,7},{7,6},{8,9},{9,8},{10,11... | collective-permute-start | bytes 2985992 | tf_op jit(solution)/shard_map/ppermute | solution.py:383
  35.6 12.6 %collective-permute-start.9 = (bf16[2,32,1728]{2,1,0:T(8,128)(2,1)S(1)}, bf16[2,32,1728]{2,1,0:T(8,128)(2,1)S(1)}, u32[]{:S(2)}, u32[]{:S(2)}) collective-permute-start(bf16[2,32,1728]{2,1,0:T(8,128)(2,1)S(1)} %collective-permute-done.4.refs_3_), channel_id=1, source_target_pairs={{0,4},{4,0},{8,12},{12,8},{16,20},{20,16},{24,28},{28,24},{1,5},{5... | collective-permute-start | bytes 663560 | tf_op jit(solution)/shard_map/ppermute | solution.py:386
  35.6 6.4 %collective-permute-start.6 = (bf16[2,32,576]{2,1,0:T(8,128)(2,1)S(1)}, bf16[2,32,576]{2,1,0:T(8,128)(2,1)S(1)}, u32[]{:S(2)}, u32[]{:S(2)}) collective-permute-start(bf16[2,32,576]{2,1,0:T(8,128)(2,1)S(1)} %get-tuple-element.62), channel_id=1, source_target_pairs={{0,8},{4,12},{8,0},{12,4},{16,24},{20,28},{24,16},{28,20},{1,9},{5... | collective-permute-start | bytes 221192 | tf_op jit(solution)/shard_map/ppermute | solution.py:389
  35.6 8.6 %collective-permute-start.7 = (bf16[2,32,576]{2,1,0:T(8,128)(2,1)S(1)}, bf16[2,32,576]{2,1,0:T(8,128)(2,1)S(1)}, u32[]{:S(2)}, u32[]{:S(2)}) collective-permute-start(bf16[2,32,576]{2,1,0:T(8,128)(2,1)S(1)} %get-tuple-element.63), channel_id=1, source_target_pairs={{0,16},{4,20},{8,24},{12,28},{16,0},{20,4},{24,8},{28,12},{1,17},{... | collective-permute-start | bytes 221192 | tf_op jit(solution)/shard_map/ppermute | solution.py:389
  60.3 9.5 %collective-permute-start.20 = (bf16[2,4,72,832]{3,2,1,0:T(8,128)(2,1)S(1)}, bf16[2,4,72,832]{3,2,1,0:T(8,128)(2,1)S(1)}, u32[]{:S(2)}, u32[]{:S(2)}) collective-permute-start(bf16[2,4,72,832]{3,2,1,0:T(8,128)(2,1)S(1)} %grad_w_other.1), channel_id=1, source_target_pairs={{0,1},{1,0},{2,3},{3,2},{4,5},{5,4},{6,7},{7,6},{8,9},{9,8},{10,11... | collective-permute-start | bytes 2875400 | tf_op jit(solution)/shard_map/ppermute | solution.py:383
  62.6 14.7 %collective-permute-start.14 = (bf16[4,72,896]{2,1,0:T(8,128)(2,1)S(1)}, bf16[4,72,896]{2,1,0:T(8,128)(2,1)S(1)}, u32[]{:S(2)}, u32[]{:S(2)}) collective-permute-start(bf16[4,72,896]{2,1,0:T(8,128)(2,1)S(1)} %grad_w_rows.5), channel_id=1, source_target_pairs={{0,2},{1,3},{2,0},{3,1},{4,6},{5,7},{6,4},{7,5},{8,10},{9,11},{10,... | collective-permute-start | bytes 1548296 | tf_op jit(solution)/shard_map/ppermute | solution.py:383
  67.8 15.3 %collective-permute-start.16 = (bf16[4,2,32,1152]{3,2,1,0:T(8,128)(2,1)S(1)}, bf16[4,2,32,1152]{3,2,1,0:T(8,128)(2,1)S(1)}, u32[]{:S(2)}, u32[]{:S(2)}) collective-permute-start(bf16[4,2,32,1152]{3,2,1,0:T(8,128)(2,1)S(1)} %get-tuple-element.72), channel_id=1, source_target_pairs={{0,4},{4,0},{8,12},{12,8},{16,20},{20,16},{24,28},{28,24},{1,5},{5... | collective-permute-start | bytes 1769480 | tf_op jit(solution)/shard_map/ppermute | solution.py:386
  70.3 17.2 %collective-permute-start.21 = (bf16[4,72,832]{2,1,0:T(8,128)(2,1)S(1)}, bf16[4,72,832]{2,1,0:T(8,128)(2,1)S(1)}, u32[]{:S(2)}, u32[]{:S(2)}) collective-permute-start(bf16[4,72,832]{2,1,0:T(8,128)(2,1)S(1)} %grad_w_rows.6), channel_id=1, source_target_pairs={{0,2},{1,3},{2,0},{3,1},{4,6},{5,7},{6,4},{7,5},{8,10},{9,11},{10,... | collective-permute-start | bytes 1437704 | tf_op jit(solution)/shard_map/ppermute | solution.py:383
  77.4 6.7 %collective-permute-start.15 = (bf16[2,72,896]{2,1,0:T(8,128)(2,1)S(1)}, bf16[2,72,896]{2,1,0:T(8,128)(2,1)S(1)}, u32[]{:S(2)}, u32[]{:S(2)}) collective-permute-start(bf16[2,72,896]{2,1,0:T(8,128)(2,1)S(1)} %get-tuple-element.71), channel_id=1, source_target_pairs={{0,8},{4,12},{8,0},{12,4},{16,24},{20,28},{24,16},{28,20},{1,9},{5... | collective-permute-start | bytes 774152 | tf_op jit(solution)/shard_map/ppermute | solution.py:389
  84.1 7.0 %collective-permute-start.22 = (bf16[72,896]{1,0:T(8,128)(2,1)S(1)}, bf16[72,896]{1,0:T(8,128)(2,1)S(1)}, u32[]{:S(2)}, u32[]{:S(2)}) collective-permute-start(bf16[72,896]{1,0:T(8,128)(2,1)S(1)} %get-tuple-element.81), channel_id=1, source_target_pairs={{0,16},{4,20},{8,24},{12,28},{16,0},{20,4},{24,8},{28,12},{1,17},{... | collective-permute-start | bytes 387080 | tf_op jit(solution)/shard_map/ppermute | solution.py:389
  91.3 12.0 %collective-permute-start.23 = (bf16[2,72,832]{2,1,0:T(8,128)(2,1)S(1)}, bf16[2,72,832]{2,1,0:T(8,128)(2,1)S(1)}, u32[]{:S(2)}, u32[]{:S(2)}) collective-permute-start(bf16[2,72,832]{2,1,0:T(8,128)(2,1)S(1)} %get-tuple-element.85), channel_id=1, source_target_pairs={{0,8},{4,12},{8,0},{12,4},{16,24},{20,28},{24,16},{28,20},{1,9},{5... | collective-permute-start | bytes 718856 | tf_op jit(solution)/shard_map/ppermute | solution.py:389
  91.4 11.9 %collective-permute-start.25 = (bf16[72,896]{1,0:T(8,128)(2,1)S(1)}, bf16[72,896]{1,0:T(8,128)(2,1)S(1)}, u32[]{:S(2)}, u32[]{:S(2)}) collective-permute-start(bf16[72,896]{1,0:T(8,128)(2,1)S(1)} %sum_z.2.refs_0_), channel_id=1, source_target_pairs={{0,16},{4,20},{8,24},{12,28},{16,0},{20,4},{24,8},{28,12},{1,17},{... | collective-permute-start | bytes 387080 | tf_op jit(solution)/shard_map/ppermute | solution.py:389
  94.4 14.3 %collective-permute-start.28 = (bf16[72,896]{1,0:T(8,128)(2,1)S(1)}, bf16[72,896]{1,0:T(8,128)(2,1)S(1)}, u32[]{:S(2)}, u32[]{:S(2)}) collective-permute-start(bf16[72,896]{1,0:T(8,128)(2,1)S(1)} %sum_z.2.refs_0_), channel_id=1, source_target_pairs={{0,4},{4,0},{8,12},{12,8},{16,20},{20,16},{24,28},{28,24},{1,5},{5... | collective-permute-start | bytes 387080 | tf_op jit(solution)/shard_map/ppermute | solution.py:386
  96.1 12.6 %collective-permute-start.27 = (bf16[72,896]{1,0:T(8,128)(2,1)S(1)}, bf16[72,896]{1,0:T(8,128)(2,1)S(1)}, u32[]{:S(2)}, u32[]{:S(2)}) collective-permute-start(bf16[72,896]{1,0:T(8,128)(2,1)S(1)} %sum_z.2.refs_0_), channel_id=1, source_target_pairs={{0,8},{4,12},{8,0},{12,4},{16,24},{20,28},{24,16},{28,20},{1,9},{5... | collective-permute-start | bytes 387080 | tf_op jit(solution)/shard_map/ppermute | solution.py:389
  103.3 8.0 %collective-permute-start.26 = (bf16[72,896]{1,0:T(8,128)(2,1)S(1)}, bf16[72,896]{1,0:T(8,128)(2,1)S(1)}, u32[]{:S(2)}, u32[]{:S(2)}) collective-permute-start(bf16[72,896]{1,0:T(8,128)(2,1)S(1)} %collective-permute-done.25.refs_1_.refs_2_), channel_id=1, source_target_pairs={{0,8},{4,12},{8,0},{12,4},{16,24},{20,28},{24,16},{28,20},{1,9},{5... | collective-permute-start | bytes 387080 | tf_op jit(solution)/shard_map/ppermute | solution.py:389
  103.4 8.0 %collective-permute-start.24 = (bf16[72,832]{1,0:T(8,128)(2,1)S(1)}, bf16[72,832]{1,0:T(8,128)(2,1)S(1)}, u32[]{:S(2)}, u32[]{:S(2)}) collective-permute-start(bf16[72,832]{1,0:T(8,128)(2,1)S(1)} %get-tuple-element.86), channel_id=1, source_target_pairs={{0,16},{4,20},{8,24},{12,28},{16,0},{20,4},{24,8},{28,12},{1,17},{... | collective-permute-start | bytes 359432 | tf_op jit(solution)/shard_map/ppermute | solution.py:389
  111.5 9.2 %collective-permute-start.34 = (bf16[88,832]{1,0:T(8,128)(2,1)S(1)}, bf16[88,832]{1,0:T(8,128)(2,1)S(1)}, u32[]{:S(2)}, u32[]{:S(2)}) collective-permute-start(bf16[88,832]{1,0:T(8,128)(2,1)S(1)} %sum_z.3.refs_6_), channel_id=1, source_target_pairs={{0,16},{4,20},{8,24},{12,28},{16,0},{20,4},{24,8},{28,12},{1,17},{... | collective-permute-start | bytes 439304 | tf_op jit(solution)/shard_map/ppermute | solution.py:389
  112.4 9.8 %collective-permute-start.33 = (bf16[88,832]{1,0:T(8,128)(2,1)S(1)}, bf16[88,832]{1,0:T(8,128)(2,1)S(1)}, u32[]{:S(2)}, u32[]{:S(2)}) collective-permute-start(bf16[88,832]{1,0:T(8,128)(2,1)S(1)} %sum_z.3.refs_6_), channel_id=1, source_target_pairs={{0,8},{4,12},{8,0},{12,4},{16,24},{20,28},{24,16},{28,20},{1,9},{5... | collective-permute-start | bytes 439304 | tf_op jit(solution)/shard_map/ppermute | solution.py:389
  113.5 8.6 %collective-permute-start.32 = (bf16[88,832]{1,0:T(8,128)(2,1)S(1)}, bf16[88,832]{1,0:T(8,128)(2,1)S(1)}, u32[]{:S(2)}, u32[]{:S(2)}) collective-permute-start(bf16[88,832]{1,0:T(8,128)(2,1)S(1)} %sum_z.3.refs_6_), channel_id=1, source_target_pairs={{0,4},{4,0},{8,12},{12,8},{16,20},{20,16},{24,28},{28,24},{1,5},{5... | collective-permute-start | bytes 439304 | tf_op jit(solution)/shard_map/ppermute | solution.py:386
  115.3 21.6 %collective-permute-start.31 = (bf16[3,72,896]{2,1,0:T(8,128)(2,1)S(1)}, bf16[3,72,896]{2,1,0:T(8,128)(2,1)S(1)}, u32[]{:S(2)}, u32[]{:S(2)}) collective-permute-start(bf16[3,72,896]{2,1,0:T(8,128)(2,1)S(1)} %stack.1), channel_id=1, source_target_pairs={{0,4},{4,0},{8,12},{12,8},{16,20},{20,16},{24,28},{28,24},{1,5},{5... | collective-permute-start | bytes 1161224 | tf_op jit(solution)/shard_map/ppermute | solution.py:386
  115.8 9.4 %collective-permute-start.17 = (bf16[2,32,1152]{2,1,0:T(8,128)(2,1)S(1)}, bf16[2,32,1152]{2,1,0:T(8,128)(2,1)S(1)}, u32[]{:S(2)}, u32[]{:S(2)}) collective-permute-start(bf16[2,32,1152]{2,1,0:T(8,128)(2,1)S(1)} %get-tuple-element.75), channel_id=1, source_target_pairs={{0,8},{4,12},{8,0},{12,4},{16,24},{20,28},{24,16},{28,20},{1,9},{5... | collective-permute-start | bytes 442376 | tf_op jit(solution)/shard_map/ppermute | solution.py:389
  120.7 10.6 %collective-permute-start.18 = (bf16[2,32,1152]{2,1,0:T(8,128)(2,1)S(1)}, bf16[2,32,1152]{2,1,0:T(8,128)(2,1)S(1)}, u32[]{:S(2)}, u32[]{:S(2)}) collective-permute-start(bf16[2,32,1152]{2,1,0:T(8,128)(2,1)S(1)} %get-tuple-element.76), channel_id=1, source_target_pairs={{0,16},{4,20},{8,24},{12,28},{16,0},{20,4},{24,8},{28,12},{1,17},{... | collective-permute-start | bytes 442376 | tf_op jit(solution)/shard_map/ppermute | solution.py:389
  122.1 11.5 %collective-permute-start.35 = (bf16[88,832]{1,0:T(8,128)(2,1)S(1)}, bf16[88,832]{1,0:T(8,128)(2,1)S(1)}, u32[]{:S(2)}, u32[]{:S(2)}) collective-permute-start(bf16[88,832]{1,0:T(8,128)(2,1)S(1)} %collective-permute-done.34.refs_8_), channel_id=1, source_target_pairs={{0,8},{4,12},{8,0},{12,4},{16,24},{20,28},{24,16},{28,20},{1,9},{5... | collective-permute-start | bytes 439304 | tf_op jit(solution)/shard_map/ppermute | solution.py:389
  122.6 12.8 %collective-permute-start.19 = (bf16[2,32,1152]{2,1,0:T(8,128)(2,1)S(1)}, bf16[2,32,1152]{2,1,0:T(8,128)(2,1)S(1)}, u32[]{:S(2)}, u32[]{:S(2)}) collective-permute-start(bf16[2,32,1152]{2,1,0:T(8,128)(2,1)S(1)} %get-tuple-element.77), channel_id=1, source_target_pairs={{0,24},{4,28},{8,16},{12,20},{16,8},{20,12},{24,0},{28,4},{1,25},{... | collective-permute-start | bytes 442376 | tf_op jit(solution)/shard_map/ppermute | solution.py:389
  125.2 11.7 %collective-permute-start.36 = (bf16[88,832]{1,0:T(8,128)(2,1)S(1)}, bf16[88,832]{1,0:T(8,128)(2,1)S(1)}, u32[]{:S(2)}, u32[]{:S(2)}) collective-permute-start(bf16[88,832]{1,0:T(8,128)(2,1)S(1)} %collective-permute-done.33.refs_7_), channel_id=1, source_target_pairs={{0,4},{4,0},{8,12},{12,8},{16,20},{20,16},{24,28},{28,24},{1,5},{5... | collective-permute-start | bytes 439304 | tf_op jit(solution)/shard_map/ppermute | solution.py:386
  (11 other events, 84.8 us)

commit v6 on v5

--- a/solution.py
+++ b/solution.py
@@ -117,13 +117,25 @@
             keep[k][b] = pick(y == 0, low, high).astype(BF16)
 
 
-def main_kernel(groups, shares, cuts, *refs):
+def join_kernel(shares, *refs):
+    parts, (out, sems) = refs[:shares], refs[shares:]
+    _, _, s = place()
+    share = out.shape[0] // shares
+    copies = []
+    for k in range(shares):
+        rows = pl.ds(pl.multiple_of((s ^ k) * share, share), share)
+        copies.append(pltpu.make_async_copy(parts[k], out.at[rows], sems.at[k]))
+        copies[-1].start()
+    for copy in copies:
+        copy.wait()
+
+
+def main_kernel(groups, share, cuts, *refs):
     near, kept, far = refs[:groups], refs[groups : 2 * groups], refs[2 * groups : 3 * groups]
-    weights = refs[3 * groups : 3 * groups + shares]
-    table, *rest = refs[3 * groups + shares :]
+    w, table, *rest = refs[3 * groups :]
     outs, scratches = rest[: 3 + len(cuts[:1])], rest[3 + len(cuts[:1]) :]
     grads, mod_t, normed = outs[:3]
-    w, mod, up, qw, kw, vw, dq, dk, dv, sems = scratches
+    mod, up, qw, kw, vw, dq, dk, dv = scratches
     _, _, s = place()
     clips, chunk, _ = near[0].shape
     depth, wide = w.shape
@@ -131,13 +143,7 @@
     frames = 2 * groups
     block = frames * SLAB
     slabs = chunk // SLAB
-    share = depth // shares
     pad = qw.shape[1]
-    copies = []
-    for k in range(shares):
-        rows = pl.ds(pl.multiple_of((s ^ k) * share, share), share) if shares > 1 else pl.ds(0, depth)
-        copies.append(pltpu.make_async_copy(weights[k], w.at[rows], sems.at[k]))
-        copies[-1].start()
     for b in range(clips):
         shift, scale, loss = table[b, 0:1, :], 1.0 + table[b, 1:2, :], table[b, 2:3, :half]
         for k in range(groups):
@@ -154,8 +160,6 @@
                     up[base : base + SLAB, :half] = upstream[i * SLAB : (i + 1) * SLAB]
     up[:, half:] = jnp.zeros((up.shape[0], pad - half), BF16)
     vw[:, half:] = jnp.zeros((block, pad - half), BF16)
-    for copy in copies:
-        copy.wait()
 
     lane = lax.broadcasted_iota(jnp.int32, (block, 2 * LANES), 1)
     row = lax.broadcasted_iota(jnp.int32, (block, 2 * block), 0)
@@ -230,16 +234,7 @@
         out[g] = (total[g * rows : (g + 1) * rows] + got[step, g].astype(F32)).astype(out.dtype)
 
 
-def hidden_kernel(shares, grads, normed, *refs):
-    weights, (far_hidden, near_hidden, sums, w, part, sems) = refs[:shares], refs[shares:]
-    _, _, s = place()
-    depth = w.shape[0]
-    share = depth // shares
-    copies = []
-    for k in range(shares):
-        rows = pl.ds(pl.multiple_of((s ^ k) * share, share), share) if shares > 1 else pl.ds(0, depth)
-        copies.append(pltpu.make_async_copy(weights[k], w.at[rows], sems.at[k]))
-        copies[-1].start()
+def hidden_kernel(grads, normed, w, far_hidden, near_hidden, sums, part):
     groups, clips, chunk, _ = near_hidden.shape
     slabs = chunk // SLAB
     side = groups * SLAB
@@ -248,9 +243,6 @@
         for n in range(clips * slabs):
             start = (2 * n + which) * side
             part[n * side : (n + 1) * side, :] = grads[start : start + side, :]
-        if which:
-            for copy in copies:
-                copy.wait()
         total = dot(part[...], w[...], ROWS_ROWS)
         for b in range(clips):
             for i in range(slabs):
@@ -422,21 +414,27 @@
         weights = [w_half, over_space(w_half, 1)]
         for x in crossed:
             weights += [x, over_space(after(x, *near[1:]), 1)]
+        weights = call(
+            functools.partial(join_kernel, shares),
+            "join_w",
+            shape((width, wide)),
+            [HBM] * shares,
+            [pltpu.SemaphoreType.DMA((shares,))],
+        )(*weights)
+        far[-1] = after(far[-1], weights)
     else:
-        weights = [lax.all_gather(w_half, "space", axis=0, tiled=True)]
+        weights = lax.all_gather(w_half, "space", axis=0, tiled=True)
 
     pad = -(-half // LANES) * LANES
     outs = [shape((tokens, wide)), shape((width, tokens)), shape((tokens, width))]
     other_rows = [shape((lines, groups, rows, cut.stop - cut.start)) for cut in cuts]
     outs += other_rows[:1]
-    w_scratch = pltpu.VMEM((width, wide), BF16)
     main = call(
-        functools.partial(main_kernel, groups, shares, cuts),
+        functools.partial(main_kernel, groups, share, cuts),
         "attend",
         outs,
-        [VMEM] * (3 * groups) + [HBM] * shares + [VMEM],
+        [VMEM] * (3 * groups + 2),
         [
-            w_scratch,
             pltpu.VMEM((tokens, width), BF16),
             pltpu.VMEM((tokens, pad), BF16),
             pltpu.VMEM((block, pad), BF16),
@@ -445,22 +443,21 @@
             pltpu.VMEM((block, pad), F32),
             pltpu.VMEM((block, pad), F32),
             pltpu.VMEM((block, pad), F32),
-            pltpu.SemaphoreType.DMA((shares,)),
         ],
         flops=2 * tokens * width * wide * 3,
         moved=20 << 20,
-    )(*near, *kept, *far, *weights, modulation)
+    )(*near, *kept, *far, weights, modulation)
     grads, mod_t, normed = main[:3]
 
     far_hidden, near_hidden, sums = call(
-        functools.partial(hidden_kernel, shares),
+        hidden_kernel,
         "grad_hidden",
         [shape((groups, clips, chunk, width))] * 2 + [shape((clips, 2, width), F32)],
-        [VMEM] * 2 + [HBM] * shares,
-        [w_scratch, pltpu.VMEM((tokens // 2, wide), BF16), pltpu.SemaphoreType.DMA((shares,))],
+        [VMEM] * 3,
+        [pltpu.VMEM((tokens // 2, wide), BF16)],
         flops=2 * tokens * width * wide,
         moved=8 << 20,
-    )(grads, normed, *weights)
+    )(grads, normed, weights)
 
     def meet(came):
         back = call(

time: 142 us -> 138 us (0.972)
  waiting for transfers between devices: 65.5 us -> 60.9 us
  starting transfers between devices: 48.2 us -> 50.7 us
  Pallas kernels: 27 us -> 25.3 us
    ppermute x19, waiting for transfers between devices: 39.6 us -> 34.8 us  [over_z(): return lax.ppermute(x, 'frame', [(i, i ^ 2 * step) for i in range(frames)])]
    ppermute x19, starting transfers between devices: 25.7 us -> 28.5 us  [over_z(): return lax.ppermute(x, 'frame', [(i, i ^ 2 * step) for i in range(frames)])]
    pallas_call x2 -> x3, Pallas kernels: 15.4 us -> 13.8 us  [the longest x1 9.57 us: per_device(): call(functools.partial(main_kernel, groups, share, cuts), 'attend', outs,...]
  transfers between devices with their start and end apart: 39 -> 39, of which waited for: 20 -> 20; matrix products, arithmetic and copies ran while one was open for 0% -> 0% of each run, Pallas kernels for 7% -> 8%
where the time goes in v6:
time: 138 us
  waiting for transfers between devices  60.9 us (44%)
  starting transfers between devices  50.7 us (37%)
  Pallas kernels  25.3 us (18%)
    ppermute x19, waiting for transfers between devices, over_z(): return lax.ppermute(x, 'frame', [(i, i ^ 2 * step) for i in range(frames)])  34.8 us
    ppermute x19, starting transfers between devices, over_z(): return lax.ppermute(x, 'frame', [(i, i ^ 2 * step) for i in range(frames)])  28.5 us
    ppermute x11, starting transfers between devices, over_y(): return lax.ppermute(x, 'frame', [(i, i ^ 1) for i in range(frames)])  14.6 us
    ppermute x11, waiting for transfers between devices, over_y(): return lax.ppermute(x, 'frame', [(i, i ^ 1) for i in range(frames)])  14.2 us
    ppermute x9, waiting for transfers between devices, over_space(): return lax.ppermute(x, 'space', [(i, i ^ step) for i in range(spaces)])  11.9 us
    pallas_call x1, Pallas kernels, per_device(): call(functools.partial(main_kernel, groups, share, cuts), 'attend', outs,...  9.57 us
    ppermute x9, starting transfers between devices, over_space(): return lax.ppermute(x, 'space', [(i, i ^ step) for i in range(spaces)])  7.57 us
    pallas_call x1, Pallas kernels, per_device(): call(functools.partial(weight_kernel, grad_scale_factor), 'grad_w', [shap...  2.8 us
  transfers between devices with their start and end apart: 39, of which 20 were waited for; matrix products, arithmetic and copies ran while one was open for 0% of the time, Pallas kernels for 8%

profile of v6, /device:TPU:0, one launch (start us, length us, event | category | flops | bytes accessed | tf_op | source)
XLA Modules:
  0.0 137.8 jit_solution(17996318987318678875)
XLA Ops:
  0.6 2.2 %lookup.1.refs_13_.mod_ref = f32[2,3,1152]{2,1,0:T(4,128)} custom-call(bf16[1000,2,1152]{2,1,0:T(2,128)(2,1)} %tab_ref.1, s32[2]{0:T(128)} %ts_ref.1, f32[1000]{0:T(1024)} %snr_ref.1, s32[2]{0:T(128)} %wi_ref.1), custom_call_target="tpu_custom_call" | custom-call | bytes 1048576 | tf_op jit(solution)/shard_map/lookup/pallas_call | solution.py:386
  3.1 3.0 %collective-permute-start.11 = (bf16[288,1728]{1,0:T(8,128)(2,1)S(1)}, bf16[288,1728]{1,0:T(8,128)(2,1)S(1)}, u32[]{:S(2)}, u32[]{:S(2)}) collective-permute-start(bf16[288,1728]{1,0:T(8,128)(2,1)S(1)} %w_half.1.refs_0_), channel_id=1, source_target_pairs={{0,2},{1,3},{2,0},{3,1},{4,6},{5,7},{6,4},{7,5},{8,10},{9,11},{10,... | collective-permute-start | bytes 2985992 | tf_op jit(solution)/shard_map/ppermute | solution.py:375
  10.9 2.6 %collective-permute-start.2 = (bf16[2,32,1728]{2,1,0:T(8,128)(2,1)S(1)}, bf16[2,32,1728]{2,1,0:T(8,128)(2,1)S(1)}, u32[]{:S(2)}, u32[]{:S(2)}) collective-permute-start(bf16[2,32,1728]{2,1,0:T(8,128)(2,1)S(1)} %get-tuple-element.58), channel_id=1, source_target_pairs={{0,16},{4,20},{8,24},{12,28},{16,0},{20,4},{24,8},{28,12},{1,17},{... | collective-permute-start | bytes 663560 | tf_op jit(solution)/shard_map/ppermute | solution.py:381
  13.4 4.5 %collective-permute-done.refs_1_ = bf16[2,32,1728]{2,1,0:T(8,128)(2,1)S(1)} collective-permute-done((bf16[2,32,1728]{2,1,0:T(8,128)(2,1)S(1)}, bf16[2,32,1728]{2,1,0:T(8,128)(2,1)S(1)}, u32[]{:S(2)}, u32[]{:S(2)}) %collective-permute-start) | collective-permute-done | bytes 221216 | tf_op jit(solution)/shard_map/ppermute | solution.py:381
  18.0 3.0 %collective-permute-start.3 = (bf16[2,32,1728]{2,1,0:T(8,128)(2,1)S(1)}, bf16[2,32,1728]{2,1,0:T(8,128)(2,1)S(1)}, u32[]{:S(2)}, u32[]{:S(2)}) collective-permute-start(bf16[2,32,1728]{2,1,0:T(8,128)(2,1)S(1)} %collective-permute-done.refs_1_), channel_id=1, source_target_pairs={{0,4},{4,0},{8,12},{12,8},{16,20},{20,16},{24,28},{28,24},{1,5},{5... | collective-permute-start | bytes 663560 | tf_op jit(solution)/shard_map/ppermute | solution.py:378
  21.0 2.5 %collective-permute-start.4 = (bf16[2,32,1728]{2,1,0:T(8,128)(2,1)S(1)}, bf16[2,32,1728]{2,1,0:T(8,128)(2,1)S(1)}, u32[]{:S(2)}, u32[]{:S(2)}) collective-permute-start(bf16[2,32,1728]{2,1,0:T(8,128)(2,1)S(1)} %get-tuple-element.60), channel_id=1, source_target_pairs={{0,24},{4,28},{8,16},{12,20},{16,8},{20,12},{24,0},{28,4},{1,25},{... | collective-permute-start | bytes 663560 | tf_op jit(solution)/shard_map/ppermute | solution.py:381
  23.5 6.0 %collective-permute-done.2.refs_2_ = bf16[2,32,1728]{2,1,0:T(8,128)(2,1)S(1)} collective-permute-done((bf16[2,32,1728]{2,1,0:T(8,128)(2,1)S(1)}, bf16[2,32,1728]{2,1,0:T(8,128)(2,1)S(1)}, u32[]{:S(2)}, u32[]{:S(2)}) %collective-permute-start.2) | collective-permute-done | bytes 221216 | tf_op jit(solution)/shard_map/ppermute | solution.py:381
  29.5 6.0 %collective-permute-done.5.refs_10_ = bf16[2,32,1728]{2,1,0:T(8,128)(2,1)S(1)} collective-permute-done((bf16[2,32,1728]{2,1,0:T(8,128)(2,1)S(1)}, bf16[2,32,1728]{2,1,0:T(8,128)(2,1)S(1)}, u32[]{:S(2)}, u32[]{:S(2)}) %collective-permute-start.5) | collective-permute-done | bytes 221216 | tf_op jit(solution)/shard_map/ppermute | solution.py:378
  35.6 3.3 %collective-permute-start.7 = (bf16[2,32,576]{2,1,0:T(8,128)(2,1)S(1)}, bf16[2,32,576]{2,1,0:T(8,128)(2,1)S(1)}, u32[]{:S(2)}, u32[]{:S(2)}) collective-permute-start(bf16[2,32,576]{2,1,0:T(8,128)(2,1)S(1)} %get-tuple-element.64), channel_id=1, source_target_pairs={{0,16},{4,20},{8,24},{12,28},{16,0},{20,4},{24,8},{28,12},{1,17},{... | collective-permute-start | bytes 221192 | tf_op jit(solution)/shard_map/ppermute | solution.py:381
  41.6 2.0 %collective-permute-done.9.refs_11_ = bf16[2,32,1728]{2,1,0:T(8,128)(2,1)S(1)} collective-permute-done((bf16[2,32,1728]{2,1,0:T(8,128)(2,1)S(1)}, bf16[2,32,1728]{2,1,0:T(8,128)(2,1)S(1)}, u32[]{:S(2)}, u32[]{:S(2)}) %collective-permute-start.9) | collective-permute-done | bytes 221216 | tf_op jit(solution)/shard_map/ppermute | solution.py:378
  43.6 2.2 %collective-permute-done.7.refs_6_ = bf16[2,32,576]{2,1,0:T(8,128)(2,1)S(1)} collective-permute-done((bf16[2,32,576]{2,1,0:T(8,128)(2,1)S(1)}, bf16[2,32,576]{2,1,0:T(8,128)(2,1)S(1)}, u32[]{:S(2)}, u32[]{:S(2)}) %collective-permute-start.7) | collective-permute-done | bytes 73760 | tf_op jit(solution)/shard_map/ppermute | solution.py:381
  45.7 9.6 %attend.1 = (bf16[512,1728]{1,0:T(8,128)(2,1)S(1)}, bf16[1152,512]{1,0:T(8,128)(2,1)S(1)}, bf16[512,1152]{1,0:T(8,128)(2,1)S(1)}, bf16[2,4,72,896]{3,2,1,0:T(8,128)(2,1)S(1)}) custom-call(bf16[2,32,1728]{2,1,0:T(8,128)(2,1)S(1)} %get-tuple-element.55.refs_0_, bf16[2,32,1728]{2,1,0:T(8,128)(2,1)S(1)} %collective-permute-done.refs_1_, ...), custom_call_target="tpu_custom_call" | custom-call | flops 6115295232 | bytes 20971520 | tf_op jit(solution)/shard_map/attend/pallas_call | solution.py:432
  59.9 2.7 %grad_hidden.1 = (bf16[4,2,32,1152]{3,2,1,0:T(8,128)(2,1)S(1)}, bf16[4,2,32,1152]{3,2,1,0:T(8,128)(2,1)S(1)}, f32[2,2,1152]{2,1,0:T(2,128)S(1)}) custom-call(bf16[512,1728]{1,0:T(8,128)(2,1)S(1)} %get-tuple-element.68.grads, bf16[512,1152]{1,0:T(8,128)(2,1)S(1)} %get-tuple-element.69.normed, bf16[1152,1728]{1,0:T(8,128)(2,1)S(1)} %join_w.1.refs_12_.w), custom_call_target="tpu_custom_call" | custom-call | flops 2038431744 | bytes 8388608 | tf_op jit(solution)/shard_map/grad_hidden/pallas_call | solution.py:452
  66.2 7.0 %collective-permute-done.14.got = bf16[4,72,896]{2,1,0:T(8,128)(2,1)S(1)} collective-permute-done((bf16[4,72,896]{2,1,0:T(8,128)(2,1)S(1)}, bf16[4,72,896]{2,1,0:T(8,128)(2,1)S(1)}, u32[]{:S(2)}, u32[]{:S(2)}) %collective-permute-start.14) | collective-permute-done | bytes 516128 | tf_op jit(solution)/shard_map/ppermute | solution.py:375
  73.3 1.8 %collective-permute-start.15 = (bf16[2,72,896]{2,1,0:T(8,128)(2,1)S(1)}, bf16[2,72,896]{2,1,0:T(8,128)(2,1)S(1)}, u32[]{:S(2)}, u32[]{:S(2)}) collective-permute-start(bf16[2,72,896]{2,1,0:T(8,128)(2,1)S(1)} %get-tuple-element.73), channel_id=1, source_target_pairs={{0,8},{4,12},{8,0},{12,4},{16,24},{20,28},{24,16},{28,20},{1,9},{5... | collective-permute-start | bytes 774152 | tf_op jit(solution)/shard_map/ppermute | solution.py:381
  75.1 2.6 %collective-permute-done.16.got = bf16[4,2,32,1152]{3,2,1,0:T(8,128)(2,1)S(1)} collective-permute-done((bf16[4,2,32,1152]{3,2,1,0:T(8,128)(2,1)S(1)}, bf16[4,2,32,1152]{3,2,1,0:T(8,128)(2,1)S(1)}, u32[]{:S(2)}, u32[]{:S(2)}) %collective-permute-start.16) | collective-permute-done | bytes 589856 | tf_op jit(solution)/shard_map/ppermute | solution.py:378
  77.7 2.3 %collective-permute-done.15.got = bf16[2,72,896]{2,1,0:T(8,128)(2,1)S(1)} collective-permute-done((bf16[2,72,896]{2,1,0:T(8,128)(2,1)S(1)}, bf16[2,72,896]{2,1,0:T(8,128)(2,1)S(1)}, u32[]{:S(2)}, u32[]{:S(2)}) %collective-permute-start.15) | collective-permute-done | bytes 258080 | tf_op jit(solution)/shard_map/ppermute | solution.py:381
  80.0 2.7 %collective-permute-start.22 = (bf16[72,896]{1,0:T(8,128)(2,1)S(1)}, bf16[72,896]{1,0:T(8,128)(2,1)S(1)}, u32[]{:S(2)}, u32[]{:S(2)}) collective-permute-start(bf16[72,896]{1,0:T(8,128)(2,1)S(1)} %get-tuple-element.83), channel_id=1, source_target_pairs={{0,16},{4,20},{8,24},{12,28},{16,0},{20,4},{24,8},{28,12},{1,17},{... | collective-permute-start | bytes 387080 | tf_op jit(solution)/shard_map/ppermute | solution.py:381
  83.4 4.0 %collective-permute-done.22.refs_1_ = bf16[72,896]{1,0:T(8,128)(2,1)S(1)} collective-permute-done((bf16[72,896]{1,0:T(8,128)(2,1)S(1)}, bf16[72,896]{1,0:T(8,128)(2,1)S(1)}, u32[]{:S(2)}, u32[]{:S(2)}) %collective-permute-start.22) | collective-permute-done | bytes 129056 | tf_op jit(solution)/shard_map/ppermute | solution.py:381
  88.0 2.3 %collective-permute-start.25 = (bf16[72,896]{1,0:T(8,128)(2,1)S(1)}, bf16[72,896]{1,0:T(8,128)(2,1)S(1)}, u32[]{:S(2)}, u32[]{:S(2)}) collective-permute-start(bf16[72,896]{1,0:T(8,128)(2,1)S(1)} %sum_z.2.refs_0_), channel_id=1, source_target_pairs={{0,16},{4,20},{8,24},{12,28},{16,0},{20,4},{24,8},{28,12},{1,17},{... | collective-permute-start | bytes 387080 | tf_op jit(solution)/shard_map/ppermute | solution.py:381
  90.3 2.0 %collective-permute-start.28 = (bf16[72,896]{1,0:T(8,128)(2,1)S(1)}, bf16[72,896]{1,0:T(8,128)(2,1)S(1)}, u32[]{:S(2)}, u32[]{:S(2)}) collective-permute-start(bf16[72,896]{1,0:T(8,128)(2,1)S(1)} %sum_z.2.refs_0_), channel_id=1, source_target_pairs={{0,4},{4,0},{8,12},{12,8},{16,20},{20,16},{24,28},{28,24},{1,5},{5... | collective-permute-start | bytes 387080 | tf_op jit(solution)/shard_map/ppermute | solution.py:378
  93.1 6.0 %collective-permute-done.23.got = bf16[2,72,832]{2,1,0:T(8,128)(2,1)S(1)} collective-permute-done((bf16[2,72,832]{2,1,0:T(8,128)(2,1)S(1)}, bf16[2,72,832]{2,1,0:T(8,128)(2,1)S(1)}, u32[]{:S(2)}, u32[]{:S(2)}) %collective-permute-start.23) | collective-permute-done | bytes 239648 | tf_op jit(solution)/shard_map/ppermute | solution.py:381
  100.2 2.0 %collective-permute-start.24 = (bf16[72,832]{1,0:T(8,128)(2,1)S(1)}, bf16[72,832]{1,0:T(8,128)(2,1)S(1)}, u32[]{:S(2)}, u32[]{:S(2)}) collective-permute-start(bf16[72,832]{1,0:T(8,128)(2,1)S(1)} %get-tuple-element.88), channel_id=1, source_target_pairs={{0,16},{4,20},{8,24},{12,28},{16,0},{20,4},{24,8},{28,12},{1,17},{... | collective-permute-start | bytes 359432 | tf_op jit(solution)/shard_map/ppermute | solution.py:381
  104.9 2.3 %collective-permute-done.30.more = f32[2,2,1152]{2,1,0:T(2,128)S(1)} collective-permute-done((f32[2,2,1152]{2,1,0:T(2,128)S(1)}, f32[2,2,1152]{2,1,0:T(2,128)S(1)}, u32[]{:S(2)}, u32[]{:S(2)}) %collective-permute-start.30) | collective-permute-done | bytes 18464 | tf_op jit(solution)/shard_map/ppermute | solution.py:375
  108.3 1.9 %collective-permute-start.33 = (bf16[88,832]{1,0:T(8,128)(2,1)S(1)}, bf16[88,832]{1,0:T(8,128)(2,1)S(1)}, u32[]{:S(2)}, u32[]{:S(2)}) collective-permute-start(bf16[88,832]{1,0:T(8,128)(2,1)S(1)} %sum_z.3.refs_6_), channel_id=1, source_target_pairs={{0,8},{4,12},{8,0},{12,4},{16,24},{20,28},{24,16},{28,20},{1,9},{5... | collective-permute-start | bytes 439304 | tf_op jit(solution)/shard_map/ppermute | solution.py:381
  112.6 4.4 %collective-permute-done.34.refs_8_ = bf16[88,832]{1,0:T(8,128)(2,1)S(1)} collective-permute-done((bf16[88,832]{1,0:T(8,128)(2,1)S(1)}, bf16[88,832]{1,0:T(8,128)(2,1)S(1)}, u32[]{:S(2)}, u32[]{:S(2)}) %collective-permute-start.34) | collective-permute-done | bytes 146464 | tf_op jit(solution)/shard_map/ppermute | solution.py:381
  119.0 2.4 %collective-permute-start.19 = (bf16[2,32,1152]{2,1,0:T(8,128)(2,1)S(1)}, bf16[2,32,1152]{2,1,0:T(8,128)(2,1)S(1)}, u32[]{:S(2)}, u32[]{:S(2)}) collective-permute-start(bf16[2,32,1152]{2,1,0:T(8,128)(2,1)S(1)} %get-tuple-element.79), channel_id=1, source_target_pairs={{0,24},{4,28},{8,16},{12,20},{16,8},{20,12},{24,0},{28,4},{1,25},{... | collective-permute-start | bytes 442376 | tf_op jit(solution)/shard_map/ppermute | solution.py:381
  121.4 1.8 %collective-permute-start.36 = (bf16[88,832]{1,0:T(8,128)(2,1)S(1)}, bf16[88,832]{1,0:T(8,128)(2,1)S(1)}, u32[]{:S(2)}, u32[]{:S(2)}) collective-permute-start(bf16[88,832]{1,0:T(8,128)(2,1)S(1)} %collective-permute-done.33.refs_7_), channel_id=1, source_target_pairs={{0,4},{4,0},{8,12},{12,8},{16,20},{20,16},{24,28},{28,24},{1,5},{5... | collective-permute-start | bytes 439304 | tf_op jit(solution)/shard_map/ppermute | solution.py:378
  123.2 4.3 %collective-permute-done.18.refs_2_ = bf16[2,32,1152]{2,1,0:T(8,128)(2,1)S(1)} collective-permute-done((bf16[2,32,1152]{2,1,0:T(8,128)(2,1)S(1)}, bf16[2,32,1152]{2,1,0:T(8,128)(2,1)S(1)}, u32[]{:S(2)}, u32[]{:S(2)}) %collective-permute-start.18) | collective-permute-done | bytes 147488 | tf_op jit(solution)/shard_map/ppermute | solution.py:381
  127.6 1.9 %collective-permute-start.37 = (bf16[88,832]{1,0:T(8,128)(2,1)S(1)}, bf16[88,832]{1,0:T(8,128)(2,1)S(1)}, u32[]{:S(2)}, u32[]{:S(2)}) collective-permute-start(bf16[88,832]{1,0:T(8,128)(2,1)S(1)} %collective-permute-done.34.refs_8_), channel_id=1, source_target_pairs={{0,4},{4,0},{8,12},{12,8},{16,20},{20,16},{24,28},{28,24},{1,5},{5... | collective-permute-start | bytes 439304 | tf_op jit(solution)/shard_map/ppermute | solution.py:378
  131.5 1.8 %collective-permute-done.37.refs_12_ = bf16[88,832]{1,0:T(8,128)(2,1)S(1)} collective-permute-done((bf16[88,832]{1,0:T(8,128)(2,1)S(1)}, bf16[88,832]{1,0:T(8,128)(2,1)S(1)}, u32[]{:S(2)}, u32[]{:S(2)}) %collective-permute-start.37) | collective-permute-done | bytes 146464 | tf_op jit(solution)/shard_map/ppermute | solution.py:378
  135.0 2.8 %grad_w.1 = (f32[288,3456]{1,0:T(8,128)}, f32[2,2,1152]{2,1,0:T(2,128)}) custom-call(bf16[72,896]{1,0:T(8,128)(2,1)S(1)} %sum_z.2.refs_0_, bf16[72,896]{1,0:T(8,128)(2,1)S(1)} %collective-permute-done.27.refs_0_.refs_1_, bf16[72,896]{1,0:T(8,128)(2,1)S(1)} %collective-permute-done.25.refs_1_.refs_2_, ...), custom_call_target="tpu_custom_call" | custom-call | bytes 1048576 | tf_op jit(solution)/shard_map/grad_w/pallas_call | solution.py:538
  (76 shorter events, 31.1 us)
Async XLA Ops:
  3.1 32.5 %collective-permute-start.11 = (bf16[288,1728]{1,0:T(8,128)(2,1)S(1)}, bf16[288,1728]{1,0:T(8,128)(2,1)S(1)}, u32[]{:S(2)}, u32[]{:S(2)}) collective-permute-start(bf16[288,1728]{1,0:T(8,128)(2,1)S(1)} %w_half.1.refs_0_), channel_id=1, source_target_pairs={{0,2},{1,3},{2,0},{3,1},{4,6},{5,7},{6,4},{7,5},{8,10},{9,11},{10,... | collective-permute-start | bytes 2985992 | tf_op jit(solution)/shard_map/ppermute | solution.py:375
  7.6 10.4 %collective-permute-start = (bf16[2,32,1728]{2,1,0:T(8,128)(2,1)S(1)}, bf16[2,32,1728]{2,1,0:T(8,128)(2,1)S(1)}, u32[]{:S(2)}, u32[]{:S(2)}) collective-permute-start(bf16[2,32,1728]{2,1,0:T(8,128)(2,1)S(1)} %get-tuple-element.56), channel_id=1, source_target_pairs={{0,8},{4,12},{8,0},{12,4},{16,24},{20,28},{24,16},{28,20},{1,9},{5... | collective-permute-start | bytes 663560 | tf_op jit(solution)/shard_map/ppermute | solution.py:381
  9.2 8.7 %collective-permute-start.1 = (bf16[2,32,1728]{2,1,0:T(8,128)(2,1)S(1)}, bf16[2,32,1728]{2,1,0:T(8,128)(2,1)S(1)}, u32[]{:S(2)}, u32[]{:S(2)}) collective-permute-start(bf16[2,32,1728]{2,1,0:T(8,128)(2,1)S(1)} %get-tuple-element.55.refs_0_), channel_id=1, source_target_pairs={{0,4},{4,0},{8,12},{12,8},{16,20},{20,16},{24,28},{28,24},{1,5},{5... | collective-permute-start | bytes 663560 | tf_op jit(solution)/shard_map/ppermute | solution.py:378
  10.9 18.7 %collective-permute-start.2 = (bf16[2,32,1728]{2,1,0:T(8,128)(2,1)S(1)}, bf16[2,32,1728]{2,1,0:T(8,128)(2,1)S(1)}, u32[]{:S(2)}, u32[]{:S(2)}) collective-permute-start(bf16[2,32,1728]{2,1,0:T(8,128)(2,1)S(1)} %get-tuple-element.58), channel_id=1, source_target_pairs={{0,16},{4,20},{8,24},{12,28},{16,0},{20,4},{24,8},{28,12},{1,17},{... | collective-permute-start | bytes 663560 | tf_op jit(solution)/shard_map/ppermute | solution.py:381
  18.0 11.6 %collective-permute-start.3 = (bf16[2,32,1728]{2,1,0:T(8,128)(2,1)S(1)}, bf16[2,32,1728]{2,1,0:T(8,128)(2,1)S(1)}, u32[]{:S(2)}, u32[]{:S(2)}) collective-permute-start(bf16[2,32,1728]{2,1,0:T(8,128)(2,1)S(1)} %collective-permute-done.refs_1_), channel_id=1, source_target_pairs={{0,4},{4,0},{8,12},{12,8},{16,20},{20,16},{24,28},{28,24},{1,5},{5... | collective-permute-start | bytes 663560 | tf_op jit(solution)/shard_map/ppermute | solution.py:378
  21.0 8.5 %collective-permute-start.4 = (bf16[2,32,1728]{2,1,0:T(8,128)(2,1)S(1)}, bf16[2,32,1728]{2,1,0:T(8,128)(2,1)S(1)}, u32[]{:S(2)}, u32[]{:S(2)}) collective-permute-start(bf16[2,32,1728]{2,1,0:T(8,128)(2,1)S(1)} %get-tuple-element.60), channel_id=1, source_target_pairs={{0,24},{4,28},{8,16},{12,20},{16,8},{20,12},{24,0},{28,4},{1,25},{... | collective-permute-start | bytes 663560 | tf_op jit(solution)/shard_map/ppermute | solution.py:381
  29.5 9.4 %collective-permute-start.10 = (bf16[288,1728]{1,0:T(8,128)(2,1)S(1)}, bf16[288,1728]{1,0:T(8,128)(2,1)S(1)}, u32[]{:S(2)}, u32[]{:S(2)}) collective-permute-start(bf16[288,1728]{1,0:T(8,128)(2,1)S(1)} %w_half.1.refs_0_), channel_id=1, source_target_pairs={{0,1},{1,0},{2,3},{3,2},{4,5},{5,4},{6,7},{7,6},{8,9},{9,8},{10,11... | collective-permute-start | bytes 2985992 | tf_op jit(solution)/shard_map/ppermute | solution.py:375
  35.5 8.0 %collective-permute-start.9 = (bf16[2,32,1728]{2,1,0:T(8,128)(2,1)S(1)}, bf16[2,32,1728]{2,1,0:T(8,128)(2,1)S(1)}, u32[]{:S(2)}, u32[]{:S(2)}) collective-permute-start(bf16[2,32,1728]{2,1,0:T(8,128)(2,1)S(1)} %collective-permute-done.4.refs_3_), channel_id=1, source_target_pairs={{0,4},{4,0},{8,12},{12,8},{16,20},{20,16},{24,28},{28,24},{1,5},{5... | collective-permute-start | bytes 663560 | tf_op jit(solution)/shard_map/ppermute | solution.py:378
  35.6 8.0 %collective-permute-start.6 = (bf16[2,32,576]{2,1,0:T(8,128)(2,1)S(1)}, bf16[2,32,576]{2,1,0:T(8,128)(2,1)S(1)}, u32[]{:S(2)}, u32[]{:S(2)}) collective-permute-start(bf16[2,32,576]{2,1,0:T(8,128)(2,1)S(1)} %get-tuple-element.63), channel_id=1, source_target_pairs={{0,8},{4,12},{8,0},{12,4},{16,24},{20,28},{24,16},{28,20},{1,9},{5... | collective-permute-start | bytes 221192 | tf_op jit(solution)/shard_map/ppermute | solution.py:381
  35.6 10.1 %collective-permute-start.7 = (bf16[2,32,576]{2,1,0:T(8,128)(2,1)S(1)}, bf16[2,32,576]{2,1,0:T(8,128)(2,1)S(1)}, u32[]{:S(2)}, u32[]{:S(2)}) collective-permute-start(bf16[2,32,576]{2,1,0:T(8,128)(2,1)S(1)} %get-tuple-element.64), channel_id=1, source_target_pairs={{0,16},{4,20},{8,24},{12,28},{16,0},{20,4},{24,8},{28,12},{1,17},{... | collective-permute-start | bytes 221192 | tf_op jit(solution)/shard_map/ppermute | solution.py:381
  38.9 6.8 %collective-permute-start.8 = (bf16[2,32,576]{2,1,0:T(8,128)(2,1)S(1)}, bf16[2,32,576]{2,1,0:T(8,128)(2,1)S(1)}, u32[]{:S(2)}, u32[]{:S(2)}) collective-permute-start(bf16[2,32,576]{2,1,0:T(8,128)(2,1)S(1)} %get-tuple-element.65), channel_id=1, source_target_pairs={{0,24},{4,28},{8,16},{12,20},{16,8},{20,12},{24,0},{28,4},{1,25},{... | collective-permute-start | bytes 221192 | tf_op jit(solution)/shard_map/ppermute | solution.py:381
  56.2 8.0 %collective-permute-start.20 = (bf16[2,4,72,832]{3,2,1,0:T(8,128)(2,1)S(1)}, bf16[2,4,72,832]{3,2,1,0:T(8,128)(2,1)S(1)}, u32[]{:S(2)}, u32[]{:S(2)}) collective-permute-start(bf16[2,4,72,832]{3,2,1,0:T(8,128)(2,1)S(1)} %grad_w_other.1), channel_id=1, source_target_pairs={{0,1},{1,0},{2,3},{3,2},{4,5},{5,4},{6,7},{7,6},{8,9},{9,8},{10,11... | collective-permute-start | bytes 2875400 | tf_op jit(solution)/shard_map/ppermute | solution.py:375
  58.5 14.7 %collective-permute-start.14 = (bf16[4,72,896]{2,1,0:T(8,128)(2,1)S(1)}, bf16[4,72,896]{2,1,0:T(8,128)(2,1)S(1)}, u32[]{:S(2)}, u32[]{:S(2)}) collective-permute-start(bf16[4,72,896]{2,1,0:T(8,128)(2,1)S(1)} %grad_w_rows.5), channel_id=1, source_target_pairs={{0,2},{1,3},{2,0},{3,1},{4,6},{5,7},{6,4},{7,5},{8,10},{9,11},{10,... | collective-permute-start | bytes 1548296 | tf_op jit(solution)/shard_map/ppermute | solution.py:375
  62.5 15.2 %collective-permute-start.16 = (bf16[4,2,32,1152]{3,2,1,0:T(8,128)(2,1)S(1)}, bf16[4,2,32,1152]{3,2,1,0:T(8,128)(2,1)S(1)}, u32[]{:S(2)}, u32[]{:S(2)}) collective-permute-start(bf16[4,2,32,1152]{3,2,1,0:T(8,128)(2,1)S(1)} %get-tuple-element.74), channel_id=1, source_target_pairs={{0,4},{4,0},{8,12},{12,8},{16,20},{20,16},{24,28},{28,24},{1,5},{5... | collective-permute-start | bytes 1769480 | tf_op jit(solution)/shard_map/ppermute | solution.py:378
  64.7 18.7 %collective-permute-start.21 = (bf16[4,72,832]{2,1,0:T(8,128)(2,1)S(1)}, bf16[4,72,832]{2,1,0:T(8,128)(2,1)S(1)}, u32[]{:S(2)}, u32[]{:S(2)}) collective-permute-start(bf16[4,72,832]{2,1,0:T(8,128)(2,1)S(1)} %grad_w_rows.6), channel_id=1, source_target_pairs={{0,2},{1,3},{2,0},{3,1},{4,6},{5,7},{6,4},{7,5},{8,10},{9,11},{10,... | collective-permute-start | bytes 1437704 | tf_op jit(solution)/shard_map/ppermute | solution.py:375
  73.3 6.7 %collective-permute-start.15 = (bf16[2,72,896]{2,1,0:T(8,128)(2,1)S(1)}, bf16[2,72,896]{2,1,0:T(8,128)(2,1)S(1)}, u32[]{:S(2)}, u32[]{:S(2)}) collective-permute-start(bf16[2,72,896]{2,1,0:T(8,128)(2,1)S(1)} %get-tuple-element.73), channel_id=1, source_target_pairs={{0,8},{4,12},{8,0},{12,4},{16,24},{20,28},{24,16},{28,20},{1,9},{5... | collective-permute-start | bytes 774152 | tf_op jit(solution)/shard_map/ppermute | solution.py:381
  80.0 7.4 %collective-permute-start.22 = (bf16[72,896]{1,0:T(8,128)(2,1)S(1)}, bf16[72,896]{1,0:T(8,128)(2,1)S(1)}, u32[]{:S(2)}, u32[]{:S(2)}) collective-permute-start(bf16[72,896]{1,0:T(8,128)(2,1)S(1)} %get-tuple-element.83), channel_id=1, source_target_pairs={{0,16},{4,20},{8,24},{12,28},{16,0},{20,4},{24,8},{28,12},{1,17},{... | collective-permute-start | bytes 387080 | tf_op jit(solution)/shard_map/ppermute | solution.py:381
  87.5 11.5 %collective-permute-start.23 = (bf16[2,72,832]{2,1,0:T(8,128)(2,1)S(1)}, bf16[2,72,832]{2,1,0:T(8,128)(2,1)S(1)}, u32[]{:S(2)}, u32[]{:S(2)}) collective-permute-start(bf16[2,72,832]{2,1,0:T(8,128)(2,1)S(1)} %get-tuple-element.87), channel_id=1, source_target_pairs={{0,8},{4,12},{8,0},{12,4},{16,24},{20,28},{24,16},{28,20},{1,9},{5... | collective-permute-start | bytes 718856 | tf_op jit(solution)/shard_map/ppermute | solution.py:381
  88.0 11.2 %collective-permute-start.25 = (bf16[72,896]{1,0:T(8,128)(2,1)S(1)}, bf16[72,896]{1,0:T(8,128)(2,1)S(1)}, u32[]{:S(2)}, u32[]{:S(2)}) collective-permute-start(bf16[72,896]{1,0:T(8,128)(2,1)S(1)} %sum_z.2.refs_0_), channel_id=1, source_target_pairs={{0,16},{4,20},{8,24},{12,28},{16,0},{20,4},{24,8},{28,12},{1,17},{... | collective-permute-start | bytes 387080 | tf_op jit(solution)/shard_map/ppermute | solution.py:381
  90.3 14.6 %collective-permute-start.28 = (bf16[72,896]{1,0:T(8,128)(2,1)S(1)}, bf16[72,896]{1,0:T(8,128)(2,1)S(1)}, u32[]{:S(2)}, u32[]{:S(2)}) collective-permute-start(bf16[72,896]{1,0:T(8,128)(2,1)S(1)} %sum_z.2.refs_0_), channel_id=1, source_target_pairs={{0,4},{4,0},{8,12},{12,8},{16,20},{20,16},{24,28},{28,24},{1,5},{5... | collective-permute-start | bytes 387080 | tf_op jit(solution)/shard_map/ppermute | solution.py:378
  92.3 12.6 %collective-permute-start.27 = (bf16[72,896]{1,0:T(8,128)(2,1)S(1)}, bf16[72,896]{1,0:T(8,128)(2,1)S(1)}, u32[]{:S(2)}, u32[]{:S(2)}) collective-permute-start(bf16[72,896]{1,0:T(8,128)(2,1)S(1)} %sum_z.2.refs_0_), channel_id=1, source_target_pairs={{0,8},{4,12},{8,0},{12,4},{16,24},{20,28},{24,16},{28,20},{1,9},{5... | collective-permute-start | bytes 387080 | tf_op jit(solution)/shard_map/ppermute | solution.py:381
  99.1 8.2 %collective-permute-start.26 = (bf16[72,896]{1,0:T(8,128)(2,1)S(1)}, bf16[72,896]{1,0:T(8,128)(2,1)S(1)}, u32[]{:S(2)}, u32[]{:S(2)}) collective-permute-start(bf16[72,896]{1,0:T(8,128)(2,1)S(1)} %collective-permute-done.25.refs_1_.refs_2_), channel_id=1, source_target_pairs={{0,8},{4,12},{8,0},{12,4},{16,24},{20,28},{24,16},{28,20},{1,9},{5... | collective-permute-start | bytes 387080 | tf_op jit(solution)/shard_map/ppermute | solution.py:381
  100.2 7.2 %collective-permute-start.24 = (bf16[72,832]{1,0:T(8,128)(2,1)S(1)}, bf16[72,832]{1,0:T(8,128)(2,1)S(1)}, u32[]{:S(2)}, u32[]{:S(2)}) collective-permute-start(bf16[72,832]{1,0:T(8,128)(2,1)S(1)} %get-tuple-element.88), channel_id=1, source_target_pairs={{0,16},{4,20},{8,24},{12,28},{16,0},{20,4},{24,8},{28,12},{1,17},{... | collective-permute-start | bytes 359432 | tf_op jit(solution)/shard_map/ppermute | solution.py:381
  107.5 9.5 %collective-permute-start.34 = (bf16[88,832]{1,0:T(8,128)(2,1)S(1)}, bf16[88,832]{1,0:T(8,128)(2,1)S(1)}, u32[]{:S(2)}, u32[]{:S(2)}) collective-permute-start(bf16[88,832]{1,0:T(8,128)(2,1)S(1)} %sum_z.3.refs_6_), channel_id=1, source_target_pairs={{0,16},{4,20},{8,24},{12,28},{16,0},{20,4},{24,8},{28,12},{1,17},{... | collective-permute-start | bytes 439304 | tf_op jit(solution)/shard_map/ppermute | solution.py:381
  108.3 9.6 %collective-permute-start.33 = (bf16[88,832]{1,0:T(8,128)(2,1)S(1)}, bf16[88,832]{1,0:T(8,128)(2,1)S(1)}, u32[]{:S(2)}, u32[]{:S(2)}) collective-permute-start(bf16[88,832]{1,0:T(8,128)(2,1)S(1)} %sum_z.3.refs_6_), channel_id=1, source_target_pairs={{0,8},{4,12},{8,0},{12,4},{16,24},{20,28},{24,16},{28,20},{1,9},{5... | collective-permute-start | bytes 439304 | tf_op jit(solution)/shard_map/ppermute | solution.py:381
  110.2 7.7 %collective-permute-start.32 = (bf16[88,832]{1,0:T(8,128)(2,1)S(1)}, bf16[88,832]{1,0:T(8,128)(2,1)S(1)}, u32[]{:S(2)}, u32[]{:S(2)}) collective-permute-start(bf16[88,832]{1,0:T(8,128)(2,1)S(1)} %sum_z.3.refs_6_), channel_id=1, source_target_pairs={{0,4},{4,0},{8,12},{12,8},{16,20},{20,16},{24,28},{28,24},{1,5},{5... | collective-permute-start | bytes 439304 | tf_op jit(solution)/shard_map/ppermute | solution.py:378
  112.0 21.4 %collective-permute-start.31 = (bf16[3,72,896]{2,1,0:T(8,128)(2,1)S(1)}, bf16[3,72,896]{2,1,0:T(8,128)(2,1)S(1)}, u32[]{:S(2)}, u32[]{:S(2)}) collective-permute-start(bf16[3,72,896]{2,1,0:T(8,128)(2,1)S(1)} %stack.1), channel_id=1, source_target_pairs={{0,4},{4,0},{8,12},{12,8},{16,20},{20,16},{24,28},{28,24},{1,5},{5... | collective-permute-start | bytes 1161224 | tf_op jit(solution)/shard_map/ppermute | solution.py:378
  112.4 9.0 %collective-permute-start.17 = (bf16[2,32,1152]{2,1,0:T(8,128)(2,1)S(1)}, bf16[2,32,1152]{2,1,0:T(8,128)(2,1)S(1)}, u32[]{:S(2)}, u32[]{:S(2)}) collective-permute-start(bf16[2,32,1152]{2,1,0:T(8,128)(2,1)S(1)} %get-tuple-element.77), channel_id=1, source_target_pairs={{0,8},{4,12},{8,0},{12,4},{16,24},{20,28},{24,16},{28,20},{1,9},{5... | collective-permute-start | bytes 442376 | tf_op jit(solution)/shard_map/ppermute | solution.py:381
  117.0 10.6 %collective-permute-start.18 = (bf16[2,32,1152]{2,1,0:T(8,128)(2,1)S(1)}, bf16[2,32,1152]{2,1,0:T(8,128)(2,1)S(1)}, u32[]{:S(2)}, u32[]{:S(2)}) collective-permute-start(bf16[2,32,1152]{2,1,0:T(8,128)(2,1)S(1)} %get-tuple-element.78), channel_id=1, source_target_pairs={{0,16},{4,20},{8,24},{12,28},{16,0},{20,4},{24,8},{28,12},{1,17},{... | collective-permute-start | bytes 442376 | tf_op jit(solution)/shard_map/ppermute | solution.py:381
  117.9 11.6 %collective-permute-start.35 = (bf16[88,832]{1,0:T(8,128)(2,1)S(1)}, bf16[88,832]{1,0:T(8,128)(2,1)S(1)}, u32[]{:S(2)}, u32[]{:S(2)}) collective-permute-start(bf16[88,832]{1,0:T(8,128)(2,1)S(1)} %collective-permute-done.34.refs_8_), channel_id=1, source_target_pairs={{0,8},{4,12},{8,0},{12,4},{16,24},{20,28},{24,16},{28,20},{1,9},{5... | collective-permute-start | bytes 439304 | tf_op jit(solution)/shard_map/ppermute | solution.py:381
  119.0 10.9 %collective-permute-start.19 = (bf16[2,32,1152]{2,1,0:T(8,128)(2,1)S(1)}, bf16[2,32,1152]{2,1,0:T(8,128)(2,1)S(1)}, u32[]{:S(2)}, u32[]{:S(2)}) collective-permute-start(bf16[2,32,1152]{2,1,0:T(8,128)(2,1)S(1)} %get-tuple-element.79), channel_id=1, source_target_pairs={{0,24},{4,28},{8,16},{12,20},{16,8},{20,12},{24,0},{28,4},{1,25},{... | collective-permute-start | bytes 442376 | tf_op jit(solution)/shard_map/ppermute | solution.py:381
  121.4 10.1 %collective-permute-start.36 = (bf16[88,832]{1,0:T(8,128)(2,1)S(1)}, bf16[88,832]{1,0:T(8,128)(2,1)S(1)}, u32[]{:S(2)}, u32[]{:S(2)}) collective-permute-start(bf16[88,832]{1,0:T(8,128)(2,1)S(1)} %collective-permute-done.33.refs_7_), channel_id=1, source_target_pairs={{0,4},{4,0},{8,12},{12,8},{16,20},{20,16},{24,28},{28,24},{1,5},{5... | collective-permute-start | bytes 439304 | tf_op jit(solution)/shard_map/ppermute | solution.py:378
  (11 other events, 45.0 us)

commit v7 on v6

--- a/solution.py
+++ b/solution.py
@@ -113,8 +113,12 @@
             send[k][b, :, :width] = normed.astype(BF16)
             up = c_ref[b, rows, :].astype(F32)
             low, high = up[:, :half], up[:, half:]
-            send[k][b, :, width:] = pick(y == 0, high, low).astype(BF16)
-            keep[k][b] = pick(y == 0, low, high).astype(BF16)
+            send[k][b, :, width : width + half] = pick(y == 0, high, low).astype(BF16)
+            mine = pick(y == 0, low, high).astype(BF16)
+            if k in (0, groups - 1):
+                keep[k > 0][b] = mine
+            else:
+                send[k][b, :, width + half :] = mine
 
 
 def join_kernel(shares, *refs):
@@ -131,8 +135,8 @@
 
 
 def main_kernel(groups, share, cuts, *refs):
-    near, kept, far = refs[:groups], refs[groups : 2 * groups], refs[2 * groups : 3 * groups]
-    w, table, *rest = refs[3 * groups :]
+    near, far, kept = refs[:groups], refs[groups : 2 * groups], refs[2 * groups : 2 * groups + 2]
+    w, table, *rest = refs[2 * groups + 2 :]
     outs, scratches = rest[: 3 + len(cuts[:1])], rest[3 + len(cuts[:1]) :]
     grads, mod_t, normed = outs[:3]
     mod, up, qw, kw, vw, dq, dk, dv = scratches
@@ -148,8 +152,8 @@
         shift, scale, loss = table[b, 0:1, :], 1.0 + table[b, 1:2, :], table[b, 2:3, :half]
         for k in range(groups):
             for at, ref, tangent in (
-                (k, near[k], kept[k][b]),
-                (groups + k, far[k], far[k][b, :, depth:]),
+                (k, near[k], kept[k > 0][b] if k in (0, groups - 1) else near[k][b, :, depth + half :]),
+                (groups + k, far[k], far[k][b, :, depth : depth + half]),
             ):
                 modulated = (ref[b, :, :depth].astype(F32) * scale + shift).astype(BF16)
                 upstream = (tangent.astype(F32) * loss).astype(BF16)
@@ -399,7 +403,8 @@
     prep = call(
         functools.partial(prep_kernel, groups),
         "prep",
-        [shape((clips, chunk, width + half))] * groups + [shape((clips, chunk, half))] * groups,
+        [shape((clips, chunk, width + half if k in (0, groups - 1) else 2 * width)) for k in range(groups)]
+        + [shape((clips, chunk, half))] * 2,
         [VMEM] * 2,
         moved=3 << 20,
     )(after(hidden, w_half), cotangent)
@@ -409,7 +414,7 @@
     for k in range(1, groups):
         near[k] = after(near[k], far[-1])
         far.append(over_y(near[k]))
-    kept = [keep[0]] + [over_z(keep[k], k) for k in range(1, groups)]
+    kept = [keep[0], over_z(keep[1], groups - 1)]
     if pieces:
         weights = [w_half, over_space(w_half, 1)]
         for x in crossed:
@@ -433,7 +438,7 @@
         functools.partial(main_kernel, groups, share, cuts),
         "attend",
         outs,
-        [VMEM] * (3 * groups + 2),
+        [VMEM] * (2 * groups + 4),
         [
             pltpu.VMEM((tokens, width), BF16),
             pltpu.VMEM((tokens, pad), BF16),
@@ -446,7 +451,7 @@
         ],
         flops=2 * tokens * width * wide * 3,
         moved=20 << 20,
-    )(*near, *kept, *far, weights, modulation)
+    )(*near, *far, *kept, weights, modulation)
     grads, mod_t, normed = main[:3]
 
     far_hidden, near_hidden, sums = call(

time: 138 us -> 140 us (1.014)
  waiting for transfers between devices: 60.9 us -> 66 us
  starting transfers between devices: 50.7 us -> 47.8 us
    ppermute x11, starting transfers between devices: 14.6 us -> 12.3 us  [over_y(): return lax.ppermute(x, 'frame', [(i, i ^ 1) for i in range(frames)])]
    ppermute x19 -> x17, waiting for transfers between devices: 34.8 us -> 37 us  [over_z(): return lax.ppermute(x, 'frame', [(i, i ^ 2 * step) for i in range(frames)])]
    ppermute x11, waiting for transfers between devices: 14.2 us -> 16.2 us  [over_y(): return lax.ppermute(x, 'frame', [(i, i ^ 1) for i in range(frames)])]
    ppermute x19 -> x17, starting transfers between devices: 28.5 us -> 27.9 us  [over_z(): return lax.ppermute(x, 'frame', [(i, i ^ 2 * step) for i in range(frames)])]
  transfers between devices with their start and end apart: 39 -> 37, of which waited for: 20 -> 21; matrix products, arithmetic and copies ran while one was open for 0% -> 0% of each run, Pallas kernels for 8% -> 8%
where the time goes in v7:
time: 140 us
  waiting for transfers between devices  66 us (47%)
  starting transfers between devices  47.8 us (34%)
  Pallas kernels  25.6 us (18%)
    ppermute x17, waiting for transfers between devices, over_z(): return lax.ppermute(x, 'frame', [(i, i ^ 2 * step) for i in range(frames)])  37 us
    ppermute x17, starting transfers between devices, over_z(): return lax.ppermute(x, 'frame', [(i, i ^ 2 * step) for i in range(frames)])  27.9 us
    ppermute x11, waiting for transfers between devices, over_y(): return lax.ppermute(x, 'frame', [(i, i ^ 1) for i in range(frames)])  16.2 us
    ppermute x9, waiting for transfers between devices, over_space(): return lax.ppermute(x, 'space', [(i, i ^ step) for i in range(spaces)])  12.8 us
    ppermute x11, starting transfers between devices, over_y(): return lax.ppermute(x, 'frame', [(i, i ^ 1) for i in range(frames)])  12.3 us
    pallas_call x1, Pallas kernels, per_device(): call(functools.partial(main_kernel, groups, share, cuts), 'attend', outs,...  9.64 us
    ppermute x9, starting transfers between devices, over_space(): return lax.ppermute(x, 'space', [(i, i ^ step) for i in range(spaces)])  7.59 us
  transfers between devices with their start and end apart: 37, of which 21 were waited for; matrix products, arithmetic and copies ran while one was open for 0% of the time, Pallas kernels for 8%

profile of v7, /device:TPU:0, one launch (start us, length us, event | category | flops | bytes accessed | tf_op | source)
XLA Modules:
  0.0 140.3 jit_solution(7185812105263057902)
XLA Ops:
  0.6 2.2 %lookup.1.refs_11_.mod_ref = f32[2,3,1152]{2,1,0:T(4,128)} custom-call(bf16[1000,2,1152]{2,1,0:T(2,128)(2,1)} %tab_ref.1, s32[2]{0:T(128)} %ts_ref.1, f32[1000]{0:T(1024)} %snr_ref.1, s32[2]{0:T(128)} %wi_ref.1), custom_call_target="tpu_custom_call" | custom-call | bytes 1048576 | tf_op jit(solution)/shard_map/lookup/pallas_call | solution.py:390
  3.1 3.0 %collective-permute-start.8 = (bf16[288,1728]{1,0:T(8,128)(2,1)S(1)}, bf16[288,1728]{1,0:T(8,128)(2,1)S(1)}, u32[]{:S(2)}, u32[]{:S(2)}) collective-permute-start(bf16[288,1728]{1,0:T(8,128)(2,1)S(1)} %w_half.1.refs_0_), channel_id=1, source_target_pairs={{0,2},{1,3},{2,0},{3,1},{4,6},{5,7},{6,4},{7,5},{8,10},{9,11},{10,... | collective-permute-start | bytes 2985992 | tf_op jit(solution)/shard_map/ppermute | solution.py:379
  11.1 2.6 %collective-permute-start.2 = (bf16[2,32,2304]{2,1,0:T(8,128)(2,1)S(1)}, bf16[2,32,2304]{2,1,0:T(8,128)(2,1)S(1)}, u32[]{:S(2)}, u32[]{:S(2)}) collective-permute-start(bf16[2,32,2304]{2,1,0:T(8,128)(2,1)S(1)} %get-tuple-element.56), channel_id=1, source_target_pairs={{0,16},{4,20},{8,24},{12,28},{16,0},{20,4},{24,8},{28,12},{1,17},{... | collective-permute-start | bytes 884744 | tf_op jit(solution)/shard_map/ppermute | solution.py:385
  13.7 2.6 %collective-permute-done.1.refs_4_ = bf16[2,32,1728]{2,1,0:T(8,128)(2,1)S(1)} collective-permute-done((bf16[2,32,1728]{2,1,0:T(8,128)(2,1)S(1)}, bf16[2,32,1728]{2,1,0:T(8,128)(2,1)S(1)}, u32[]{:S(2)}, u32[]{:S(2)}) %collective-permute-start.1) | collective-permute-done | bytes 221216 | tf_op jit(solution)/shard_map/ppermute | solution.py:382
  16.3 5.0 %collective-permute-done.refs_1_ = bf16[2,32,2304]{2,1,0:T(8,128)(2,1)S(1)} collective-permute-done((bf16[2,32,2304]{2,1,0:T(8,128)(2,1)S(1)}, bf16[2,32,2304]{2,1,0:T(8,128)(2,1)S(1)}, u32[]{:S(2)}, u32[]{:S(2)}) %collective-permute-start) | collective-permute-done | bytes 294944 | tf_op jit(solution)/shard_map/ppermute | solution.py:385
  21.2 2.8 %collective-permute-start.3 = (bf16[2,32,2304]{2,1,0:T(8,128)(2,1)S(1)}, bf16[2,32,2304]{2,1,0:T(8,128)(2,1)S(1)}, u32[]{:S(2)}, u32[]{:S(2)}) collective-permute-start(bf16[2,32,2304]{2,1,0:T(8,128)(2,1)S(1)} %collective-permute-done.refs_1_), channel_id=1, source_target_pairs={{0,4},{4,0},{8,12},{12,8},{16,20},{20,16},{24,28},{28,24},{1,5},{5... | collective-permute-start | bytes 884744 | tf_op jit(solution)/shard_map/ppermute | solution.py:382
  24.1 2.2 %collective-permute-done.2.refs_2_ = bf16[2,32,2304]{2,1,0:T(8,128)(2,1)S(1)} collective-permute-done((bf16[2,32,2304]{2,1,0:T(8,128)(2,1)S(1)}, bf16[2,32,2304]{2,1,0:T(8,128)(2,1)S(1)}, u32[]{:S(2)}, u32[]{:S(2)}) %collective-permute-start.2) | collective-permute-done | bytes 294944 | tf_op jit(solution)/shard_map/ppermute | solution.py:385
  26.3 3.6 %collective-permute-done.3.refs_5_ = bf16[2,32,2304]{2,1,0:T(8,128)(2,1)S(1)} collective-permute-done((bf16[2,32,2304]{2,1,0:T(8,128)(2,1)S(1)}, bf16[2,32,2304]{2,1,0:T(8,128)(2,1)S(1)}, u32[]{:S(2)}, u32[]{:S(2)}) %collective-permute-start.3) | collective-permute-done | bytes 294944 | tf_op jit(solution)/shard_map/ppermute | solution.py:382
  31.6 2.6 %collective-permute-start.4 = (bf16[2,32,1728]{2,1,0:T(8,128)(2,1)S(1)}, bf16[2,32,1728]{2,1,0:T(8,128)(2,1)S(1)}, u32[]{:S(2)}, u32[]{:S(2)}) collective-permute-start(bf16[2,32,1728]{2,1,0:T(8,128)(2,1)S(1)} %get-tuple-element.58), channel_id=1, source_target_pairs={{0,24},{4,28},{8,16},{12,20},{16,8},{20,12},{24,0},{28,4},{1,25},{... | collective-permute-start | bytes 663560 | tf_op jit(solution)/shard_map/ppermute | solution.py:385
  34.2 5.3 %collective-permute-done.4.refs_3_ = bf16[2,32,1728]{2,1,0:T(8,128)(2,1)S(1)} collective-permute-done((bf16[2,32,1728]{2,1,0:T(8,128)(2,1)S(1)}, bf16[2,32,1728]{2,1,0:T(8,128)(2,1)S(1)}, u32[]{:S(2)}, u32[]{:S(2)}) %collective-permute-start.4) | collective-permute-done | bytes 221216 | tf_op jit(solution)/shard_map/ppermute | solution.py:385
  39.9 2.6 %collective-permute-start.10 = (bf16[2,32,576]{2,1,0:T(8,128)(2,1)S(1)}, bf16[2,32,576]{2,1,0:T(8,128)(2,1)S(1)}, u32[]{:S(2)}, u32[]{:S(2)}) collective-permute-start(bf16[2,32,576]{2,1,0:T(8,128)(2,1)S(1)} %get-tuple-element.63), channel_id=1, source_target_pairs={{0,24},{4,28},{8,16},{12,20},{16,8},{20,12},{24,0},{28,4},{1,25},{... | collective-permute-start | bytes 221192 | tf_op jit(solution)/shard_map/ppermute | solution.py:385
  44.0 3.5 %collective-permute-done.6.refs_7_ = bf16[2,32,1728]{2,1,0:T(8,128)(2,1)S(1)} collective-permute-done((bf16[2,32,1728]{2,1,0:T(8,128)(2,1)S(1)}, bf16[2,32,1728]{2,1,0:T(8,128)(2,1)S(1)}, u32[]{:S(2)}, u32[]{:S(2)}) %collective-permute-start.6) | collective-permute-done | bytes 221216 | tf_op jit(solution)/shard_map/ppermute | solution.py:382
  47.6 9.6 %attend.1 = (bf16[512,1728]{1,0:T(8,128)(2,1)S(1)}, bf16[1152,512]{1,0:T(8,128)(2,1)S(1)}, bf16[512,1152]{1,0:T(8,128)(2,1)S(1)}, bf16[2,4,72,896]{3,2,1,0:T(8,128)(2,1)S(1)}) custom-call(bf16[2,32,1728]{2,1,0:T(8,128)(2,1)S(1)} %get-tuple-element.53.refs_0_, bf16[2,32,2304]{2,1,0:T(8,128)(2,1)S(1)} %collective-permute-done.refs_1_, ...), custom_call_target="tpu_custom_call" | custom-call | flops 6115295232 | bytes 20971520 | tf_op jit(solution)/shard_map/attend/pallas_call | solution.py:437
  61.8 2.7 %grad_hidden.1 = (bf16[4,2,32,1152]{3,2,1,0:T(8,128)(2,1)S(1)}, bf16[4,2,32,1152]{3,2,1,0:T(8,128)(2,1)S(1)}, f32[2,2,1152]{2,1,0:T(2,128)S(1)}) custom-call(bf16[512,1728]{1,0:T(8,128)(2,1)S(1)} %get-tuple-element.64.grads, bf16[512,1152]{1,0:T(8,128)(2,1)S(1)} %get-tuple-element.65.normed, bf16[1152,1728]{1,0:T(8,128)(2,1)S(1)} %join_w.1.refs_10_.w), custom_call_target="tpu_custom_call" | custom-call | flops 2038431744 | bytes 8388608 | tf_op jit(solution)/shard_map/grad_hidden/pallas_call | solution.py:457
  66.8 8.3 %collective-permute-done.12.got = bf16[4,72,896]{2,1,0:T(8,128)(2,1)S(1)} collective-permute-done((bf16[4,72,896]{2,1,0:T(8,128)(2,1)S(1)}, bf16[4,72,896]{2,1,0:T(8,128)(2,1)S(1)}, u32[]{:S(2)}, u32[]{:S(2)}) %collective-permute-start.12) | collective-permute-done | bytes 516128 | tf_op jit(solution)/shard_map/ppermute | solution.py:379
  75.2 1.9 %collective-permute-start.13 = (bf16[2,72,896]{2,1,0:T(8,128)(2,1)S(1)}, bf16[2,72,896]{2,1,0:T(8,128)(2,1)S(1)}, u32[]{:S(2)}, u32[]{:S(2)}) collective-permute-start(bf16[2,72,896]{2,1,0:T(8,128)(2,1)S(1)} %get-tuple-element.69), channel_id=1, source_target_pairs={{0,8},{4,12},{8,0},{12,4},{16,24},{20,28},{24,16},{28,20},{1,9},{5... | collective-permute-start | bytes 774152 | tf_op jit(solution)/shard_map/ppermute | solution.py:385
  77.1 2.6 %collective-permute-done.14.got = bf16[4,2,32,1152]{3,2,1,0:T(8,128)(2,1)S(1)} collective-permute-done((bf16[4,2,32,1152]{3,2,1,0:T(8,128)(2,1)S(1)}, bf16[4,2,32,1152]{3,2,1,0:T(8,128)(2,1)S(1)}, u32[]{:S(2)}, u32[]{:S(2)}) %collective-permute-start.14) | collective-permute-done | bytes 589856 | tf_op jit(solution)/shard_map/ppermute | solution.py:382
  79.7 2.3 %collective-permute-done.13.got = bf16[2,72,896]{2,1,0:T(8,128)(2,1)S(1)} collective-permute-done((bf16[2,72,896]{2,1,0:T(8,128)(2,1)S(1)}, bf16[2,72,896]{2,1,0:T(8,128)(2,1)S(1)}, u32[]{:S(2)}, u32[]{:S(2)}) %collective-permute-start.13) | collective-permute-done | bytes 258080 | tf_op jit(solution)/shard_map/ppermute | solution.py:385
  82.1 3.0 %collective-permute-start.20 = (bf16[72,896]{1,0:T(8,128)(2,1)S(1)}, bf16[72,896]{1,0:T(8,128)(2,1)S(1)}, u32[]{:S(2)}, u32[]{:S(2)}) collective-permute-start(bf16[72,896]{1,0:T(8,128)(2,1)S(1)} %get-tuple-element.79), channel_id=1, source_target_pairs={{0,16},{4,20},{8,24},{12,28},{16,0},{20,4},{24,8},{28,12},{1,17},{... | collective-permute-start | bytes 387080 | tf_op jit(solution)/shard_map/ppermute | solution.py:385
  85.6 3.9 %collective-permute-done.20.refs_1_ = bf16[72,896]{1,0:T(8,128)(2,1)S(1)} collective-permute-done((bf16[72,896]{1,0:T(8,128)(2,1)S(1)}, bf16[72,896]{1,0:T(8,128)(2,1)S(1)}, u32[]{:S(2)}, u32[]{:S(2)}) %collective-permute-start.20) | collective-permute-done | bytes 129056 | tf_op jit(solution)/shard_map/ppermute | solution.py:385
  90.0 2.2 %collective-permute-start.23 = (bf16[72,896]{1,0:T(8,128)(2,1)S(1)}, bf16[72,896]{1,0:T(8,128)(2,1)S(1)}, u32[]{:S(2)}, u32[]{:S(2)}) collective-permute-start(bf16[72,896]{1,0:T(8,128)(2,1)S(1)} %sum_z.2.refs_0_), channel_id=1, source_target_pairs={{0,16},{4,20},{8,24},{12,28},{16,0},{20,4},{24,8},{28,12},{1,17},{... | collective-permute-start | bytes 387080 | tf_op jit(solution)/shard_map/ppermute | solution.py:385
  92.8 1.8 %collective-permute-start.25 = (bf16[72,896]{1,0:T(8,128)(2,1)S(1)}, bf16[72,896]{1,0:T(8,128)(2,1)S(1)}, u32[]{:S(2)}, u32[]{:S(2)}) collective-permute-start(bf16[72,896]{1,0:T(8,128)(2,1)S(1)} %sum_z.2.refs_0_), channel_id=1, source_target_pairs={{0,8},{4,12},{8,0},{12,4},{16,24},{20,28},{24,16},{28,20},{1,9},{5... | collective-permute-start | bytes 387080 | tf_op jit(solution)/shard_map/ppermute | solution.py:385
  94.6 6.8 %collective-permute-done.21.got = bf16[2,72,832]{2,1,0:T(8,128)(2,1)S(1)} collective-permute-done((bf16[2,72,832]{2,1,0:T(8,128)(2,1)S(1)}, bf16[2,72,832]{2,1,0:T(8,128)(2,1)S(1)}, u32[]{:S(2)}, u32[]{:S(2)}) %collective-permute-start.21) | collective-permute-done | bytes 239648 | tf_op jit(solution)/shard_map/ppermute | solution.py:385
  102.2 2.0 %collective-permute-start.22 = (bf16[72,832]{1,0:T(8,128)(2,1)S(1)}, bf16[72,832]{1,0:T(8,128)(2,1)S(1)}, u32[]{:S(2)}, u32[]{:S(2)}) collective-permute-start(bf16[72,832]{1,0:T(8,128)(2,1)S(1)} %get-tuple-element.84), channel_id=1, source_target_pairs={{0,16},{4,20},{8,24},{12,28},{16,0},{20,4},{24,8},{28,12},{1,17},{... | collective-permute-start | bytes 359432 | tf_op jit(solution)/shard_map/ppermute | solution.py:385
  105.4 1.8 %collective-permute-start.28 = (f32[2,2,1152]{2,1,0:T(2,128)S(1)}, f32[2,2,1152]{2,1,0:T(2,128)S(1)}, u32[]{:S(2)}, u32[]{:S(2)}) collective-permute-start(f32[2,2,1152]{2,1,0:T(2,128)S(1)} %add.3.sums), channel_id=1, source_target_pairs={{0,2},{1,3},{2,0},{3,1},{4,6},{5,7},{6,4},{7,5},{8,10},{9,11},{10,... | collective-permute-start | bytes 55304 | tf_op jit(solution)/shard_map/ppermute | solution.py:379
  107.2 2.0 %collective-permute-done.28.more = f32[2,2,1152]{2,1,0:T(2,128)S(1)} collective-permute-done((f32[2,2,1152]{2,1,0:T(2,128)S(1)}, f32[2,2,1152]{2,1,0:T(2,128)S(1)}, u32[]{:S(2)}, u32[]{:S(2)}) %collective-permute-start.28) | collective-permute-done | bytes 18464 | tf_op jit(solution)/shard_map/ppermute | solution.py:379
  110.3 1.9 %collective-permute-start.31 = (bf16[88,832]{1,0:T(8,128)(2,1)S(1)}, bf16[88,832]{1,0:T(8,128)(2,1)S(1)}, u32[]{:S(2)}, u32[]{:S(2)}) collective-permute-start(bf16[88,832]{1,0:T(8,128)(2,1)S(1)} %sum_z.3.refs_6_), channel_id=1, source_target_pairs={{0,8},{4,12},{8,0},{12,4},{16,24},{20,28},{24,16},{28,20},{1,9},{5... | collective-permute-start | bytes 439304 | tf_op jit(solution)/shard_map/ppermute | solution.py:385
  114.7 4.4 %collective-permute-done.32.refs_8_ = bf16[88,832]{1,0:T(8,128)(2,1)S(1)} collective-permute-done((bf16[88,832]{1,0:T(8,128)(2,1)S(1)}, bf16[88,832]{1,0:T(8,128)(2,1)S(1)}, u32[]{:S(2)}, u32[]{:S(2)}) %collective-permute-start.32) | collective-permute-done | bytes 146464 | tf_op jit(solution)/shard_map/ppermute | solution.py:385
  121.4 2.0 %collective-permute-start.17 = (bf16[2,32,1152]{2,1,0:T(8,128)(2,1)S(1)}, bf16[2,32,1152]{2,1,0:T(8,128)(2,1)S(1)}, u32[]{:S(2)}, u32[]{:S(2)}) collective-permute-start(bf16[2,32,1152]{2,1,0:T(8,128)(2,1)S(1)} %get-tuple-element.75), channel_id=1, source_target_pairs={{0,24},{4,28},{8,16},{12,20},{16,8},{20,12},{24,0},{28,4},{1,25},{... | collective-permute-start | bytes 442376 | tf_op jit(solution)/shard_map/ppermute | solution.py:385
  124.0 5.2 %collective-permute-done.16.refs_2_ = bf16[2,32,1152]{2,1,0:T(8,128)(2,1)S(1)} collective-permute-done((bf16[2,32,1152]{2,1,0:T(8,128)(2,1)S(1)}, bf16[2,32,1152]{2,1,0:T(8,128)(2,1)S(1)}, u32[]{:S(2)}, u32[]{:S(2)}) %collective-permute-start.16) | collective-permute-done | bytes 147488 | tf_op jit(solution)/shard_map/ppermute | solution.py:385
  133.6 2.2 %collective-permute-done.35.refs_12_ = bf16[88,832]{1,0:T(8,128)(2,1)S(1)} collective-permute-done((bf16[88,832]{1,0:T(8,128)(2,1)S(1)}, bf16[88,832]{1,0:T(8,128)(2,1)S(1)}, u32[]{:S(2)}, u32[]{:S(2)}) %collective-permute-start.35) | collective-permute-done | bytes 146464 | tf_op jit(solution)/shard_map/ppermute | solution.py:382
  137.5 2.8 %grad_w.1 = (f32[288,3456]{1,0:T(8,128)}, f32[2,2,1152]{2,1,0:T(2,128)}) custom-call(bf16[72,896]{1,0:T(8,128)(2,1)S(1)} %sum_z.2.refs_0_, bf16[72,896]{1,0:T(8,128)(2,1)S(1)} %collective-permute-done.25.refs_0_.refs_1_, bf16[72,896]{1,0:T(8,128)(2,1)S(1)} %collective-permute-done.23.refs_1_.refs_2_, ...), custom_call_target="tpu_custom_call" | custom-call | bytes 1048576 | tf_op jit(solution)/shard_map/grad_w/pallas_call | solution.py:543
  (72 shorter events, 31.9 us)
Async XLA Ops:
  3.1 36.5 %collective-permute-start.8 = (bf16[288,1728]{1,0:T(8,128)(2,1)S(1)}, bf16[288,1728]{1,0:T(8,128)(2,1)S(1)}, u32[]{:S(2)}, u32[]{:S(2)}) collective-permute-start(bf16[288,1728]{1,0:T(8,128)(2,1)S(1)} %w_half.1.refs_0_), channel_id=1, source_target_pairs={{0,2},{1,3},{2,0},{3,1},{4,6},{5,7},{6,4},{7,5},{8,10},{9,11},{10,... | collective-permute-start | bytes 2985992 | tf_op jit(solution)/shard_map/ppermute | solution.py:379
  7.8 13.4 %collective-permute-start = (bf16[2,32,2304]{2,1,0:T(8,128)(2,1)S(1)}, bf16[2,32,2304]{2,1,0:T(8,128)(2,1)S(1)}, u32[]{:S(2)}, u32[]{:S(2)}) collective-permute-start(bf16[2,32,2304]{2,1,0:T(8,128)(2,1)S(1)} %get-tuple-element.54), channel_id=1, source_target_pairs={{0,8},{4,12},{8,0},{12,4},{16,24},{20,28},{24,16},{28,20},{1,9},{5... | collective-permute-start | bytes 884744 | tf_op jit(solution)/shard_map/ppermute | solution.py:385
  9.5 6.8 %collective-permute-start.1 = (bf16[2,32,1728]{2,1,0:T(8,128)(2,1)S(1)}, bf16[2,32,1728]{2,1,0:T(8,128)(2,1)S(1)}, u32[]{:S(2)}, u32[]{:S(2)}) collective-permute-start(bf16[2,32,1728]{2,1,0:T(8,128)(2,1)S(1)} %get-tuple-element.53.refs_0_), channel_id=1, source_target_pairs={{0,4},{4,0},{8,12},{12,8},{16,20},{20,16},{24,28},{28,24},{1,5},{5... | collective-permute-start | bytes 663560 | tf_op jit(solution)/shard_map/ppermute | solution.py:382
  11.1 15.2 %collective-permute-start.2 = (bf16[2,32,2304]{2,1,0:T(8,128)(2,1)S(1)}, bf16[2,32,2304]{2,1,0:T(8,128)(2,1)S(1)}, u32[]{:S(2)}, u32[]{:S(2)}) collective-permute-start(bf16[2,32,2304]{2,1,0:T(8,128)(2,1)S(1)} %get-tuple-element.56), channel_id=1, source_target_pairs={{0,16},{4,20},{8,24},{12,28},{16,0},{20,4},{24,8},{28,12},{1,17},{... | collective-permute-start | bytes 884744 | tf_op jit(solution)/shard_map/ppermute | solution.py:385
  21.2 8.6 %collective-permute-start.3 = (bf16[2,32,2304]{2,1,0:T(8,128)(2,1)S(1)}, bf16[2,32,2304]{2,1,0:T(8,128)(2,1)S(1)}, u32[]{:S(2)}, u32[]{:S(2)}) collective-permute-start(bf16[2,32,2304]{2,1,0:T(8,128)(2,1)S(1)} %collective-permute-done.refs_1_), channel_id=1, source_target_pairs={{0,4},{4,0},{8,12},{12,8},{16,20},{20,16},{24,28},{28,24},{1,5},{5... | collective-permute-start | bytes 884744 | tf_op jit(solution)/shard_map/ppermute | solution.py:382
  29.9 9.7 %collective-permute-start.5 = (bf16[2,32,2304]{2,1,0:T(8,128)(2,1)S(1)}, bf16[2,32,2304]{2,1,0:T(8,128)(2,1)S(1)}, u32[]{:S(2)}, u32[]{:S(2)}) collective-permute-start(bf16[2,32,2304]{2,1,0:T(8,128)(2,1)S(1)} %collective-permute-done.2.refs_2_), channel_id=1, source_target_pairs={{0,4},{4,0},{8,12},{12,8},{16,20},{20,16},{24,28},{28,24},{1,5},{5... | collective-permute-start | bytes 884744 | tf_op jit(solution)/shard_map/ppermute | solution.py:382
  31.6 7.9 %collective-permute-start.4 = (bf16[2,32,1728]{2,1,0:T(8,128)(2,1)S(1)}, bf16[2,32,1728]{2,1,0:T(8,128)(2,1)S(1)}, u32[]{:S(2)}, u32[]{:S(2)}) collective-permute-start(bf16[2,32,1728]{2,1,0:T(8,128)(2,1)S(1)} %get-tuple-element.58), channel_id=1, source_target_pairs={{0,24},{4,28},{8,16},{12,20},{16,8},{20,12},{24,0},{28,4},{1,25},{... | collective-permute-start | bytes 663560 | tf_op jit(solution)/shard_map/ppermute | solution.py:385
  34.2 8.3 %collective-permute-start.7 = (bf16[288,1728]{1,0:T(8,128)(2,1)S(1)}, bf16[288,1728]{1,0:T(8,128)(2,1)S(1)}, u32[]{:S(2)}, u32[]{:S(2)}) collective-permute-start(bf16[288,1728]{1,0:T(8,128)(2,1)S(1)} %w_half.1.refs_0_), channel_id=1, source_target_pairs={{0,1},{1,0},{2,3},{3,2},{4,5},{5,4},{6,7},{7,6},{8,9},{9,8},{10,11... | collective-permute-start | bytes 2985992 | tf_op jit(solution)/shard_map/ppermute | solution.py:379
  39.6 8.0 %collective-permute-start.6 = (bf16[2,32,1728]{2,1,0:T(8,128)(2,1)S(1)}, bf16[2,32,1728]{2,1,0:T(8,128)(2,1)S(1)}, u32[]{:S(2)}, u32[]{:S(2)}) collective-permute-start(bf16[2,32,1728]{2,1,0:T(8,128)(2,1)S(1)} %collective-permute-done.4.refs_3_), channel_id=1, source_target_pairs={{0,4},{4,0},{8,12},{12,8},{16,20},{20,16},{24,28},{28,24},{1,5},{5... | collective-permute-start | bytes 663560 | tf_op jit(solution)/shard_map/ppermute | solution.py:382
  39.9 7.7 %collective-permute-start.10 = (bf16[2,32,576]{2,1,0:T(8,128)(2,1)S(1)}, bf16[2,32,576]{2,1,0:T(8,128)(2,1)S(1)}, u32[]{:S(2)}, u32[]{:S(2)}) collective-permute-start(bf16[2,32,576]{2,1,0:T(8,128)(2,1)S(1)} %get-tuple-element.63), channel_id=1, source_target_pairs={{0,24},{4,28},{8,16},{12,20},{16,8},{20,12},{24,0},{28,4},{1,25},{... | collective-permute-start | bytes 221192 | tf_op jit(solution)/shard_map/ppermute | solution.py:385
  58.1 7.0 %collective-permute-start.18 = (bf16[2,4,72,832]{3,2,1,0:T(8,128)(2,1)S(1)}, bf16[2,4,72,832]{3,2,1,0:T(8,128)(2,1)S(1)}, u32[]{:S(2)}, u32[]{:S(2)}) collective-permute-start(bf16[2,4,72,832]{3,2,1,0:T(8,128)(2,1)S(1)} %grad_w_other.1), channel_id=1, source_target_pairs={{0,1},{1,0},{2,3},{3,2},{4,5},{5,4},{6,7},{7,6},{8,9},{9,8},{10,11... | collective-permute-start | bytes 2875400 | tf_op jit(solution)/shard_map/ppermute | solution.py:379
  60.4 14.7 %collective-permute-start.12 = (bf16[4,72,896]{2,1,0:T(8,128)(2,1)S(1)}, bf16[4,72,896]{2,1,0:T(8,128)(2,1)S(1)}, u32[]{:S(2)}, u32[]{:S(2)}) collective-permute-start(bf16[4,72,896]{2,1,0:T(8,128)(2,1)S(1)} %grad_w_rows.5), channel_id=1, source_target_pairs={{0,2},{1,3},{2,0},{3,1},{4,6},{5,7},{6,4},{7,5},{8,10},{9,11},{10,... | collective-permute-start | bytes 1548296 | tf_op jit(solution)/shard_map/ppermute | solution.py:379
  64.5 15.1 %collective-permute-start.14 = (bf16[4,2,32,1152]{3,2,1,0:T(8,128)(2,1)S(1)}, bf16[4,2,32,1152]{3,2,1,0:T(8,128)(2,1)S(1)}, u32[]{:S(2)}, u32[]{:S(2)}) collective-permute-start(bf16[4,2,32,1152]{3,2,1,0:T(8,128)(2,1)S(1)} %get-tuple-element.70), channel_id=1, source_target_pairs={{0,4},{4,0},{8,12},{12,8},{16,20},{20,16},{24,28},{28,24},{1,5},{5... | collective-permute-start | bytes 1769480 | tf_op jit(solution)/shard_map/ppermute | solution.py:382
  65.6 20.0 %collective-permute-start.19 = (bf16[4,72,832]{2,1,0:T(8,128)(2,1)S(1)}, bf16[4,72,832]{2,1,0:T(8,128)(2,1)S(1)}, u32[]{:S(2)}, u32[]{:S(2)}) collective-permute-start(bf16[4,72,832]{2,1,0:T(8,128)(2,1)S(1)} %grad_w_rows.6), channel_id=1, source_target_pairs={{0,2},{1,3},{2,0},{3,1},{4,6},{5,7},{6,4},{7,5},{8,10},{9,11},{10,... | collective-permute-start | bytes 1437704 | tf_op jit(solution)/shard_map/ppermute | solution.py:379
  75.2 6.8 %collective-permute-start.13 = (bf16[2,72,896]{2,1,0:T(8,128)(2,1)S(1)}, bf16[2,72,896]{2,1,0:T(8,128)(2,1)S(1)}, u32[]{:S(2)}, u32[]{:S(2)}) collective-permute-start(bf16[2,72,896]{2,1,0:T(8,128)(2,1)S(1)} %get-tuple-element.69), channel_id=1, source_target_pairs={{0,8},{4,12},{8,0},{12,4},{16,24},{20,28},{24,16},{28,20},{1,9},{5... | collective-permute-start | bytes 774152 | tf_op jit(solution)/shard_map/ppermute | solution.py:385
  82.1 7.4 %collective-permute-start.20 = (bf16[72,896]{1,0:T(8,128)(2,1)S(1)}, bf16[72,896]{1,0:T(8,128)(2,1)S(1)}, u32[]{:S(2)}, u32[]{:S(2)}) collective-permute-start(bf16[72,896]{1,0:T(8,128)(2,1)S(1)} %get-tuple-element.79), channel_id=1, source_target_pairs={{0,16},{4,20},{8,24},{12,28},{16,0},{20,4},{24,8},{28,12},{1,17},{... | collective-permute-start | bytes 387080 | tf_op jit(solution)/shard_map/ppermute | solution.py:385
  89.6 11.9 %collective-permute-start.21 = (bf16[2,72,832]{2,1,0:T(8,128)(2,1)S(1)}, bf16[2,72,832]{2,1,0:T(8,128)(2,1)S(1)}, u32[]{:S(2)}, u32[]{:S(2)}) collective-permute-start(bf16[2,72,832]{2,1,0:T(8,128)(2,1)S(1)} %get-tuple-element.83), channel_id=1, source_target_pairs={{0,8},{4,12},{8,0},{12,4},{16,24},{20,28},{24,16},{28,20},{1,9},{5... | collective-permute-start | bytes 718856 | tf_op jit(solution)/shard_map/ppermute | solution.py:385
  90.0 11.5 %collective-permute-start.23 = (bf16[72,896]{1,0:T(8,128)(2,1)S(1)}, bf16[72,896]{1,0:T(8,128)(2,1)S(1)}, u32[]{:S(2)}, u32[]{:S(2)}) collective-permute-start(bf16[72,896]{1,0:T(8,128)(2,1)S(1)} %sum_z.2.refs_0_), channel_id=1, source_target_pairs={{0,16},{4,20},{8,24},{12,28},{16,0},{20,4},{24,8},{28,12},{1,17},{... | collective-permute-start | bytes 387080 | tf_op jit(solution)/shard_map/ppermute | solution.py:385
  92.2 15.0 %collective-permute-start.26 = (bf16[72,896]{1,0:T(8,128)(2,1)S(1)}, bf16[72,896]{1,0:T(8,128)(2,1)S(1)}, u32[]{:S(2)}, u32[]{:S(2)}) collective-permute-start(bf16[72,896]{1,0:T(8,128)(2,1)S(1)} %sum_z.2.refs_0_), channel_id=1, source_target_pairs={{0,4},{4,0},{8,12},{12,8},{16,20},{20,16},{24,28},{28,24},{1,5},{5... | collective-permute-start | bytes 387080 | tf_op jit(solution)/shard_map/ppermute | solution.py:382
  92.8 14.4 %collective-permute-start.25 = (bf16[72,896]{1,0:T(8,128)(2,1)S(1)}, bf16[72,896]{1,0:T(8,128)(2,1)S(1)}, u32[]{:S(2)}, u32[]{:S(2)}) collective-permute-start(bf16[72,896]{1,0:T(8,128)(2,1)S(1)} %sum_z.2.refs_0_), channel_id=1, source_target_pairs={{0,8},{4,12},{8,0},{12,4},{16,24},{20,28},{24,16},{28,20},{1,9},{5... | collective-permute-start | bytes 387080 | tf_op jit(solution)/shard_map/ppermute | solution.py:385
  101.5 7.9 %collective-permute-start.24 = (bf16[72,896]{1,0:T(8,128)(2,1)S(1)}, bf16[72,896]{1,0:T(8,128)(2,1)S(1)}, u32[]{:S(2)}, u32[]{:S(2)}) collective-permute-start(bf16[72,896]{1,0:T(8,128)(2,1)S(1)} %collective-permute-done.23.refs_1_.refs_2_), channel_id=1, source_target_pairs={{0,8},{4,12},{8,0},{12,4},{16,24},{20,28},{24,16},{28,20},{1,9},{5... | collective-permute-start | bytes 387080 | tf_op jit(solution)/shard_map/ppermute | solution.py:385
  102.2 7.2 %collective-permute-start.22 = (bf16[72,832]{1,0:T(8,128)(2,1)S(1)}, bf16[72,832]{1,0:T(8,128)(2,1)S(1)}, u32[]{:S(2)}, u32[]{:S(2)}) collective-permute-start(bf16[72,832]{1,0:T(8,128)(2,1)S(1)} %get-tuple-element.84), channel_id=1, source_target_pairs={{0,16},{4,20},{8,24},{12,28},{16,0},{20,4},{24,8},{28,12},{1,17},{... | collective-permute-start | bytes 359432 | tf_op jit(solution)/shard_map/ppermute | solution.py:385
  109.5 9.5 %collective-permute-start.32 = (bf16[88,832]{1,0:T(8,128)(2,1)S(1)}, bf16[88,832]{1,0:T(8,128)(2,1)S(1)}, u32[]{:S(2)}, u32[]{:S(2)}) collective-permute-start(bf16[88,832]{1,0:T(8,128)(2,1)S(1)} %sum_z.3.refs_6_), channel_id=1, source_target_pairs={{0,16},{4,20},{8,24},{12,28},{16,0},{20,4},{24,8},{28,12},{1,17},{... | collective-permute-start | bytes 439304 | tf_op jit(solution)/shard_map/ppermute | solution.py:385
  110.3 9.5 %collective-permute-start.31 = (bf16[88,832]{1,0:T(8,128)(2,1)S(1)}, bf16[88,832]{1,0:T(8,128)(2,1)S(1)}, u32[]{:S(2)}, u32[]{:S(2)}) collective-permute-start(bf16[88,832]{1,0:T(8,128)(2,1)S(1)} %sum_z.3.refs_6_), channel_id=1, source_target_pairs={{0,8},{4,12},{8,0},{12,4},{16,24},{20,28},{24,16},{28,20},{1,9},{5... | collective-permute-start | bytes 439304 | tf_op jit(solution)/shard_map/ppermute | solution.py:385
  112.2 7.6 %collective-permute-start.30 = (bf16[88,832]{1,0:T(8,128)(2,1)S(1)}, bf16[88,832]{1,0:T(8,128)(2,1)S(1)}, u32[]{:S(2)}, u32[]{:S(2)}) collective-permute-start(bf16[88,832]{1,0:T(8,128)(2,1)S(1)} %sum_z.3.refs_6_), channel_id=1, source_target_pairs={{0,4},{4,0},{8,12},{12,8},{16,20},{20,16},{24,28},{28,24},{1,5},{5... | collective-permute-start | bytes 439304 | tf_op jit(solution)/shard_map/ppermute | solution.py:382
  112.8 23.0 %collective-permute-start.29 = (bf16[3,72,896]{2,1,0:T(8,128)(2,1)S(1)}, bf16[3,72,896]{2,1,0:T(8,128)(2,1)S(1)}, u32[]{:S(2)}, u32[]{:S(2)}) collective-permute-start(bf16[3,72,896]{2,1,0:T(8,128)(2,1)S(1)} %stack.1), channel_id=1, source_target_pairs={{0,4},{4,0},{8,12},{12,8},{16,20},{20,16},{24,28},{28,24},{1,5},{5... | collective-permute-start | bytes 1161224 | tf_op jit(solution)/shard_map/ppermute | solution.py:382
  114.5 9.0 %collective-permute-start.15 = (bf16[2,32,1152]{2,1,0:T(8,128)(2,1)S(1)}, bf16[2,32,1152]{2,1,0:T(8,128)(2,1)S(1)}, u32[]{:S(2)}, u32[]{:S(2)}) collective-permute-start(bf16[2,32,1152]{2,1,0:T(8,128)(2,1)S(1)} %get-tuple-element.73), channel_id=1, source_target_pairs={{0,8},{4,12},{8,0},{12,4},{16,24},{20,28},{24,16},{28,20},{1,9},{5... | collective-permute-start | bytes 442376 | tf_op jit(solution)/shard_map/ppermute | solution.py:385
  119.0 10.2 %collective-permute-start.16 = (bf16[2,32,1152]{2,1,0:T(8,128)(2,1)S(1)}, bf16[2,32,1152]{2,1,0:T(8,128)(2,1)S(1)}, u32[]{:S(2)}, u32[]{:S(2)}) collective-permute-start(bf16[2,32,1152]{2,1,0:T(8,128)(2,1)S(1)} %get-tuple-element.74), channel_id=1, source_target_pairs={{0,16},{4,20},{8,24},{12,28},{16,0},{20,4},{24,8},{28,12},{1,17},{... | collective-permute-start | bytes 442376 | tf_op jit(solution)/shard_map/ppermute | solution.py:385
  119.8 9.9 %collective-permute-start.33 = (bf16[88,832]{1,0:T(8,128)(2,1)S(1)}, bf16[88,832]{1,0:T(8,128)(2,1)S(1)}, u32[]{:S(2)}, u32[]{:S(2)}) collective-permute-start(bf16[88,832]{1,0:T(8,128)(2,1)S(1)} %collective-permute-done.32.refs_8_), channel_id=1, source_target_pairs={{0,8},{4,12},{8,0},{12,4},{16,24},{20,28},{24,16},{28,20},{1,9},{5... | collective-permute-start | bytes 439304 | tf_op jit(solution)/shard_map/ppermute | solution.py:385
  121.4 10.7 %collective-permute-start.17 = (bf16[2,32,1152]{2,1,0:T(8,128)(2,1)S(1)}, bf16[2,32,1152]{2,1,0:T(8,128)(2,1)S(1)}, u32[]{:S(2)}, u32[]{:S(2)}) collective-permute-start(bf16[2,32,1152]{2,1,0:T(8,128)(2,1)S(1)} %get-tuple-element.75), channel_id=1, source_target_pairs={{0,24},{4,28},{8,16},{12,20},{16,8},{20,12},{24,0},{28,4},{1,25},{... | collective-permute-start | bytes 442376 | tf_op jit(solution)/shard_map/ppermute | solution.py:385
  123.4 10.2 %collective-permute-start.34 = (bf16[88,832]{1,0:T(8,128)(2,1)S(1)}, bf16[88,832]{1,0:T(8,128)(2,1)S(1)}, u32[]{:S(2)}, u32[]{:S(2)}) collective-permute-start(bf16[88,832]{1,0:T(8,128)(2,1)S(1)} %collective-permute-done.31.refs_7_), channel_id=1, source_target_pairs={{0,4},{4,0},{8,12},{12,8},{16,20},{20,16},{24,28},{28,24},{1,5},{5... | collective-permute-start | bytes 439304 | tf_op jit(solution)/shard_map/ppermute | solution.py:382
  129.8 7.7 %collective-permute-start.36 = (bf16[88,832]{1,0:T(8,128)(2,1)S(1)}, bf16[88,832]{1,0:T(8,128)(2,1)S(1)}, u32[]{:S(2)}, u32[]{:S(2)}) collective-permute-start(bf16[88,832]{1,0:T(8,128)(2,1)S(1)} %collective-permute-done.33.refs_9_), channel_id=1, source_target_pairs={{0,4},{4,0},{8,12},{12,8},{16,20},{20,16},{24,28},{28,24},{1,5},{5... | collective-permute-start | bytes 439304 | tf_op jit(solution)/shard_map/ppermute | solution.py:382
  (9 other events, 33.6 us)
